TPU v7x, 32 devices: a whole 2x2x4 slice. The times are simulated.
32 devices in a mesh: seq: 4 (over z), fsdp: 8 (over y, x, core).
Axes of the slice: x: 2, y: 2, z: 4, core: 2. Of those that a mesh axis runs over, the one named last changes fastest.
Arguments:
- tokens: bfloat16 [8, 2048, 1536], P('fsdp', 'seq'), may hold values from -6 to 6
- pre_gain: bfloat16 [1536], P(('seq', 'fsdp')), may hold values from 0.5 to 1.5
- in_weight: bfloat16 [1536, 6448], P(('seq', 'fsdp')), may hold values from -0.15625 to 0.15625
- conv_weight: bfloat16 [4, 3328], P(None, ('seq', 'fsdp')), may hold values from -3 to 3
- conv_bias: bfloat16 [3328], P(('seq', 'fsdp')), may hold values from -1.75 to 1.75
- step_bias: float32 [48], replicated, may hold values from -7 to -2.3
- decay_log: float32 [48], replicated, may hold values from -1 to 1
- skip_gain: float32 [48], replicated, may hold values from 0.2 to 1
- norm_gain: bfloat16 [3072], P(('seq', 'fsdp')), may hold values from 0.5 to 1.5
- out_weight: bfloat16 [3072, 1536], P(('seq', 'fsdp')), may hold values from -0.109375 to 0.109375
- cotangent: bfloat16 [8, 2048, 1536], P('fsdp', 'seq'), may hold values from -6 to 6
Outputs:
- mixed: bfloat16 [8, 2048, 1536], P('fsdp', 'seq')
- grad_tokens: float32 [8, 2048, 1536], P('fsdp', 'seq')
- grad_pre_gain: float32 [1536], P(('seq', 'fsdp'))
- grad_in_weight: float32 [1536, 6448], P(('seq', 'fsdp'))
- grad_conv_weight: float32 [4, 3328], P(None, ('seq', 'fsdp'))
- grad_conv_bias: float32 [3328], P(('seq', 'fsdp'))
- grad_step_bias: float32 [48], replicated
- grad_decay_log: float32 [48], replicated
- grad_skip_gain: float32 [48], replicated
- grad_norm_gain: float32 [3072], P(('seq', 'fsdp'))
- grad_out_weight: float32 [3072, 1536], P(('seq', 'fsdp'))
All inputs are finite; a program needn't handle non-finite values.
Results may differ from a plain program's by a relative error of at most 0.0067.
Values may be sent and summed in bfloat16 or wider, within the bound.
A program may use at most 320 MiB of HBM per device.

v0:
```python
import jax
import jax.numpy as jnp
from jax import lax
from jax.sharding import PartitionSpec as P

INNER = 3072
HEADS = 48
HEAD_DIM = 64
STATE = 128
CONV = 4
BLOCK_LEN = 256
CHANNELS = 3328
PROJ = 6448


HIGHEST = lax.Precision.HIGHEST


def carried_in(x, axis, join, neutral, backward):
    count = lax.axis_size(axis)
    place = lax.axis_index(axis)
    ahead = count - 1 - place if backward else place
    gathered = jax.tree.map(
        lambda a, kind: lax.all_gather(a.astype(kind), axis),
        x,
        jax.tree.map(lambda a: jnp.bfloat16 if a.dtype == jnp.float32 else a.dtype, x),
    )
    state = jax.tree.map(lambda a, e: jnp.zeros_like(a) + jnp.asarray(e, a.dtype), x, neutral)

    def one(hop, state):
        source = count - 1 - hop if backward else hop
        return join(
            state,
            jax.tree.map(
                lambda a, own: lax.dynamic_index_in_dim(a, source, 0, False).astype(own.dtype),
                gathered,
                x,
            ),
        )

    return lax.fori_loop(0, ahead, one, state)


def passed_along(x, axis, by):
    peers = lax.axis_size(axis)
    pairs = [(i, i + by) for i in range(peers) if 0 <= i + by < peers]
    return lax.ppermute(x, axis, pairs)


def shortened(x):
    return jax.tree.map(lambda a: a.astype(jnp.bfloat16) if a.dtype == jnp.float32 else a, x)


def pre_norm(inputs, gain_vec):
    return inputs * lax.rsqrt(jnp.mean(inputs * inputs, axis=-1, keepdims=True) + 1e-05) * gain_vec


def ssd_local(projected, edge_rows, conv_weight, conv_bias, step_bias, decay_log, skip_gain):
    sequences = projected.shape[0]
    positions = projected.shape[1]
    blocks = positions // BLOCK_LEN
    gate_in = projected[:, :, :INNER]
    conv_in = projected[:, :, INNER : INNER + CHANNELS]
    step_raw = projected[:, :, INNER + CHANNELS :]
    padded = jnp.concatenate([edge_rows, conv_in], axis=1)
    conv_out = conv_bias + jnp.zeros_like(conv_in)
    for tap_index in range(CONV):
        conv_out = conv_out + padded[:, tap_index : tap_index + positions] * conv_weight[tap_index]
    active = jax.nn.silu(conv_out)
    values_in = active[:, :, :INNER].reshape(sequences, positions, HEADS, HEAD_DIM)
    input_map = active[:, :, INNER : INNER + STATE].reshape(sequences, blocks, BLOCK_LEN, STATE)
    output_map = active[:, :, INNER + STATE :]
    step_size = jax.nn.softplus(step_raw + step_bias)
    log_decay = -jnp.exp(decay_log) * step_size
    log_run = jnp.cumsum(log_decay.reshape(sequences, blocks, BLOCK_LEN, HEADS), axis=2)
    causal = jnp.tril(jnp.ones((BLOCK_LEN, BLOCK_LEN), bool))
    log_gap = log_run[:, :, :, None, :] - log_run[:, :, None, :, :]
    decay_pairs = jnp.exp(jnp.where(causal[None, None, :, :, None], log_gap, -1e30))
    scaled = (values_in * step_size[..., None]).reshape(
        sequences, blocks, BLOCK_LEN, HEADS, HEAD_DIM
    )
    output_blocks = output_map.reshape(sequences, blocks, BLOCK_LEN, STATE)
    scores = jnp.einsum("bcqn,bcsn->bcqs", output_blocks, input_map, precision=HIGHEST)
    inner_out = jnp.einsum(
        "bcqsh,bcshp->bcqhp", scores[..., None] * decay_pairs, scaled, precision=HIGHEST
    )
    to_end = jnp.exp(log_run[:, :, -1:, :] - log_run)
    block_states = jnp.einsum(
        "bcshp,bcsn->bchpn", scaled * to_end[..., None], input_map, precision=HIGHEST
    )
    block_decay = jnp.exp(log_run[:, :, -1, :])
    running = jnp.zeros((sequences, HEADS, HEAD_DIM, STATE), jnp.float32)
    starts = []
    for block_index in range(blocks):
        starts.append(running)
        running = (
            block_decay[:, block_index, :, None, None] * running + block_states[:, block_index]
        )
    start_states = jnp.stack(starts, axis=1)
    carried = (
        jnp.einsum("bcqn,bchpn->bcqhp", output_blocks, start_states, precision=HIGHEST)
        * jnp.exp(log_run)[..., None]
    )
    mixer_out = (inner_out + carried).reshape(sequences, positions, HEADS, HEAD_DIM) + skip_gain[
        :, None
    ] * values_in
    block_totals = log_run[:, :, -1, :]
    log_offset = jnp.cumsum(block_totals, axis=1) - block_totals
    log_device = (log_run + log_offset[:, :, None, :]).reshape(sequences, positions, HEADS)
    decay_total = jnp.exp(jnp.sum(log_decay, axis=1))
    return (
        mixer_out.reshape(sequences, positions, INNER),
        output_map,
        log_device,
        gate_in,
        running,
        decay_total,
    )


def gated_carry(mixer_out, output_map, log_device, gate_in, incoming, gain_vec):
    sequences = mixer_out.shape[0]
    positions = mixer_out.shape[1]
    carried = (
        jnp.einsum("btn,bhpn->bthp", output_map, incoming, precision=HIGHEST)
        * jnp.exp(log_device)[..., None]
    )
    gated = (mixer_out + carried.reshape(sequences, positions, INNER)) * jax.nn.silu(gate_in)
    return gated * lax.rsqrt(jnp.mean(gated * gated, axis=-1, keepdims=True) + 1e-05) * gain_vec


def combine_states(earlier, latter):
    decay_early, state_early = earlier
    decay_late, state_late = latter
    return (decay_early * decay_late, decay_late[:, :, None, None] * state_early + state_late)


def pass_forward(decay_total, final_state):
    identity = (jnp.ones_like(decay_total), jnp.zeros_like(final_state))
    return carried_in((decay_total, final_state), "seq", combine_states, identity, False)[1]


def pass_backward(decay_total, state_grad):
    identity = (jnp.ones_like(decay_total), jnp.zeros_like(state_grad))
    return carried_in((decay_total, state_grad), "seq", combine_states, identity, True)[1]


def local(
    tokens,
    pre_gain,
    in_weight,
    conv_weight,
    conv_bias,
    step_bias,
    decay_log,
    skip_gain,
    norm_gain,
    out_weight,
    cotangent,
):
    gain_full, inw_full, convw_full, convb_full, normg_full, outw_full = (
        lax.all_gather(pre_gain, ("seq", "fsdp"), axis=0, tiled=True),
        lax.all_gather(in_weight, ("seq", "fsdp"), axis=0, tiled=True),
        lax.all_gather(conv_weight, ("seq", "fsdp"), axis=1, tiled=True),
        lax.all_gather(conv_bias, ("seq", "fsdp"), axis=0, tiled=True),
        lax.all_gather(norm_gain, ("seq", "fsdp"), axis=0, tiled=True),
        lax.all_gather(out_weight, ("seq", "fsdp"), axis=0, tiled=True),
    )
    sequences, positions, features = tokens.shape
    total_rows = sequences * positions
    inputs = tokens.astype(jnp.float32)
    normed, norm_pullback = jax.vjp(pre_norm, inputs, gain_full.astype(jnp.float32))
    normed_low = normed.astype(jnp.bfloat16).reshape(total_rows, features)
    projected = jnp.dot(normed_low, inw_full, preferred_element_type=jnp.float32).reshape(
        sequences, positions, PROJ
    )
    edge_rows = passed_along(
        projected[:, positions - CONV + 1 :, INNER : INNER + CHANNELS].astype(jnp.bfloat16),
        "seq",
        1,
    ).astype(jnp.float32)
    local_out, local_pullback = jax.vjp(
        ssd_local,
        projected,
        edge_rows,
        convw_full.astype(jnp.float32),
        convb_full.astype(jnp.float32),
        step_bias,
        decay_log,
        skip_gain,
    )
    mixer_part, output_map, log_device, gate_in, final_state, decay_total = local_out
    incoming = pass_forward(decay_total, final_state)
    normed_out, gate_pullback = jax.vjp(
        gated_carry,
        mixer_part,
        output_map,
        log_device,
        gate_in,
        incoming,
        normg_full.astype(jnp.float32),
    )
    normed_out_low = normed_out.astype(jnp.bfloat16).reshape(total_rows, INNER)
    branch = jnp.dot(normed_out_low, outw_full, preferred_element_type=jnp.float32)
    mixed = (inputs + branch.reshape(sequences, positions, features)).astype(jnp.bfloat16)
    inw_back, outw_back = (
        lax.all_gather(in_weight, ("seq", "fsdp"), axis=0, tiled=True),
        lax.all_gather(out_weight, ("seq", "fsdp"), axis=0, tiled=True),
    )
    cot_rows = cotangent.reshape(total_rows, features)
    grad_out_weight = jnp.einsum(
        "ti,td->id", normed_out_low, cot_rows, preferred_element_type=jnp.float32
    )
    grad_normed_out = lax.dot_general(
        cot_rows, outw_back, (((1,), (1,)), ((), ())), preferred_element_type=jnp.float32
    )
    grad_mixer, grad_output_map, grad_log_device, grad_gate_in, grad_incoming, grad_norm_gain = (
        gate_pullback(grad_normed_out.reshape(sequences, positions, INNER))
    )
    returned = pass_backward(decay_total, grad_incoming)
    grad_decay_total = jnp.sum(returned * incoming, axis=(2, 3))
    local_grads = local_pullback(
        (grad_mixer, grad_output_map, grad_log_device, grad_gate_in, returned, grad_decay_total)
    )
    (
        grad_projected,
        grad_edge,
        grad_conv_weight,
        grad_conv_bias,
        grad_step_bias,
        grad_decay_log,
        grad_skip_gain,
    ) = local_grads
    edge_grad = passed_along(shortened(grad_edge), "seq", -1).astype(grad_edge.dtype)
    grad_projected = grad_projected.at[:, positions - CONV + 1 :, INNER : INNER + CHANNELS].add(
        edge_grad
    )
    grad_proj_low = grad_projected.astype(jnp.bfloat16).reshape(total_rows, PROJ)
    grad_in_weight = jnp.einsum(
        "td,te->de", normed_low, grad_proj_low, preferred_element_type=jnp.float32
    )
    grad_normed = lax.dot_general(
        grad_proj_low, inw_back, (((1,), (1,)), ((), ())), preferred_element_type=jnp.float32
    )
    grad_inputs, grad_pre_gain = norm_pullback(grad_normed.reshape(sequences, positions, features))
    grad_tokens = cotangent.astype(jnp.float32) + grad_inputs
    head_grads = lax.psum((grad_step_bias, grad_decay_log, grad_skip_gain), ("seq", "fsdp"))
    owned = (
        lax.psum_scatter(grad_pre_gain, ("seq", "fsdp"), scatter_dimension=0, tiled=True),
        lax.psum_scatter(grad_in_weight, ("seq", "fsdp"), scatter_dimension=0, tiled=True),
        lax.psum_scatter(grad_conv_weight, ("seq", "fsdp"), scatter_dimension=1, tiled=True),
        lax.psum_scatter(grad_conv_bias, ("seq", "fsdp"), scatter_dimension=0, tiled=True),
        lax.psum_scatter(grad_norm_gain, ("seq", "fsdp"), scatter_dimension=0, tiled=True),
        lax.psum_scatter(grad_out_weight, ("seq", "fsdp"), scatter_dimension=0, tiled=True),
    )
    return (
        mixed,
        grad_tokens,
        owned[0],
        owned[1],
        owned[2],
        owned[3],
        head_grads[0],
        head_grads[1],
        head_grads[2],
        owned[4],
        owned[5],
    )


def solution(mesh):
    placed = (
        P("fsdp", "seq", None),
        P(("seq", "fsdp")),
        P(("seq", "fsdp"), None),
        P(None, ("seq", "fsdp")),
        P(("seq", "fsdp")),
        P(),
        P(),
        P(),
        P(("seq", "fsdp")),
        P(("seq", "fsdp"), None),
        P("fsdp", "seq", None),
    )
    return jax.shard_map(
        local,
        mesh=mesh,
        in_specs=placed,
        out_specs=(
            P("fsdp", "seq", None),
            P("fsdp", "seq", None),
            P(("seq", "fsdp")),
            P(("seq", "fsdp"), None),
            P(None, ("seq", "fsdp")),
            P(("seq", "fsdp")),
            P(),
            P(),
            P(),
            P(("seq", "fsdp")),
            P(("seq", "fsdp"), None),
        ),
        check_vma=False,
    )
```

profile of v0, /device:TPU:0, one launch (start us, length us, event | category | flops | bytes accessed | tf_op | source)
XLA Modules:
  0.0 1431.4 jit_solution(9974922040084814405)
XLA Ops:
  10.5 43.2 %all-reduce.31 = (bf16[1536]{0:T(1024)(128)(2,1)S(1)}, bf16[3328]{0:T(1024)(128)(2,1)S(1)}, bf16[3072]{0:T(1024)(128)(2,1)S(1)}) all-reduce(bf16[1536]{0:T(1024)(128)(2,1)S(1)} %dynamic-update-slice.4, bf16[3328]{0:T(1024)(128)(2,1)S(1)} %dynamic-update-slice.3, ...), channel_id=1, replica_groups=mesh['seq'=4,'fsdp'=8] {'seq','fsdp'}, use_global_device_ids=true, to_apply=%add.23 | all-reduce | flops 7936 | bytes 31744
  53.8 40.5 %all-gather.2 = bf16[32,104,4]{1,2,0:T(4,128)(2,1)S(1)} all-gather(bf16[1,104,4]{1,2,0:T(4,128)(2,1)} %bitcast.379), channel_id=1, replica_groups=mesh['seq'=4,'fsdp'=8] {'seq','fsdp'}, dimensions={0}, use_global_device_ids=true | all-gather | bytes 27456 | tf_op jit(solution)/shard_map/all_gather | solution.py:164
  97.0 48.6 %all-gather.8.cloned.1.call-done = bf16[1536,6448]{1,0:T(8,128)(2,1)} async-done(((bf16[48,6448]{1,0:T(8,128)(2,1)}), bf16[1536,6448]{1,0:T(8,128)(2,1)}) %all-gather.8.cloned.1.call-update) | async-done | bytes 19808272 | tf_op jit(solution)/shard_map/all_gather | solution.py:163
  145.6 18.2 %convolution_bitcast_fusion = f32[1,512,6448]{1,2,0:T(8,128)} fusion(bf16[1536,6448]{1,0:T(8,128)(2,1)} %all-gather.8.cloned.1.call-done, bf16[1,512,1536]{2,1,0:T(8,128)(2,1)} %param.17, f32[1536]{0:T(1024)S(1)} %convert_element_type.128, f32[512]{0:T(512)S(1)} %fusion.129), kind=kOutput, calls=%fused_computation.28 | convolution fusion | flops 10144972800 | bytes 34594816 | tf_op jit(solution)/shard_map/dot_general | solution.py:174
  182.7 19.1 %fusion.21 = (f32[1,512,3328]{1,2,0:T(8,128)S(1)}, f32[1,512,3328]{1,2,0:T(8,128)}) fusion(f32[1,512,3328]{1,2,0:T(8,128)} %slice.127, f32[3328]{0:T(1024)S(1)} %get-tuple-element.226, f32[3328]{0:T(1024)S(1)} %get-tuple-element.227, f32[1,3,3328]{1,2,0:T(8,128)S(1)} %copy.248, f32[3328]{0:T(1024)S(1)} %get-tuple-element.228, ...), kind=kLoop, calls=%fused_computation.45 | loop fusion | flops 25559040 | bytes 20553728 | tf_op jit(solution)/shard_map/jvp(jit(silu))/mul | solution.py:69
  229.9 10.9 all-reduce.24
  259.0 29.3 %bitcast_add_fusion.1 = f32[1,2,256,48,64]{2,4,3,1,0:T(8,128)} fusion(f32[2,256,48,64]{1,3,2,0:T(8,128)S(1)} %fusion.59, f32[2,256,48]{1,2,0:T(8,128)S(1)} %bitcast.356, f32[2,256,48]{1,2,0:T(8,128)S(1)} %bitcast.369, f32[2,256,256]{2,1,0:T(8,128)S(1)} %fusion.151, pred[256,256]{1,0:T(8,128)(4,1)S(1)} %iota_compare_fusion, ...), kind=kOutput, calls=%fused_computation.54 | convolution fusion | flops 4855431168 | bytes 19759104 | tf_op jit(solution)/shard_map/jvp(bcqsh,bcshp->bcqhp)/dot_general | solution.py:84
  288.3 11.0 copy.260
  326.1 47.3 %all-gather.12.cloned.1.call-done = bf16[3072,1536]{1,0:T(8,128)(2,1)} async-done(((bf16[96,1536]{1,0:T(8,128)(2,1)}), bf16[3072,1536]{1,0:T(8,128)(2,1)}) %all-gather.12.cloned.1.call-update) | async-done | bytes 9437200 | tf_op jit(solution)/shard_map/all_gather | solution.py:167
  373.5 14.0 fusion.28
  387.5 11.8 multiply_reduce_fusion.4
  437.1 12.4 fusion.94
  449.6 38.2 %fusion.6 = (f32[2,256,48]{1,2,0:T(8,128)}, f32[2,256,48]{1,2,0:T(8,128)}, f32[2,256,256]{2,1,0:T(8,128)S(1)}) fusion(f32[2,256,48]{1,2,0:T(8,128)S(1)} %bitcast.370, f32[2,256,256]{2,1,0:T(8,128)S(1)} %copy-done.42, pred[256,256]{1,0:T(8,128)(4,1)S(1)} %copy-done.61, f32[2,256,48,64]{1,0,3,2:T(2,128)} %reshape.926, f32[2,256,48]{1,2,0:T(8,128)S(1)} %copy-done.23, ...), kind=kOutput, calls=%fused_computation.14 | convolution fusion | flops 4889853952 | bytes 14090240 | tf_op jit(solution)/shard_map/transpose(jvp(bcqsh,bcshp->bcqhp))/dot_general | solution.py:84
  525.5 11.4 fusion.33
  545.2 24.1 %bitcast_add_fusion = f32[1,2,256,48,64]{2,4,3,1,0:T(8,128)} fusion(f32[2,48,64,256]{3,2,1,0:T(8,128)} %get-tuple-element.293, f32[2,256,48]{1,2,0:T(8,128)S(1)} %bitcast.354, f32[2,256,48]{1,2,0:T(8,128)S(1)} %bitcast.371, f32[2,256,256]{2,1,0:T(8,128)S(1)} %copy-done.43, pred[256,256]{1,0:T(8,128)(4,1)} %copy-done.60, f32[1,2,256,48,64]{2,1,4,3,0:T(2,128)} %reshape.946), kind=kOutput, calls=%fused_computation.53 | convolution fusion | flops 4853858304 | bytes 19660800 | tf_op jit(solution)/shard_map/transpose(jvp(bcqsh,bcshp->bcqhp))/dot_general | solution.py:84
  578.0 11.1 copy.272
  606.6 18.4 %multiply_reduce_fusion.2 = (f32[3328]{0:T(1024)S(1)}, f32[3328]{0:T(1024)S(1)}, f32[3328]{0:T(1024)S(1)}, f32[3328]{0:T(1024)}, f32[3328]{0:T(1024)S(1)}, /*index=5*/f32[1,512,3328]{1,2,0:T(8,128)}) fusion(f32[1,512,3328]{1,2,0:T(8,128)S(1)} %bitcast.338, f32[1,3,3328]{1,2,0:T(8,128)S(1)} %copy-done.9, f32[1,512,6448]{1,2,0:T(8,128)} %convolution_bitcast_fusion, ...), kind=kLoop, calls=%fused_computation.42 | loop fusion | flops 39173888 | bytes 34185216 | tf_op jit(solution)/shard_map/transpose(jvp())/reduce_sum | solution.py:68
  691.6 20.1 %fusion.49 = (f32[1536]{0:T(1024)}, f32[512]{0:T(512)S(1)}, f32[512,1536]{1,0:T(8,128)}) fusion(bf16[1,512,1536]{2,1,0:T(8,128)(2,1)} %param.17, f32[512]{0:T(512)S(1)} %copy-done.71, f32[1536]{0:T(1024)S(1)} %copy-done.65, bf16[1536,6448]{1,0:T(8,128)(2,1)} %all-gather.8.cloned.1.call-done, f32[1,512,6448]{1,2,0:T(8,128)} %scatter-add.4), kind=kOutput, calls=%fused_computation.104 | convolution fusion | flops 10150631424 | bytes 37748736 | tf_op jit(solution)/shard_map/dot_general | solution.py:242
  711.8 12.3 fusion.83
  725.5 22.2 %fusion.22 = f32[1536,6448]{1,0:T(8,128)} fusion(f32[1,512,6448]{1,2,0:T(8,128)} %scatter-add.4, bf16[1,512,1536]{2,1,0:T(8,128)(2,1)S(1)} %copy-done.13, f32[1536]{0:T(1024)S(1)} %copy-done.65, f32[512]{0:T(512)S(1)} %copy-done.71), kind=kOutput, calls=%fused_computation.47 | convolution fusion | flops 10148274176 | bytes 54403072 | tf_op jit(solution)/shard_map/td,te->de/dot_general | solution.py:239
  747.8 11.1 fusion.52
  761.5 73.3 %all-reduce.34.cloned.1.call-done = (f32[1536]{0:T(1024)}, f32[4,3328]{1,0:T(4,128)}, f32[3328]{0:T(1024)}, f32[48]{0:T(128)}, f32[48]{0:T(128)}, /*index=5*/f32[48]{0:T(128)}, f32[3072]{0:T(1024)}) async-done(((f32[1536]{0:T(1024)}, f32[4,3328]{1,0:T(4,128)}, f32[3328]{0:T(1024)}, f32[48]{0:T(128)}, f32[48]{0:T(128)}, /*index=5*/f32[48]{0:T(128)}, f32[3072]{0:T(1024)}), (f32[1536]{0:T(1024)}, ...) | async-done | bytes 85584
  839.9 209.4 %reduce-scatter.6.cloned.1.call-done = f32[96,1536]{1,0:T(8,128)} async-done(((f32[3072,1536]{1,0:T(8,128)}), f32[96,1536]{1,0:T(8,128)}) %reduce-scatter.6.cloned.1.call-update) | async-done | bytes 589840 | tf_op jit(solution)/shard_map/reduce_scatter | solution.py:254
  1049.3 371.4 %reduce-scatter.4.cloned.1.call-done = f32[48,6448]{1,0:T(8,128)} async-done(((f32[1536,6448]{1,0:T(8,128)}), f32[48,6448]{1,0:T(8,128)}) %reduce-scatter.4.cloned.1.call-update) | async-done | bytes 1238032 | tf_op jit(solution)/shard_map/reduce_scatter | solution.py:250
  (358 shorter events, 291.6 us)
Async XLA Ops:
  7.2 138.5 %all-gather.8.cloned.1.call-start = ((), (), s32[]{:S(2)}) async-start(), calls=%async_computation.2 | async-start | bytes 20680704 | tf_op jit(solution)/shard_map/all_gather | solution.py:163
  7.9 300.5 %all-gather.10.cloned.1.call-start = ((), (), s32[]{:S(2)}) async-start(), calls=%async_computation.3 | async-start | bytes 3932160 | tf_op jit(solution)/shard_map/all_gather | solution.py:24
  53.8 91.9 %copy-start.64 = (f32[1536]{0:T(1024)}, f32[1536]{0:T(1024)S(1)}, u32[]{:S(2)}) copy-start(f32[1536]{0:T(1024)S(1)} %convert_element_type.128) | copy-start | bytes 18436
  94.5 88.2 %copy-start.49 = (f32[3328]{0:T(1024)}, f32[3328]{0:T(1024)S(1)}, u32[]{:S(2)}) copy-start(f32[3328]{0:T(1024)S(1)} %get-tuple-element.225) | copy-start | bytes 39940
  94.5 88.2 %copy-start.51 = (f32[3328]{0:T(1024)}, f32[3328]{0:T(1024)S(1)}, u32[]{:S(2)}) copy-start(f32[3328]{0:T(1024)S(1)} %get-tuple-element.226) | copy-start | bytes 39940
  94.5 88.2 %copy-start.53 = (f32[3328]{0:T(1024)}, f32[3328]{0:T(1024)S(1)}, u32[]{:S(2)}) copy-start(f32[3328]{0:T(1024)S(1)} %get-tuple-element.227) | copy-start | bytes 39940
  94.5 88.2 %copy-start.55 = (f32[3328]{0:T(1024)}, f32[3328]{0:T(1024)S(1)}, u32[]{:S(2)}) copy-start(f32[3328]{0:T(1024)S(1)} %get-tuple-element.228) | copy-start | bytes 39940
  96.3 49.3 %copy-start.66 = (f32[512]{0:T(512)}, f32[512]{0:T(512)S(1)}, u32[]{:S(2)}) copy-start(f32[512]{0:T(512)S(1)} %fusion.51) | copy-start | bytes 6148
  97.0 66.8 %copy-start.80 = (f32[48]{0:T(128)}, f32[48]{0:T(128)S(1)}, u32[]{:S(2)}) copy-start(f32[48]{0:T(128)S(1)} %exponential_negate_fusion) | copy-start | bytes 580
  97.0 66.8 %copy-start.70 = (f32[512]{0:T(512)}, f32[512]{0:T(512)S(1)}, u32[]{:S(2)}) copy-start(f32[512]{0:T(512)S(1)} %fusion.129) | copy-start | bytes 6148
  97.0 66.8 %copy-start.78 = (f32[48]{0:T(128)S(1)}, f32[48]{0:T(128)}, u32[]{:S(2)}) copy-start(f32[48]{0:T(128)} %param.22) | copy-start | bytes 580
  165.0 64.6 %copy-start.83 = (f32[48]{0:T(128)}, f32[48]{0:T(128)S(1)}, u32[]{:S(2)}) copy-start(f32[48]{0:T(128)S(1)} %get-tuple-element.273) | copy-start | bytes 580
  172.7 9.7 collective-permute-start
  175.6 48.8 %copy-start.74 = (f32[48]{0:T(128)}, f32[48]{0:T(128)S(1)}, u32[]{:S(2)}) copy-start(f32[48]{0:T(128)S(1)} %get-tuple-element.287) | copy-start | bytes 580
  175.7 48.8 %copy-start.76 = (f32[48]{0:T(128)}, f32[48]{0:T(128)S(1)}, u32[]{:S(2)}) copy-start(f32[48]{0:T(128)S(1)} %get-tuple-element.288) | copy-start | bytes 580
  227.3 146.1 %all-gather.12.cloned.1.call-start = ((), (), s32[]{:S(2)}) async-start(), calls=%async_computation.4 | async-start | bytes 9732096 | tf_op jit(solution)/shard_map/all_gather | solution.py:167
  228.1 287.3 %all-gather.14.cloned.1.call-start = ((), (), s32[]{:S(2)}) async-start(), calls=%async_computation.7 | async-start | bytes 3932160 | tf_op jit(solution)/shard_map/all_gather | solution.py:24
  228.7 158.7 %copy-start.62 = (f32[3072]{0:T(1024)}, f32[3072]{0:T(1024)S(1)}, u32[]{:S(2)}) copy-start(f32[3072]{0:T(1024)S(1)} %convert_element_type.135) | copy-start | bytes 36868
  326.1 61.3 %copy-start.72 = (f32[512]{0:T(512)}, f32[512]{0:T(512)S(1)}, u32[]{:S(2)}) copy-start(f32[512]{0:T(512)S(1)} %fusion.130) | copy-start | bytes 6148
  411.5 423.3 %all-reduce.34.cloned.1.call-start = ((), (), s32[]{:S(2)}) async-start(), calls=%async_computation.8 | async-start | bytes 183296
  449.6 42.5 %copy-start.16 = (f32[2,256,128,1]{2,1,3,0:T(8,128)S(1)}, f32[2,256,128,1]{2,1,3,0:T(8,128)}, u32[]{:S(2)}) copy-start(f32[2,256,128,1]{2,1,3,0:T(8,128)} %copy-done.15) | copy-start | bytes 786436
  659.1 19.3 %collective-permute-start.1 = (bf16[1,3,3328]{2,1,0:T(4,128)(2,1)}, bf16[1,3,3328]{2,1,0:T(4,128)(2,1)S(1)}, u32[]{:S(2)}, u32[]{:S(2)}) collective-permute-start(bf16[1,3,3328]{2,1,0:T(4,128)(2,1)} %copy.293), channel_id=1, source_target_pairs={{8,0},{16,8},{24,16},{9,1},{17,9},{25,17},{10,2},{18,10},{26,18},{... | collective-permute-start | bytes 59912 | tf_op jit(solution)/shard_map/ppermute | solution.py:47
  711.8 337.6 %reduce-scatter.6.cloned.1.call-start = ((), (), s32[]{:S(2)}) async-start(), calls=%async_computation.6 | async-start | bytes 19464192 | tf_op jit(solution)/shard_map/reduce_scatter | solution.py:254
  724.1 696.5 %reduce-scatter.4.cloned.1.call-start = ((), (), s32[]{:S(2)}) async-start(), calls=%async_computation.5 | async-start | bytes 41361408 | tf_op jit(solution)/shard_map/reduce_scatter | solution.py:250
  (80 other events, 1069.2 us)
Sparse Core Ops, SparseCore 0:
  10.9 134.6 all-gather.7
  227.5 62.3 all-gather.9
  292.7 80.6 all-gather.11
  411.6 62.0 all-gather.13
  711.9 122.8 all-reduce.33
  841.6 207.6 reduce-scatter.5
  1056.3 364.3 reduce-scatter.3
where the time goes:
time: 1440 us; the launch traced here: 1430 us
  waiting for transfers between devices  751 us (52%)
  matrix products  271 us (19%)
  other arithmetic  153 us (11%)
  local copies, waits for them, and re-layouts  142 us (10%)
  blocking collectives  94.6 us (7%)
  between operations  16.8 us (1%)
    reduce_scatter x1, waiting for transfers between devices, local(): lax.psum_scatter(grad_in_weight, ('seq', 'fsdp'), scatter_dimension=0, ti...  371 us
    reduce_scatter x1, waiting for transfers between devices, local(): lax.psum_scatter(grad_out_weight, ('seq', 'fsdp'), scatter_dimension=0, t...  209 us
    dot_general x3, matrix products, ssd_local(): jnp.einsum('bcqsh,bcshp->bcqhp', scores[..., None] * decay_pairs, scaled,...  91.6 us
    unnamed x8, waiting for transfers between devices  74.7 us
    unnamed x2, blocking collectives  54.2 us
    all_gather x1, waiting for transfers between devices, local(): lax.all_gather(in_weight, ('seq', 'fsdp'), axis=0, tiled=True)  48.6 us
    all_gather x1, waiting for transfers between devices, local(): lax.all_gather(out_weight, ('seq', 'fsdp'), axis=0, tiled=True)  47.3 us
    all_gather x1, blocking collectives, local(): lax.all_gather(conv_weight, ('seq', 'fsdp'), axis=1, tiled=True)  40.5 us
  transfers between devices with their start and end apart: 9, of which 5 were waited for; matrix products, arithmetic and copies ran while one was open for 19% of the time, Pallas kernels for 0%

commit v1 on v0

v1 whole, which is shorter than its diff:
```python
import functools
import jax
import jax.numpy as jnp
from jax import lax
from jax.experimental import pallas as pl
from jax.experimental.pallas import tpu as pltpu
from jax.sharding import PartitionSpec as P

INNER = 3072
HEADS = 48
HEAD_DIM = 64
STATE = 128
CONV = 4
BLOCK_LEN = 256
CHANNELS = 3328
PROJ = 6448
EDGE = 16
GROUP = 4
GROUPS = HEADS // GROUP
GCOLS = GROUP * HEAD_DIM
PAIRS = GROUP // 2
STRIP = 128
LOG2E = 1.4426950408889634
F32 = jnp.float32
BF16 = jnp.bfloat16

NT = (((1,), (1,)), ((), ()))
TN = (((0,), (0,)), ((), ()))
NN = (((1,), (0,)), ((), ()))


def dot(a, b, dims=NN):
    return lax.dot_general(a, b, dims, preferred_element_type=F32)


def first_half(shape):
    return lax.broadcasted_iota(jnp.int32, shape, len(shape) - 1) < HEAD_DIM


def per_pair(cols, kind, pair, rows):
    at = kind * GROUP + 2 * pair
    left, right = cols[rows, at : at + 1], cols[rows, at + 1 : at + 2]
    shape = (left.shape[0], 2 * HEAD_DIM)
    return jnp.where(
        first_half(shape), jnp.broadcast_to(left, shape), jnp.broadcast_to(right, shape)
    )


def convolved(p_ref, w_ref, b_ref, lo, count, lanes):
    out = b_ref[0:1, lanes] + jnp.zeros((count, lanes.size), F32)
    for tap in range(CONV):
        at = EDGE - CONV + 1 + tap + lo
        out = out + p_ref[at : at + count, lanes] * w_ref[tap : tap + 1, lanes]
    return out


def sigmoid(v):
    return 0.5 + 0.5 * jnp.tanh(0.5 * v)


def softplus(v):
    return jnp.maximum(v, 0.0) + jnp.log1p(jnp.exp(-jnp.abs(v)))


def lower_triangle():
    row = lax.broadcasted_iota(jnp.int32, (BLOCK_LEN, BLOCK_LEN), 0)
    col = lax.broadcasted_iota(jnp.int32, (BLOCK_LEN, BLOCK_LEN), 1)
    return jnp.where(row >= col, 1.0, 0.0)


def exact_dot(a, b, dims=NN):
    return lax.dot_general(
        a, b, dims, precision=lax.Precision.HIGHEST, preferred_element_type=F32
    )


def steps_kernel(
    p_ref, w_ref, b_ref, bias_ref, decay_ref, cols_ref, rows_ref, maps_ref, er_ref, decays_ref
):
    positions = maps_ref.shape[0]
    blocks = positions // BLOCK_LEN
    lower = lower_triangle()
    used = lax.broadcasted_iota(jnp.int32, (1, 128), 1) < HEADS
    rate = -jnp.exp(decay_ref[...])
    total = jnp.zeros((1, 128), F32)
    for block in range(blocks):
        lo = block * BLOCK_LEN
        rows = slice(lo, lo + BLOCK_LEN)
        conv = convolved(p_ref, w_ref, b_ref, lo, BLOCK_LEN, pl.ds(0, 2 * STATE))
        maps_ref[rows, :] = (conv * sigmoid(conv)).astype(BF16)
        step = softplus(p_ref[EDGE + lo : EDGE + lo + BLOCK_LEN, 2 * STATE : 2 * STATE + 128] + bias_ref[...])
        step = jnp.where(used, step, 0.0)
        run = exact_dot(lower, rate * step)
        end = run[BLOCK_LEN - 1 :]
        total = total + end
        run2 = run * LOG2E
        grown = jnp.exp(run)
        er_ref[rows, :] = grown
        decays_ref[block : block + 1, :] = jnp.exp(end)
        turned = run2.T
        kinds = (step, run2, grown, jnp.exp(end - run))
        for group in range(GROUPS):
            heads = slice(group * GROUP, (group + 1) * GROUP)
            rows_ref[group, :, rows] = turned[heads]
            cols_ref[group, rows, :] = jnp.concatenate([kind[:, heads] for kind in kinds], axis=1)
    decays_ref[blocks : blocks + 1, :] = jnp.exp(total)
    decays_ref[blocks + 1 :, :] = jnp.zeros((8 - blocks - 1, 128), F32)


def steps_of(p, w, b, bias, decay_log, positions):
    ext = p.shape[0]
    at = INNER // PIECE
    return pl.pallas_call(
        steps_kernel,
        grid=(1,),
        in_specs=[
            pl.BlockSpec((ext, PIECE), lambda i: (0, at)),
            pl.BlockSpec((8, PIECE), lambda i: (0, at)),
            pl.BlockSpec((1, PIECE), lambda i: (0, at)),
            pl.BlockSpec((1, 128), lambda i: (0, 0)),
            pl.BlockSpec((1, 128), lambda i: (0, 0)),
        ],
        out_specs=[pl.BlockSpec(memory_space=pltpu.VMEM)] * 5,
        out_shape=[
            jax.ShapeDtypeStruct((GROUPS, positions, 4 * GROUP), F32),
            jax.ShapeDtypeStruct((GROUPS, GROUP, positions), F32),
            jax.ShapeDtypeStruct((positions, 2 * STATE), BF16),
            jax.ShapeDtypeStruct((positions, 128), F32),
            jax.ShapeDtypeStruct((8, 128), F32),
        ],
        compiler_params=pltpu.CompilerParams(vmem_limit_bytes=48 * 2**20),
        cost_estimate=pl.CostEstimate(
            flops=4 * positions * BLOCK_LEN * 128, bytes_accessed=16 * positions * 512,
            transcendentals=positions * 1024,
        ),
        name="steps",
    )(p, w, b, bias, decay_log)


def masked_scores(maps_ref, scores_ref, blocks):
    row = lax.broadcasted_iota(jnp.int32, (BLOCK_LEN, BLOCK_LEN), 0)
    col = lax.broadcasted_iota(jnp.int32, (BLOCK_LEN, BLOCK_LEN), 1)
    for block in range(blocks):
        rows = slice(block * BLOCK_LEN, (block + 1) * BLOCK_LEN)
        scores = dot(maps_ref[rows, STATE:], maps_ref[rows, :STATE], NT)
        scores_ref[block] = jnp.where(row >= col, scores, 0.0)


def chain_copy(site, group, by, sent, got, send_sem, recv_sem):
    return pltpu.make_async_remote_copy(
        src_ref=sent.at[group % sent.shape[0]], dst_ref=got.at[group], send_sem=send_sem.at[group],
        recv_sem=recv_sem.at[group], device_id=(site.over(by), site.f), device_id_type=MESH,
    )


def by_head(decays, group, kind, rows=GCOLS):
    return jnp.concatenate(
        [
            jnp.full((HEAD_DIM, STATE), decays[kind, group * GROUP + head], F32)
            for head in range(rows // HEAD_DIM)
        ],
        axis=0,
    )


def scan_forward_kernel(
    pieces, lag, decays, p_ref, w_ref, b_ref, cols_ref, late_ref, rows_ref, maps_ref, skip_ref, own,
    y_ref, starts_ref, whole,
    scores_ref, x_ref, states_ref, sent, got, chain_send, chain_recv, *gather_refs,
):
    positions = y_ref.shape[0]
    blocks = positions // BLOCK_LEN
    step = pl.program_id(0)
    site = Site()
    behind = site.zs - 1

    @pl.when(step == 0)
    def _():
        site.greet()
        masked_scores(maps_ref, scores_ref, blocks)

    gather = Gather(site, own, whole, *gather_refs)
    at_stages(gather.stages, pieces, lag, step, gather.run)

    @pl.when(step < GROUPS)
    def _():
        slot = step % site.zs
        for pair in range(PAIRS):
            lanes = pl.ds(pair * 2 * HEAD_DIM, 2 * HEAD_DIM)
            for block in range(blocks):
                lo = block * BLOCK_LEN
                rows = slice(lo, lo + BLOCK_LEN)
                conv = convolved(p_ref, w_ref, b_ref, lo, BLOCK_LEN, lanes)
                x = conv * sigmoid(conv)
                x_ref[slot, rows, lanes] = x
                xs = x * per_pair(cols_ref, 0, pair, rows)
                ended = (xs * per_pair(cols_ref, 3, pair, rows)).astype(BF16)
                states_ref[slot, block, pair * 2 * HEAD_DIM : (pair + 1) * 2 * HEAD_DIM, :] = dot(
                    ended, maps_ref[rows, :STATE], TN
                )

    linked = step - site.z

    @pl.when(jnp.logical_and(linked >= 0, linked < GROUPS))
    def _():
        slot = linked % site.zs

        @pl.when(site.z == 0)
        def _():
            got[linked] = jnp.zeros((GCOLS, STATE), BF16)

        @pl.when(site.z > 0)
        def _():
            chain_copy(site, linked, 1, sent, got, chain_send, chain_recv).wait_recv()

        @pl.when(site.z < behind)
        def _():
            final = states_ref[slot, 0]
            for block in range(1, blocks):
                final = by_head(decays, linked, block) * final + states_ref[slot, block]
            sent[linked % sent.shape[0]] = (
                by_head(decays, linked, blocks) * got[linked].astype(F32) + final
            ).astype(BF16)
            chain_copy(site, linked, 1, sent, got, chain_send, chain_recv).start()

    group = step - behind

    @pl.when(jnp.logical_and(group >= 0, group < GROUPS))
    def _():
        slot = group % site.zs
        start = got[group].astype(F32)
        for block in range(blocks):
            if block:
                start = by_head(decays, group, block - 1) * start + states_ref[slot, block - 1]
            starts_ref[block] = start.astype(BF16)
        half = first_half((BLOCK_LEN, 2 * HEAD_DIM))
        for pair in range(PAIRS):
            lanes = pl.ds(pair * 2 * HEAD_DIM, 2 * HEAD_DIM)
            span = slice(pair * 2 * HEAD_DIM, (pair + 1) * 2 * HEAD_DIM)
            for block in range(blocks):
                lo = block * BLOCK_LEN
                rows = slice(lo, lo + BLOCK_LEN)
                x = x_ref[slot, rows, lanes]
                low = (x * per_pair(late_ref, 0, pair, rows)).astype(BF16)
                none = jnp.zeros_like(low)
                one, two = jnp.where(half, low, none), jnp.where(half, none, low)
                rest = skip_ref[0:1, lanes] * x + dot(
                    maps_ref[rows, STATE:], starts_ref[block, span, :], NT
                ) * per_pair(late_ref, 2, pair, rows)
                for strip in range(BLOCK_LEN // STRIP):
                    top = strip * STRIP
                    lim = top + STRIP
                    pieces_ = []
                    for side in range(2):
                        head = 2 * pair + side
                        at = GROUP + head
                        gap = (
                            late_ref[lo + top : lo + lim, at : at + 1]
                            - rows_ref[head : head + 1, lo : lo + lim]
                        )
                        decay = jnp.exp2(jnp.minimum(gap, 0.0))
                        pieces_.append((scores_ref[block, top:lim, :lim] * decay).astype(BF16))
                    y = dot(pieces_[0], one[:lim]) + dot(pieces_[1], two[:lim])
                    y_ref[lo + top : lo + lim, lanes] = y + rest[top:lim]

        @pl.when(site.z < behind)
        def _():
            chain_copy(site, group, 1, sent, got, chain_send, chain_recv).wait_send()


def hosted_steps(pieces, stages):
    zs = lax.axis_size("seq")
    steps = GROUPS + zs - 1
    lag = max(1, (steps - pieces) // (stages - 1))
    return max(steps, pieces + lag * (stages - 1)), lag


def chain_scratch():
    ring = max(lax.axis_size("seq"), LAG + 2)
    return [
        pltpu.VMEM((ring, GCOLS, STATE), BF16),
        pltpu.VMEM((GROUPS, GCOLS, STATE), BF16),
        pltpu.SemaphoreType.DMA((GROUPS,)),
        pltpu.SemaphoreType.DMA((GROUPS,)),
    ]


def scan_forward(decays, p, w, b, cols, rows, maps, skip, own, positions, collective_id):
    blocks = positions // BLOCK_LEN
    ext = p.shape[0]
    zs, n = lax.axis_size("seq"), lax.axis_size("fsdp")
    rows_there, columns = own.shape[1:]
    pieces = columns // PIECE
    steps, lag = hosted_steps(pieces, stages_of(n) - 1)

    def early(s):
        return jnp.minimum(s, GROUPS - 1)

    def late(s):
        return jnp.clip(s - (zs - 1), 0, GROUPS - 1)

    anywhere = pl.BlockSpec(memory_space=pl.ANY)
    return pl.pallas_call(
        functools.partial(scan_forward_kernel, pieces, lag),
        grid=(steps,),
        in_specs=[
            pl.BlockSpec(memory_space=pltpu.SMEM),
            pl.BlockSpec((ext, GCOLS), lambda s: (0, early(s))),
            pl.BlockSpec((8, GCOLS), lambda s: (0, early(s))),
            pl.BlockSpec((1, GCOLS), lambda s: (0, early(s))),
            pl.BlockSpec((None, positions, 4 * GROUP), lambda s: (early(s), 0, 0)),
            pl.BlockSpec((None, positions, 4 * GROUP), lambda s: (late(s), 0, 0)),
            pl.BlockSpec((None, GROUP, positions), lambda s: (late(s), 0, 0)),
            pl.BlockSpec((positions, 2 * STATE), lambda s: (0, 0)),
            pl.BlockSpec((1, GCOLS), lambda s: (0, late(s))),
            anywhere,
        ],
        out_specs=[
            pl.BlockSpec((positions, GCOLS), lambda s: (0, late(s))),
            pl.BlockSpec((blocks, GCOLS, STATE), lambda s: (0, late(s), 0)),
            anywhere,
        ],
        out_shape=[
            jax.ShapeDtypeStruct((positions, INNER), F32),
            jax.ShapeDtypeStruct((blocks, INNER, STATE), BF16),
            jax.ShapeDtypeStruct((zs, n, rows_there, columns), BF16),
        ],
        scratch_shapes=[
            pltpu.VMEM((blocks, BLOCK_LEN, BLOCK_LEN), F32),
            pltpu.VMEM((zs, positions, GCOLS), F32),
            pltpu.VMEM((zs, blocks, GCOLS, STATE), F32),
        ]
        + chain_scratch()
        + gather_scratch(pieces),
        compiler_params=pltpu.CompilerParams(
            collective_id=collective_id, has_side_effects=True, vmem_limit_bytes=48 * 2**20
        ),
        cost_estimate=pl.CostEstimate(
            flops=12 * positions * INNER * BLOCK_LEN, bytes_accessed=24 * positions * INNER,
            transcendentals=HEADS * positions * BLOCK_LEN,
        ),
        name="scan_forward",
    )(decays, p, w, b, cols, cols, rows, maps, skip, own)


def gate_kernel(
    y_ref, gate_ref, gno_ref, gain_ref, er_ref, maps_ref,
    out_ref, dy_ref, dye_ref, ggate_ref, ends_ref, gated_ref,
):
    rows = y_ref.shape[0]
    width = 2 * HEAD_DIM
    shape = (rows, width)
    square = jnp.zeros(shape, F32)
    cross = jnp.zeros(shape, F32)

    def decayed(pair):
        return jnp.where(
            first_half(shape),
            jnp.broadcast_to(er_ref[:, 2 * pair : 2 * pair + 1], shape),
            jnp.broadcast_to(er_ref[:, 2 * pair + 1 : 2 * pair + 2], shape),
        )

    for pair in range(HEADS // 2):
        lanes = slice(pair * width, (pair + 1) * width)
        gate = gate_ref[:, lanes]
        gated = y_ref[:, lanes] * gate * sigmoid(gate)
        gated_ref[:, lanes] = gated
        square = square + gated * gated
        cross = cross + gated * (gain_ref[:, lanes] * gno_ref[:, lanes])
    r1 = lax.rsqrt(jnp.sum(square, axis=-1, keepdims=True) * (1.0 / INNER) + 1e-05)
    back = r1 * r1 * r1 * (jnp.sum(cross, axis=-1, keepdims=True) * (1.0 / INNER))

    @pl.when(pl.program_id(0) % (BLOCK_LEN // rows) == 0)
    def _():
        ends_ref[...] = jnp.zeros_like(ends_ref)

    for pair in range(HEADS // 2):
        lanes = slice(pair * width, (pair + 1) * width)
        gate = gate_ref[:, lanes]
        sig = sigmoid(gate)
        gated = gated_ref[:, lanes]
        gain = gain_ref[:, lanes]
        out_ref[:, lanes] = (gated * r1 * gain).astype(BF16)
        ggated = gno_ref[:, lanes] * r1 * gain - gated * back
        low = (ggated * (gate * sig)).astype(BF16)
        dy_ref[:, lanes] = low
        ggate_ref[:, lanes] = (
            ggated * y_ref[:, lanes] * (sig * (1.0 + gate * (1.0 - sig)))
        ).astype(BF16)
        scaled = (low.astype(F32) * decayed(pair)).astype(BF16)
        dye_ref[:, lanes] = scaled
        ends_ref[lanes, :] += dot(scaled, maps_ref[:, STATE:], TN)


def gated(y, gate, gno, gain, er, maps):
    positions = y.shape[0]
    tile = 128
    per_block = BLOCK_LEN // tile
    wide = pl.BlockSpec((tile, INNER), lambda i: (i, 0))
    states = pl.BlockSpec((None, INNER, STATE), lambda i: (i // per_block, 0, 0))
    low = jax.ShapeDtypeStruct((positions, INNER), BF16)
    return pl.pallas_call(
        gate_kernel,
        grid=(positions // tile,),
        in_specs=[
            wide,
            wide,
            wide,
            pl.BlockSpec((1, INNER), lambda i: (0, 0)),
            pl.BlockSpec((tile, 128), lambda i: (i, 0)),
            pl.BlockSpec((tile, 2 * STATE), lambda i: (i, 0)),
        ],
        out_specs=[wide] * 4 + [states],
        out_shape=[
            low,
            low,
            low,
            low,
            jax.ShapeDtypeStruct((positions // BLOCK_LEN, INNER, STATE), F32),
        ],
        scratch_shapes=[pltpu.VMEM((tile, INNER), F32)],
        compiler_params=pltpu.CompilerParams(vmem_limit_bytes=48 * 2**20),
        cost_estimate=pl.CostEstimate(
            flops=4 * positions * INNER * STATE, bytes_accessed=24 * positions * INNER,
            transcendentals=2 * positions * INNER,
        ),
        name="gate",
    )(y, gate, gno, gain, er, maps)


OUT_PIECES = 6
OUT_SPLIT = 2


def scan_backward_kernel(
    decays, p_ref, w_ref, b_ref, cols_ref, rows_ref, maps_ref, skip_ref, y_ref, dy_ref,
    dye_ref, st_ref, grads_ref, turned_ref, cot_ref, ggate_ref, wgate_ref, wconv_ref,
    plast_ref, wlast_ref, blast_ref, bias_ref, decay_ref, grown_ref, tokens_ref, gain_ref,
    own_ref, gtokens_ref, total_ref,
    scores_ref, dscores_ref, dpad_ref, gacc_ref, dl_ref, x_ref, tail_ref, runs_ref, direct_ref, ends_ref,
    cross_ref, sent, got, chain_send, chain_recv, edge_sent, edge_got, edge_send, edge_recv,
    t_sent, t_got, t_send, t_recv, *scatter_refs,
):
    step_at = pl.program_id(0)
    site = Site()
    behind = site.zs - 1
    positions = y_ref.shape[0]
    gates = INNER // PIECE
    ahead = PIECE // GCOLS
    later = step_at - OUT_PIECES

    @pl.when(step_at == 0)
    def _():
        site.greet()
        gtokens_ref[...] = jnp.zeros_like(gtokens_ref)
        runs_ref[...] = jnp.zeros_like(runs_ref)
        direct_ref[...] = jnp.zeros_like(direct_ref)
        t_sent[0, CONV + 1 :, 0:INNER] = jnp.zeros((8 - CONV - 1, INNER), F32)

    def edge_copy(group):
        return pltpu.make_async_remote_copy(
            src_ref=edge_sent.at[group], dst_ref=edge_got.at[group], send_sem=edge_send.at[group],
            recv_sem=edge_recv.at[group], device_id=(site.over(behind), site.f), device_id_type=MESH,
        )

    def add_normed(weight_ref):
        def one(i, carry):
            span = pl.ds(pl.multiple_of(i * PIECE, 128), PIECE)
            gtokens_ref[:, span] += dot(x_ref[step_at % XRING], weight_ref[span, :], NT)
            return carry

        lax.fori_loop(0, gtokens_ref.shape[1] // PIECE, one, 0)

    @pl.when(step_at < OUT_PIECES)
    def _():
        cots = cot_ref.shape[1] // PIECE
        span = pl.ds(pl.multiple_of((step_at % cots) * PIECE, 128), PIECE)
        x_ref[step_at % XRING] = cot_ref[:, span]

    inside = jnp.logical_and(later >= 0, later < 2 * gates)

    @pl.when(jnp.logical_and(inside, later % 2 == 1))
    def _():
        x_ref[step_at % XRING] = ggate_ref[...]
        add_normed(wgate_ref)

    @pl.when(jnp.logical_and(inside, later % 2 == 0))
    def _():
        for side in range(ahead):
            group = (later // 2) * ahead + side
            lanes = slice(side * GCOLS, (side + 1) * GCOLS)

            @pl.when(site.z < behind)
            def _(group=group, lanes=lanes):
                edge_copy(group).wait_recv()
                x_ref[step_at % XRING, positions - 8 :, lanes] = (
                    tail_ref[group] + edge_got[group]
                ).astype(BF16)

            @pl.when(site.z > 0)
            def _(group=group):
                edge_copy(group).wait_send()

        add_normed(wconv_ref)

    last = OUT_PIECES + 2 * gates
    start = last - LAG - 1
    slot = last % XRING
    wide = 2 * STATE
    totals = Totals(site, t_sent, t_got, t_send, t_recv)

    def last_edge():
        return pltpu.make_async_remote_copy(
            src_ref=edge_sent.at[GROUPS], dst_ref=edge_got.at[GROUPS], send_sem=edge_send.at[GROUPS],
            recv_sem=edge_recv.at[GROUPS], device_id=(site.over(behind), site.f), device_id_type=MESH,
        )

    @pl.when(step_at == start)
    def _():
        tail, edge = maps_backward(plast_ref, wlast_ref, blast_ref, gacc_ref, dpad_ref, x_ref, slot, t_sent)
        tail_ref[GROUPS] = tail
        edge_sent[GROUPS] = edge

        @pl.when(site.z > 0)
        def _():
            last_edge().start()

        steps_backward(
            plast_ref, bias_ref, decay_ref, grown_ref, runs_ref, direct_ref, ends_ref, cross_ref, x_ref, slot,
            t_sent,
        )
        totals.start(0)

    for t in range(totals.count):

        @pl.when(step_at == start + 1 + t)
        def _(t=t):
            totals.next(t)

    @pl.when(step_at == start + 1 + totals.count)
    def _():
        total_ref[...] = t_sent[totals.count % 2]

    @pl.when(step_at == last)
    def _():
        @pl.when(site.z < behind)
        def _():
            last_edge().wait_recv()
            x_ref[slot, positions - 8 :, 0:wide] = (tail_ref[GROUPS] + edge_got[GROUPS]).astype(BF16)

        @pl.when(site.z > 0)
        def _():
            last_edge().wait_send()

        add_normed(wconv_ref)

    tile = 128
    after = step_at - last - 1

    @pl.when(jnp.logical_and(after >= 0, after < positions // tile))
    def _():
        rows = pl.ds(pl.multiple_of(after * tile, tile), tile)
        features = gtokens_ref.shape[1]
        inputs = tokens_ref[rows, :].astype(F32)
        r0 = lax.rsqrt(jnp.sum(inputs * inputs, axis=-1, keepdims=True) * (1.0 / features) + 1e-05)
        f = gain_ref[...] * gtokens_ref[rows, :]
        share = r0 * r0 * r0 * (jnp.sum(f * inputs, axis=-1, keepdims=True) * (1.0 / features))
        gtokens_ref[rows, :] = cot_ref[rows, :].astype(F32) + r0 * f - inputs * share

    def is_later(piece):
        return jnp.minimum(piece, OUT_PIECES) // OUT_PIECES

    def kind(piece):
        return (1 - is_later(piece)) * (1 + jnp.minimum(piece, OUT_PIECES - 1) // (OUT_PIECES // OUT_SPLIT))

    def column(piece):
        after = jnp.maximum(piece - OUT_PIECES, 0)
        return jnp.minimum(piece, OUT_PIECES) + is_later(piece) * (1 - after % 2) * gates + after // 2

    scatter = Streamed(site, turned_ref, kind, x_ref, own_ref, column, scatter_refs)
    at_stages(scatter.stages, last + 1, LAG, step_at, scatter.run)

    linked = step_at - (behind - site.z)
    blocks = positions // BLOCK_LEN

    @pl.when(jnp.logical_and(linked >= 0, linked < GROUPS))
    def _():
        @pl.when(site.z == behind)
        def _():
            got[linked] = jnp.zeros((GCOLS, STATE), BF16)

        @pl.when(site.z < behind)
        def _():
            chain_copy(site, linked, behind, sent, got, chain_send, chain_recv).wait_recv()

        @pl.when(site.z > 0)
        def _():
            span = pl.ds(pl.multiple_of(linked * GCOLS, GCOLS), GCOLS)
            grad = got[linked].astype(F32)
            for block in reversed(range(blocks)):
                grad = by_head(decays, linked, block) * grad + grads_ref[block, span, :]
            sent[linked % sent.shape[0]] = grad.astype(BF16)
            chain_copy(site, linked, behind, sent, got, chain_send, chain_recv).start()

    group = step_at - max(behind, LAG + 1)

    @pl.when(jnp.logical_and(group >= 0, group < GROUPS))
    def _():
        scan_backward_group(
            group, decays, p_ref, w_ref, b_ref, cols_ref, rows_ref, maps_ref, skip_ref, y_ref,
            dy_ref, dye_ref, st_ref, grads_ref, x_ref, tail_ref, edge_sent, t_sent, runs_ref, direct_ref,
            ends_ref, cross_ref, scores_ref, dscores_ref, dpad_ref, gacc_ref, dl_ref, got,
        )

        @pl.when(site.z > 0)
        def _():
            edge_copy(group).start()
            chain_copy(site, group, behind, sent, got, chain_send, chain_recv).wait_send()


def maps_backward(p_ref, w_ref, b_ref, grad_ref, dpad_ref, x_ref, slot, t_sent):
    positions, wide = grad_ref.shape
    blocks = positions // BLOCK_LEN
    lanes = pl.ds(0, wide)
    taps = [jnp.zeros((1, wide), F32) for _ in range(CONV + 1)]
    for block in range(blocks):
        lo = block * BLOCK_LEN
        conv = convolved(p_ref, w_ref, b_ref, lo, BLOCK_LEN, lanes)
        sig = sigmoid(conv)
        dconv = grad_ref[lo : lo + BLOCK_LEN, :] * (sig * (1.0 + conv * (1.0 - sig)))
        dpad_ref[8 + lo : 8 + lo + BLOCK_LEN, :] = dconv
        for tap in range(CONV):
            at = EDGE - CONV + 1 + tap + lo
            taps[tap] = taps[tap] + jnp.sum(
                dconv * p_ref[at : at + BLOCK_LEN, 0:wide], axis=0, keepdims=True
            )
        taps[CONV] = taps[CONV] + jnp.sum(dconv, axis=0, keepdims=True)
    for index in range(CONV + 1):
        t_sent[0, index : index + 1, INNER : INNER + wide] = taps[index]
    t_sent[0, CONV + 1 :, INNER : INNER + wide] = jnp.zeros((8 - CONV - 1, wide), F32)

    def back_rows(at, count):
        back = jnp.zeros((count, wide), F32)
        for tap in range(CONV):
            start = at + CONV - 1 - tap
            back = back + dpad_ref[start : start + count, :] * w_ref[tap : tap + 1, 0:wide]
        return back

    for block in range(blocks):
        lo = block * BLOCK_LEN
        x_ref[slot, lo : lo + BLOCK_LEN, 0:wide] = back_rows(8 + lo, BLOCK_LEN).astype(BF16)
    return back_rows(positions, 8), back_rows(0, 8)


def steps_backward(
    p_ref, bias_ref, decay_ref, decays_ref, runs_ref, direct_ref, ends_ref, cross_ref, x_ref, slot, t_sent
):
    positions = runs_ref.shape[0]
    blocks = positions // BLOCK_LEN
    wide = 2 * STATE
    used = lax.broadcasted_iota(jnp.int32, (1, 128), 1) < HEADS
    rate = -jnp.exp(decay_ref[...])
    by_heads = jnp.zeros((8, 128), F32)
    for at in range(0, INNER, PIECE):
        spread = jnp.where(
            (at + lax.broadcasted_iota(jnp.int32, (PIECE, 128), 0)) // HEAD_DIM
            == lax.broadcasted_iota(jnp.int32, (PIECE, 128), 1),
            1.0,
            0.0,
        )
        by_heads = by_heads + exact_dot(ends_ref[:, at : at + PIECE], spread)
    per_group = blocks * GROUP
    crossed = jnp.sum(cross_ref[...].reshape(GROUPS * per_group, STATE), axis=1, keepdims=True)
    row = lax.broadcasted_iota(jnp.int32, (GROUPS * per_group, 128), 0)
    lane = lax.broadcasted_iota(jnp.int32, (GROUPS * per_group, 128), 1)
    same = (row // per_group) * GROUP + row % GROUP == lane
    tri_row = lax.broadcasted_iota(jnp.int32, (BLOCK_LEN, BLOCK_LEN), 0)
    tri_col = lax.broadcasted_iota(jnp.int32, (BLOCK_LEN, BLOCK_LEN), 1)
    upper = jnp.where(tri_row <= tri_col, 1.0, 0.0)
    grad_bias = jnp.zeros((1, 128), F32)
    grad_decay = jnp.zeros((1, 128), F32)
    for block in range(blocks):
        lo = block * BLOCK_LEN
        rows = slice(lo, lo + BLOCK_LEN)
        here = jnp.logical_and(same, (row % per_group) // GROUP == block)
        end = by_heads[block : block + 1] + decays_ref[block : block + 1, :] * jnp.sum(
            jnp.where(here, crossed, 0.0), axis=0, keepdims=True
        )
        arg = p_ref[EDGE + lo : EDGE + lo + BLOCK_LEN, wide : wide + 128] + bias_ref[...]
        step = softplus(arg)
        grad_log = exact_dot(upper, runs_ref[rows, :]) + end
        grad_step = jnp.where(used, (direct_ref[rows, :] + rate * grad_log) * sigmoid(arg), 0.0)
        grad_bias = grad_bias + jnp.sum(grad_step, axis=0, keepdims=True)
        grad_decay = grad_decay + jnp.sum(
            jnp.where(used, grad_log * (rate * step), 0.0), axis=0, keepdims=True
        )
        x_ref[slot, rows, wide : wide + 128] = grad_step.astype(BF16)
        x_ref[slot, rows, wide + 128 :] = jnp.zeros((BLOCK_LEN, PIECE - wide - 128), BF16)
    t_sent[0, :, INNER + wide :] = jnp.concatenate(
        [grad_bias, grad_decay, by_heads[blocks : blocks + 1], jnp.zeros((5, 128), F32)], axis=0
    )


def scan_backward_group(
    step_at, decays, p_ref, w_ref, b_ref, cols_ref, rows_ref, maps_ref, skip_ref, y_ref, dy_ref,
    dye_ref, st_ref, grads_ref, x_ref, tail_ref, edge_ref, t_sent, runs_ref, direct_ref, ends_ref,
    cross_ref, scores_ref, dscores_ref, dpad_ref, gacc_ref, dl_ref, got,
):
    positions = y_ref.shape[0]
    blocks = positions // BLOCK_LEN
    width = 2 * HEAD_DIM

    @pl.when(step_at == 0)
    def _():
        masked_scores(maps_ref, scores_ref, blocks)
        ends_ref[...] = jnp.zeros_like(ends_ref)
        dscores_ref[...] = jnp.zeros_like(dscores_ref)
        gacc_ref[...] = jnp.zeros_like(gacc_ref)
        dpad_ref[0:8, :] = jnp.zeros((8, GCOLS), F32)
        dpad_ref[positions + 8 : positions + 16, :] = jnp.zeros((8, GCOLS), F32)

    ahead = PIECE // GCOLS
    slot = (OUT_PIECES + 2 * (step_at // ahead)) % XRING
    offset = (step_at % ahead) * GCOLS
    group_span = pl.ds(pl.multiple_of(step_at * GCOLS, GCOLS), GCOLS)
    grad = got[step_at].astype(F32)
    for block in reversed(range(blocks)):
        if block < blocks - 1:
            grad = by_head(decays, step_at, block + 1) * grad + grads_ref[block + 1, group_span, :]
        dl_ref[block] = grad.astype(BF16)
        product = grad * st_ref[block].astype(F32)
        for head in range(GROUP):
            at = block * GROUP + head
            cross_ref[step_at, at : at + 1, :] = jnp.sum(
                product[head * HEAD_DIM : (head + 1) * HEAD_DIM], axis=0, keepdims=True
            )

    half = first_half((BLOCK_LEN, width))
    for pair in range(PAIRS):
        lanes = pl.ds(pair * width, width)
        span = slice(pair * width, (pair + 1) * width)
        gw = [jnp.zeros((1, width), F32) for _ in range(CONV + 2)]
        for block in range(blocks):
            lo = block * BLOCK_LEN
            rows = slice(lo, lo + BLOCK_LEN)
            conv = convolved(p_ref, w_ref, b_ref, lo, BLOCK_LEN, lanes)
            sig = sigmoid(conv)
            x = conv * sig
            step = per_pair(cols_ref, 0, pair, rows)
            to_end = per_pair(cols_ref, 3, pair, rows)
            xs = x * step
            low = xs.astype(BF16)
            ended = (xs * to_end).astype(BF16)
            dyl = dy_ref[rows, lanes]
            dyf = dyl.astype(F32)
            none = jnp.zeros_like(dyl)
            sides = (jnp.where(half, dyl, none), jnp.where(half, none, dyl))
            turned = dyf.T.astype(BF16)
            dxt = [None, None]
            for strip in range(BLOCK_LEN // STRIP):
                top = strip * STRIP
                lim = top + STRIP
                scores = scores_ref[block, top:lim, :lim]
                gathered = jnp.zeros((STRIP, lim), F32)
                for side in range(2):
                    head = 2 * pair + side
                    at = GROUP + head
                    gap = (
                        cols_ref[lo + top : lo + lim, at : at + 1]
                        - rows_ref[head : head + 1, lo : lo + lim]
                    )
                    decay = jnp.exp2(jnp.minimum(gap, 0.0))
                    gathered = gathered + dot(sides[side][top:lim], low[:lim], NT) * decay
                    part = dot(
                        turned[side * HEAD_DIM : (side + 1) * HEAD_DIM, top:lim],
                        (scores * decay).astype(BF16),
                    )
                    if strip == 0:
                        dxt[side] = jnp.concatenate(
                            [part, jnp.zeros((HEAD_DIM, BLOCK_LEN - STRIP), F32)], axis=1
                        )
                    else:
                        dxt[side] = dxt[side] + part
                dscores_ref[block, top:lim, :lim] += gathered
            inner = jnp.concatenate(dxt, axis=0).T
            dls = dl_ref[block, span, :]
            outer = dot(maps_ref[rows, :STATE], dls, NT) * to_end
            gacc_ref[rows, :STATE] += dot(ended, dls)
            gacc_ref[rows, STATE:] += dot(dye_ref[rows, lanes], st_ref[block, span, :])
            dxs = inner + outer
            skip = skip_ref[0:1, lanes]
            vs = xs * outer
            runs = dyf * (y_ref[rows, lanes] - skip * x) - low.astype(F32) * inner - vs
            direct = x * dxs
            lane = lax.broadcasted_iota(jnp.int32, (BLOCK_LEN, 128), 1)
            for sums_ref, values in ((runs_ref, runs), (direct_ref, direct)):
                left = jnp.sum(jnp.where(half, values, 0.0), axis=1, keepdims=True)
                right = jnp.sum(jnp.where(half, 0.0, values), axis=1, keepdims=True)
                at = step_at * GROUP + 2 * pair
                sums_ref[rows, :] += jnp.where(
                    lane == at, left, jnp.where(lane == at + 1, right, 0.0)
                )
            group_lanes = pl.ds(pl.multiple_of(step_at * GCOLS + pair * width, width), width)
            ends_ref[block : block + 1, group_lanes] = jnp.sum(vs, axis=0, keepdims=True)
            gw[CONV + 1] = gw[CONV + 1] + jnp.sum(dyf * x, axis=0, keepdims=True)
            dconv = (dxs * step + skip * dyf) * (sig * (1.0 + conv * (1.0 - sig)))
            gw[CONV] = gw[CONV] + jnp.sum(dconv, axis=0, keepdims=True)
            dpad_ref[8 + lo : 8 + lo + BLOCK_LEN, lanes] = dconv
            for tap in range(CONV):
                at = EDGE - CONV + 1 + tap + lo
                gw[tap] = gw[tap] + jnp.sum(
                    dconv * p_ref[at : at + BLOCK_LEN, lanes], axis=0, keepdims=True
                )
        group_lanes = pl.ds(pl.multiple_of(step_at * GCOLS + pair * width, width), width)
        for index in range(CONV + 1):
            t_sent[0, index : index + 1, group_lanes] = gw[index]
        ends_ref[blocks : blocks + 1, group_lanes] = gw[CONV + 1]
        edge = jnp.zeros((8, width), F32)
        for tap in range(CONV):
            edge = edge + dpad_ref[CONV - 1 - tap : CONV - 1 - tap + 8, lanes] * w_ref[tap : tap + 1, lanes]
        edge_ref[step_at, :, lanes] = edge
        for block in range(blocks):
            lo = block * BLOCK_LEN
            back = jnp.zeros((BLOCK_LEN, width), F32)
            for tap in range(CONV):
                at = 8 + CONV - 1 - tap + lo
                back = back + dpad_ref[at : at + BLOCK_LEN, lanes] * w_ref[tap : tap + 1, lanes]
            x_ref[slot, lo : lo + BLOCK_LEN, pl.ds(pl.multiple_of(offset + pair * width, width), width)] = (
                back.astype(BF16)
            )
            if block == blocks - 1:
                tail_ref[step_at, :, lanes] = back[BLOCK_LEN - 8 :]

    @pl.when(step_at == GROUPS - 1)
    def _():
        row = lax.broadcasted_iota(jnp.int32, (BLOCK_LEN, BLOCK_LEN), 0)
        col = lax.broadcasted_iota(jnp.int32, (BLOCK_LEN, BLOCK_LEN), 1)
        for block in range(blocks):
            rows = slice(block * BLOCK_LEN, (block + 1) * BLOCK_LEN)
            low = jnp.where(row >= col, dscores_ref[block], 0.0).astype(BF16)
            gacc_ref[rows, :STATE] += dot(low, maps_ref[rows, STATE:], TN)
            gacc_ref[rows, STATE:] += dot(low, maps_ref[rows, :STATE])


def scan_backward(
    decays, p, w, b, cols, rows, maps, skip, y, dy, dye, starts, ends, turned, cot, grad_gate,
    inw_gate, inw_conv, bias, decay_log, tokens, gain, own_rows, collective_id,
):
    positions = y.shape[0]
    features = inw_gate.shape[0]
    blocks = positions // BLOCK_LEN
    ext = p.shape[0]
    zs, n = lax.axis_size("seq"), lax.axis_size("fsdp")
    gates = INNER // PIECE
    pieces = OUT_PIECES + 2 * gates + 1
    count = exchange_count(zs, n)
    steps = pieces + max(LAG * (stages_of(n) - 1), count - LAG)
    width = CHANNELS + 128
    dma = pltpu.SemaphoreType.DMA

    def late(s):
        return jnp.clip(s - max(zs - 1, LAG + 1), 0, GROUPS - 1)

    def turn(s, most):
        return jnp.clip((s - OUT_PIECES) // 2, 0, most)

    once = pl.Buffered(1)
    own = pl.BlockSpec((positions, GCOLS), lambda s: (0, late(s)))
    eight = pl.BlockSpec((8, GCOLS), lambda s: (0, late(s)))
    states = pl.BlockSpec((blocks, GCOLS, STATE), lambda s: (0, late(s), 0))

    def whole(x):
        return pl.BlockSpec(x.shape, lambda s: (0,) * len(x.shape), pipeline_mode=once)

    return pl.pallas_call(
        scan_backward_kernel,
        grid=(steps,),
        in_specs=[
            pl.BlockSpec(memory_space=pltpu.SMEM),
            pl.BlockSpec((ext, GCOLS), lambda s: (0, late(s))),
            eight,
            pl.BlockSpec((1, GCOLS), lambda s: (0, late(s))),
            pl.BlockSpec((None, positions, 4 * GROUP), lambda s: (late(s), 0, 0)),
            pl.BlockSpec((None, GROUP, positions), lambda s: (late(s), 0, 0)),
            whole(maps),
            pl.BlockSpec((1, GCOLS), lambda s: (0, late(s))),
            own,
            own,
            own,
            states,
            whole(ends),
            whole(turned),
            whole(cot),
            pl.BlockSpec((positions, PIECE), lambda s: (0, turn(s - 1, gates - 1))),
            pl.BlockSpec((features, PIECE), lambda s: (0, turn(s - 1, gates - 1))),
            pl.BlockSpec((features, PIECE), lambda s: (0, turn(s, gates))),
            pl.BlockSpec((ext, PIECE), lambda s: (0, gates), pipeline_mode=once),
            pl.BlockSpec((8, PIECE), lambda s: (0, gates), pipeline_mode=once),
            pl.BlockSpec((1, PIECE), lambda s: (0, gates), pipeline_mode=once),
            whole(bias),
            whole(decay_log),
            whole(decays),
            whole(tokens),
            whole(gain),
        ],
        out_specs=[
            pl.BlockSpec((own_rows, pieces * PIECE), lambda s: (0, 0), pipeline_mode=once),
            pl.BlockSpec((positions, features), lambda s: (0, 0), pipeline_mode=once),
            pl.BlockSpec((8, width), lambda s: (0, 0), pipeline_mode=once),
        ],
        out_shape=[
            jax.ShapeDtypeStruct((own_rows, pieces * PIECE), F32),
            jax.ShapeDtypeStruct((positions, features), F32),
            jax.ShapeDtypeStruct((8, width), F32),
        ],
        scratch_shapes=[
            pltpu.VMEM((blocks, BLOCK_LEN, BLOCK_LEN), F32),
            pltpu.VMEM((blocks, BLOCK_LEN, BLOCK_LEN), F32),
            pltpu.VMEM((positions + 16, GCOLS), F32),
            pltpu.VMEM((positions, 2 * STATE), F32),
            pltpu.VMEM((blocks, GCOLS, STATE), BF16),
            pltpu.VMEM((XRING, positions, PIECE), BF16),
            pltpu.VMEM((GROUPS + 1, 8, GCOLS), F32),
            pltpu.VMEM((positions, 128), F32),
            pltpu.VMEM((positions, 128), F32),
            pltpu.VMEM((8, INNER), F32),
            pltpu.VMEM((GROUPS, blocks * GROUP, STATE), F32),
        ]
        + chain_scratch()
        + [
            pltpu.VMEM((GROUPS + 1, 8, GCOLS), F32),
            pltpu.VMEM((GROUPS + 1, 8, GCOLS), F32),
            dma((GROUPS + 1,)),
            dma((GROUPS + 1,)),
            pltpu.VMEM((2, 8, width), F32),
            pltpu.VMEM((count, 8, width), F32),
            dma((count,)),
            dma((count,)),
        ]
        + Streamed.scratch(own_rows),
        compiler_params=pltpu.CompilerParams(
            collective_id=collective_id, has_side_effects=True, vmem_limit_bytes=63 * 2**20
        ),
        cost_estimate=pl.CostEstimate(
            flops=24 * positions * INNER * BLOCK_LEN, bytes_accessed=30 * positions * INNER,
            transcendentals=HEADS * positions * BLOCK_LEN,
        ),
        name="scan_backward",
    )(
        decays, p, w, b, cols, rows, maps, skip, y, dy, dye, starts, ends, turned, cot, grad_gate,
        inw_gate, inw_conv, p, w, b, bias, decay_log, decays, tokens, gain,
    )


PIECE = 512
LAG = 2
HALF = PIECE // 2
MESH = pl.DeviceIdType.MESH


class Site:
    def __init__(self):
        self.zs, self.n = lax.axis_size("seq"), lax.axis_size("fsdp")
        self.z, self.f = lax.axis_index("seq"), lax.axis_index("fsdp")
        self.chips = self.n // 2
        self.bits = self.chips.bit_length() - 1

    def bit(self, j):
        return (self.f // 2**j) % 2

    def flip(self, js):
        f = self.f
        for j in js:
            f = f + (1 - 2 * self.bit(j)) * 2**j
        return f

    def over(self, dz):
        return (self.z + dz) % self.zs

    def greet(self):
        barrier = pltpu.get_barrier_semaphore()
        for dz in range(1, self.zs):
            pl.semaphore_signal(barrier, inc=1, device_id=(self.over(dz), self.f), device_id_type=MESH)
        for j in range(self.bits + 1):
            pl.semaphore_signal(barrier, inc=1, device_id=(self.z, self.flip([j])), device_id_type=MESH)
        pl.semaphore_wait(barrier, self.zs + self.bits)


def subsets(js):
    found = [()]
    for j in js:
        found = found + [s + (j,) for s in found]
    return found


class Gather:
    def __init__(self, site, own, whole, local_sem, send_sem, recv_sem):
        self.site, self.own, self.whole = site, own, whole
        self.local_sem, self.send_sem, self.recv_sem = local_sem, send_sem, recv_sem
        self.along = len(own.shape) == 2
        self.skipped = 0 if self.along else 1
        self.stages = site.bits + 3 - self.skipped

    @staticmethod
    def slots(zs, n):
        return zs + 4 * (n // 2 - 1)

    def moves(self, piece):
        s = self.site
        start = piece * PIECE
        whole = pl.ds(pl.multiple_of(start, 128), PIECE)
        halves = (
            pl.ds(pl.multiple_of(start, 128), HALF),
            pl.ds(pl.multiple_of(start + HALF, 128), HALF),
        )
        slot = 0
        plan = [[] for _ in range(s.bits + 3)]
        for dz in range(1, s.zs):
            if not self.along:
                slot += 1
                continue
            plan[0].append(
                (slot, self.own.at[:, whole], self.whole.at[s.z, s.f, :, whole],
                 (s.over(dz), s.f), self.whole.at[s.over(s.zs - dz), s.f, :, whole])
            )
            slot += 1
        sibling = s.flip([0])

        def known(js, cols):
            if not js and not self.along:
                return self.own.at[:, :, cols]
            return self.whole.at[:, s.flip(js), :, cols]

        def shared(js, cols):
            return (slot, known(js, cols), self.whole.at[:, s.flip(js), :, cols],
                    (s.z, sibling), self.whole.at[:, s.flip(list(js) + [0]), :, cols])

        plan[1].append(shared([], whole))
        slot += 1
        up = list(range(1, s.bits + 1))
        for half, order in enumerate((up, up[::-1])):
            cols = halves[half]
            for at, j in enumerate(order):
                for js in subsets(order[:at]):
                    js = list(js)
                    plan[at + 1].append(
                        (slot, known(js, cols), self.whole.at[:, s.flip(js), :, cols],
                         (s.z, s.flip([j])), self.whole.at[:, s.flip(js + [j]), :, cols])
                    )
                    slot += 1
                    plan[at + 2].append(shared(js + [j], cols))
                    slot += 1
        return plan[self.skipped :]

    def leaving(self, piece, moves):
        return [
            pltpu.make_async_remote_copy(
                src_ref=src, dst_ref=dst, send_sem=self.send_sem.at[piece, slot],
                recv_sem=self.recv_sem.at[piece, slot], device_id=device, device_id_type=MESH,
            )
            for slot, src, dst, device, _ in moves
        ]

    def arriving(self, piece, moves):
        return [
            pltpu.make_async_remote_copy(
                src_ref=src, dst_ref=incoming, send_sem=self.send_sem.at[piece, slot],
                recv_sem=self.recv_sem.at[piece, slot], device_id=device, device_id_type=MESH,
            )
            for slot, src, _, device, incoming in moves
        ]

    def run(self, stage, piece):
        s = self.site
        plan = self.moves(piece)
        cols = pl.ds(pl.multiple_of(piece * PIECE, 128), PIECE)

        def local():
            if self.along:
                src, dst = self.own.at[:, cols], self.whole.at[s.z, s.f, :, cols]
            else:
                src, dst = self.own.at[:, :, cols], self.whole.at[:, s.f, :, cols]
            return pltpu.make_async_copy(src, dst, self.local_sem.at[piece])

        to_core = [[m for m in moves if self.is_core(stage_at, m)] for stage_at, moves in enumerate(plan)]
        others = [[m for m in moves if not self.is_core(stage_at, m)] for stage_at, moves in enumerate(plan)]
        if stage == 0:
            local().start()
        if stage == 1:
            local().wait()
        if 0 < stage:
            for copy in self.arriving(piece, others[stage - 1]):
                copy.wait_recv()
        if stage < self.stages - 1:
            for copy in self.leaving(piece, others[stage] + to_core[stage]):
                copy.start()
        else:
            for moves in to_core:
                for copy in self.arriving(piece, moves):
                    copy.wait_recv()
            for moves in plan:
                for copy in self.leaving(piece, moves):
                    copy.wait_send()

    def is_core(self, stage, move):
        slot = move[0]
        zs = self.site.zs
        if slot < zs - 1:
            return False
        return (slot - (zs - 1)) % 2 == 0


def at_stages(stages, pieces, lag, step, run):
    for stage in reversed(range(stages)):
        piece = step - lag * stage

        @pl.when(jnp.logical_and(piece >= 0, piece < pieces))
        def _(stage=stage, piece=piece):
            run(stage, piece)


def stages_of(n):
    return (n // 2).bit_length() + 2


def along_line(step, start, site, own, line, local_sem, send_sem, recv_sem):
    local = functools.partial(pltpu.make_async_copy, own, line.at[site.z], local_sem)

    def passing(hop, way):
        z = site.z - way * hop
        return pltpu.make_async_remote_copy(
            src_ref=own if hop == 0 else line.at[z], dst_ref=line.at[z],
            send_sem=send_sem.at[hop, (1 - way) // 2], recv_sem=recv_sem.at[hop, (1 - way) // 2],
            device_id=(site.z + way, site.f), device_id_type=MESH,
        )

    def arriving(hop, way):
        z = site.z - way * (hop + 1)
        return pltpu.make_async_remote_copy(
            src_ref=own, dst_ref=line.at[z],
            send_sem=send_sem.at[hop, (1 - way) // 2], recv_sem=recv_sem.at[hop, (1 - way) // 2],
            device_id=(site.z - way, site.f), device_id_type=MESH,
        )

    def inside(z):
        return jnp.logical_and(z >= 0, z < site.zs)

    for hop in range(site.zs):

        @pl.when(step == start + LAG * hop)
        def _(hop=hop):
            if hop == 0:
                local().start()
            else:
                for way in (1, -1):

                    @pl.when(inside(site.z - way * hop))
                    def _(way=way):
                        arriving(hop - 1, way).wait_recv()

            if hop < site.zs - 1:
                for way in (1, -1):

                    @pl.when(jnp.logical_and(inside(site.z - way * hop), inside(site.z + way)))
                    def _(way=way):
                        passing(hop, way).start()

            else:
                local().wait()
                for early in range(site.zs - 1):
                    for way in (1, -1):

                        @pl.when(jnp.logical_and(inside(site.z - way * early), inside(site.z + way)))
                        def _(way=way, early=early):
                            passing(early, way).wait_send()


def gather_kernel(pieces, start, own, late, last, whole, line, before, *refs):
    step = pl.program_id(0)
    site = Site()

    @pl.when(step == 0)
    def _():
        site.greet()

    edge_send, edge_recv = refs[3:5]

    def edge():
        return pltpu.make_async_remote_copy(
            src_ref=last, dst_ref=before, send_sem=edge_send, recv_sem=edge_recv,
            device_id=(site.over(1), site.f), device_id_type=MESH,
        )

    @pl.when(step == 0)
    def _():
        edge().start()

    gather = Gather(site, own, whole, *refs[:3])
    at_stages(gather.stages, pieces, LAG, step, gather.run)
    along_line(step, start, site, late, line, *refs[5:])

    @pl.when(step == pl.num_programs(0) - 1)
    def _():
        edge().wait()


def gather_scratch(pieces):
    slots = Gather.slots(lax.axis_size("seq"), lax.axis_size("fsdp"))
    return [
        pltpu.SemaphoreType.DMA((pieces,)),
        pltpu.SemaphoreType.DMA((pieces, slots)),
        pltpu.SemaphoreType.DMA((pieces, slots)),
    ]


def gathered(own, late, last, collective_id):
    rows, columns = own.shape
    zs, n = lax.axis_size("seq"), lax.axis_size("fsdp")
    pieces = columns // PIECE
    steps = max(pieces + LAG * (stages_of(n) - 1), LAG * zs)
    start = min(pieces // 2, steps - LAG * (zs - 1) - 1)
    anywhere = pl.BlockSpec(memory_space=pl.ANY)
    dma = pltpu.SemaphoreType.DMA
    return pl.pallas_call(
        functools.partial(gather_kernel, pieces, start),
        grid=(steps,),
        in_specs=[anywhere] * 3,
        out_specs=[anywhere] * 3,
        out_shape=[
            jax.ShapeDtypeStruct((zs, n, rows, columns), own.dtype),
            jax.ShapeDtypeStruct((zs,) + late.shape, late.dtype),
            jax.ShapeDtypeStruct(last.shape, last.dtype),
        ],
        scratch_shapes=gather_scratch(pieces) + [dma, dma, dma, dma((zs - 1, 2)), dma((zs - 1, 2))],
        compiler_params=pltpu.CompilerParams(collective_id=collective_id, has_side_effects=True),
        cost_estimate=pl.CostEstimate(
            flops=0, bytes_accessed=2 * zs * n * rows * columns, transcendentals=0
        ),
        name="gather_rows",
    )(own, late, last)


class Scatter:
    def take(self, refs):
        bits = self.site.bits
        self.kept = refs[:bits]
        self.sent = refs[bits : 2 * bits]
        self.got = refs[2 * bits : 3 * bits]
        self.z_kept, self.z_sent, self.z_got, self.send_sem, self.recv_sem = refs[3 * bits :]
        self.stages = bits + 3

    @staticmethod
    def common(pieces, rows):
        zs, n = lax.axis_size("seq"), lax.axis_size("fsdp")
        chips = n // 2
        bits = chips.bit_length() - 1
        slots = 1 + 2 * bits + zs - 1
        steps = [(pieces, 2, zs, chips >> (k + 1), rows, HALF) for k in range(bits)]
        return (
            [pltpu.VMEM(s, F32) for s in steps]
            + [pltpu.VMEM(s, BF16) for s in steps]
            + [pltpu.VMEM(s, BF16) for s in steps]
            + [
                pltpu.VMEM((pieces, rows, PIECE), F32),
                pltpu.VMEM((pieces, zs, rows, PIECE), BF16),
                pltpu.VMEM((pieces, zs - 1, rows, PIECE), BF16),
                pltpu.SemaphoreType.DMA((pieces, slots)),
                pltpu.SemaphoreType.DMA((pieces, slots)),
            ]
        )

    def remote(self, piece, slot, src, dst, device):
        at = self.at(piece)
        return pltpu.make_async_remote_copy(
            src_ref=src, dst_ref=dst, send_sem=self.send_sem.at[at, slot],
            recv_sem=self.recv_sem.at[at, slot], device_id=device, device_id_type=MESH,
        )

    def order(self, half):
        up = list(range(1, self.site.bits + 1))
        return up[::-1] if half == 0 else up

    def across(self, piece, k, half):
        s, at = self.site, self.at(piece)
        return self.remote(
            piece, 1 + 2 * k + half, self.sent[k].at[at, half], self.got[k].at[at, half],
            (s.z, s.flip([self.order(half)[k]])),
        )

    def along(self, piece, dz):
        s, at = self.site, self.at(piece)
        return self.remote(
            piece, 2 * s.bits + dz, self.z_sent.at[at, s.over(dz)], self.z_got.at[at, dz - 1],
            (s.over(dz), s.f),
        )

    def run(self, stage, piece):
        s, at = self.site, self.at(piece)
        bits = s.bits
        if stage == 0:
            self.begin(piece)
            self.to_core(piece).start()
            return
        if stage == 1:
            self.join(piece)
            self.to_core(piece).wait()
        elif stage <= bits + 1:
            for half in range(2):
                self.across(piece, stage - 2, half).wait()
        if stage <= bits:
            k = stage - 1
            for half in range(2):
                order = self.order(half)
                left = sorted(order[k:])
                j = order[k]
                place = left.index(j)
                mine = s.bit(j)

                def one(zi, carry, half=half, k=k, place=place, mine=mine):
                    for i in range(s.chips >> (k + 1)):
                        low = i % 2**place
                        base = (i - low) * 2 + low
                        self.sent[k][at, half, zi, i] = self.current(
                            k, piece, half, zi, base + (1 - mine) * 2**place
                        ).astype(BF16)
                        self.kept[k][at, half, zi, i] = self.current(
                            k, piece, half, zi, base + mine * 2**place
                        )
                    return carry

                lax.fori_loop(0, s.zs, one, 0)
                self.across(piece, k, half).start()
        elif stage == bits + 1:
            for half in range(2):
                lanes = slice(half * HALF, (half + 1) * HALF)

                def one(zi, carry, half=half, lanes=lanes):
                    self.z_sent[at, zi, :, lanes] = self.current(bits, piece, half, zi, 0).astype(BF16)
                    return carry

                lax.fori_loop(0, s.zs, one, 0)
                self.z_kept[at, :, lanes] = self.current(bits, piece, half, s.z, 0)
            for dz in range(1, s.zs):
                self.along(piece, dz).start()
        else:
            total = self.z_kept[at]
            for dz in range(1, s.zs):
                self.along(piece, dz).wait()
                total = total + self.z_got[at, dz - 1].astype(F32)
            self.out[:, pl.ds(pl.multiple_of(self.column(piece) * PIECE, 128), PIECE)] = total

    def current(self, k, piece, half, zi, index):
        at = self.at(piece)
        lanes = slice(half * HALF, (half + 1) * HALF)
        if k == 0:
            return self.first(piece, zi, index, lanes) + self.came[at, zi, index, :, lanes].astype(F32)
        return self.kept[k - 1][at, half, zi, index] + self.got[k - 1][at, half, zi, index].astype(F32)


RING = 4
XRING = 6


class Streamed(Scatter):
    def __init__(self, site, turned, kind, x, out, column, refs):
        self.site, self.turned, self.x, self.out = site, turned, x, out
        self.kind, self.column = kind, column
        self.ring, self.x_ring = refs[0].shape[0], x.shape[0]
        self.away, self.own, self.came = refs[:3]
        self.take(refs[3:])

    @staticmethod
    def scratch(rows, ring=RING):
        zs, n = lax.axis_size("seq"), lax.axis_size("fsdp")
        full = (zs, n // 2, rows, PIECE)
        return [
            pltpu.VMEM((ring,) + full, BF16),
            pltpu.VMEM(full, F32),
            pltpu.VMEM((ring,) + full, BF16),
        ] + Scatter.common(ring, rows)

    def at(self, piece):
        return piece % self.ring

    def to_core(self, piece):
        s, at = self.site, self.at(piece)
        return self.remote(piece, 0, self.away.at[at], self.came.at[at], (s.z, s.flip([0])))

    def product(self, core, piece, store):
        s = self.site
        rows = self.away.shape[3]
        together = 2 - s.zs % 2
        count = together * s.chips * rows

        def one(i, carry):
            lhs = self.turned[self.kind(piece), core, pl.ds(pl.multiple_of(i * count, 16), count), :]
            value = dot(lhs, self.x[piece % self.x_ring]).reshape(together, s.chips, rows, PIECE)
            store(pl.ds(i * together, together), value)
            return carry

        lax.fori_loop(0, s.zs // together, one, 0)

    def begin(self, piece):
        at = self.at(piece)

        def store(zi, value):
            self.away[at, zi] = value.astype(BF16)

        self.product(1 - self.site.bit(0), piece, store)

    def join(self, piece):
        def store(zi, value):
            self.own[zi] = value

        self.product(self.site.bit(0), piece, store)

    def first(self, piece, zi, index, lanes):
        return self.own[zi, index, :, lanes]


def exchange_count(zs, n):
    return (n.bit_length() - 1) + (zs.bit_length() - 1)


class Totals:
    def __init__(self, site, sent, got, send_sem, recv_sem):
        self.site, self.sent, self.got = site, sent, got
        self.send_sem, self.recv_sem = send_sem, recv_sem
        self.count = exchange_count(site.zs, site.n)

    def move(self, t):
        s = self.site
        if t <= s.bits:
            device = (s.z, s.flip([t]))
        else:
            j = t - s.bits - 1
            device = (s.z + (1 - 2 * ((s.z // 2**j) % 2)) * 2**j, s.f)
        return pltpu.make_async_remote_copy(
            src_ref=self.sent.at[t % 2], dst_ref=self.got.at[t], send_sem=self.send_sem.at[t],
            recv_sem=self.recv_sem.at[t], device_id=device, device_id_type=MESH,
        )

    def start(self, t):
        if t < self.count:
            self.move(t).start()

    def next(self, t):
        if t < self.count:
            self.move(t).wait()
            self.sent[(t + 1) % 2] = self.sent[t % 2] + self.got[t]
            self.start(t + 1)


CONV_COLS = 3584


def local(
    tokens, pre_gain, in_weight, conv_weight, conv_bias, step_bias, decay_log, skip_gain,
    norm_gain, out_weight, cotangent,
):
    both = ("seq", "fsdp")
    _, positions, features = tokens.shape
    blocks = positions // BLOCK_LEN
    devices = lax.axis_size("seq") * lax.axis_size("fsdp")

    rows = in_weight.shape[0]
    padded_rows = -(-rows // 16) * 16
    vectors = jnp.concatenate([pre_gain, conv_weight.reshape(-1), conv_bias, norm_gain])
    extra = -(-vectors.size // rows)
    sizes = (pre_gain.size, conv_weight.size, conv_bias.size, norm_gain.size)
    cuts = [sum(sizes[:i]) for i in range(5)]
    used = PROJ - INNER
    more_rows = ((0, padded_rows - rows), (0, 0))
    own = jnp.concatenate(
        [
            in_weight[:, INNER:],
            jnp.pad(vectors, (0, extra * rows - vectors.size)).reshape(rows, extra),
            jnp.zeros((rows, CONV_COLS - used - extra), BF16),
        ],
        axis=1,
    )
    inw_conv, gate_line, before = gathered(
        jnp.pad(own, more_rows),
        jnp.pad(in_weight[:, :INNER], more_rows),
        tokens[0, positions - EDGE :],
        1,
    )
    later, before = lax.optimization_barrier((out_weight, before))
    outw_full = lax.all_gather(later, both, axis=0, tiled=True)
    inw_conv = inw_conv[:, :, :rows].reshape(features, CONV_COLS)
    small_full = inw_conv[:, used : used + extra].reshape(devices, rows * extra)
    gain_full = small_full[:, : cuts[1]].reshape(1, features).astype(F32)
    convw_full = (
        small_full[:, cuts[1] : cuts[2]]
        .reshape(devices, CONV, -1)
        .transpose(1, 0, 2)
        .reshape(CONV, CHANNELS)
        .astype(F32)
    )
    convb_full = small_full[:, cuts[2] : cuts[3]].reshape(1, CHANNELS).astype(F32)
    normg_full = small_full[:, cuts[3] : cuts[4]].reshape(1, INNER).astype(F32)

    before = jnp.where(lax.axis_index("seq") == 0, jnp.zeros_like(before), before)
    ext = jnp.concatenate([before, tokens[0]], axis=0).astype(F32)
    r0_ext = lax.rsqrt(jnp.mean(ext * ext, axis=-1, keepdims=True) + 1e-05)
    normed_ext = (ext * r0_ext * gain_full).astype(BF16)
    inputs, r0, normed = ext[EDGE:], r0_ext[EDGE:], normed_ext[EDGE:]

    p = dot(normed_ext, inw_conv)
    unused = ((0, 0), (0, CONV_COLS - CHANNELS))
    w = jnp.pad(convw_full, ((0, 8 - CONV), (0, CONV_COLS - CHANNELS)))
    b = jnp.pad(convb_full, unused)
    wide_heads = ((0, 0), (0, 128 - HEADS))
    bias, decay_row = jnp.pad(step_bias[None], wide_heads), jnp.pad(decay_log[None], wide_heads)
    cols, run_rows, maps, run_exp, decays = steps_of(
        p, w, b, bias, decay_row, positions
    )
    skip = jnp.repeat(skip_gain, HEAD_DIM)[None]
    y, starts, inw_gate = scan_forward(
        decays, p, w, b, cols, run_rows, maps, skip, gate_line, positions, 2
    )
    inw_gate = inw_gate[:, :, :rows].reshape(features, INNER)
    gate = dot(normed, inw_gate)
    cot = cotangent[0]
    grad_normed_out = dot(cot, outw_full, NT)
    normed_out, dy, dye, grad_gate, ends = gated(
        y, gate, grad_normed_out, normg_full, run_exp, maps
    )
    mixed = (inputs + dot(normed_out, outw_full)).astype(BF16)[None]

    def turned(x, split):
        x = jnp.pad(x.T.reshape(-1, 2, split, rows, positions), ((0, 0),) * 3 + more_rows)
        return x.transpose(2, 1, 0, 3, 4).reshape(split, 2, -1, positions)

    turned_all = jnp.concatenate([turned(normed, 1), turned(normed_out, OUT_SPLIT)])
    own_main, grad_tokens, totals = scan_backward(
        decays, p, w, b, cols, run_rows, maps, skip, y, dy, dye, starts, ends, turned_all, cot, grad_gate,
        inw_gate, inw_conv, bias, decay_row, tokens[0], gain_full, padded_rows, 3,
    )
    own_main = own_main[:rows]
    out_cols = OUT_PIECES * PIECE
    own_out = own_main[:, :out_cols].reshape(rows, OUT_SPLIT, features).transpose(1, 0, 2)
    own_out = own_out.reshape(OUT_SPLIT * rows, features)
    own_in = own_main[:, out_cols : out_cols + PROJ]
    per_tap = conv_weight.shape[1]
    me = lax.axis_index("seq") * lax.axis_size("fsdp") + lax.axis_index("fsdp")
    own_taps = lax.dynamic_slice_in_dim(totals, me * per_tap, per_tap, axis=1)
    heads = totals[:3, CHANNELS : CHANNELS + HEADS]

    return (
        mixed,
        grad_tokens[None],
        jnp.sum(own_in * in_weight.astype(F32), axis=1) / pre_gain.astype(F32),
        own_in,
        own_taps[:CONV],
        own_taps[CONV],
        heads[0],
        heads[1],
        heads[2],
        jnp.sum(own_out * out_weight.astype(F32), axis=1) / norm_gain.astype(F32),
        own_out,
    )


def solution(mesh):
    split = P(("seq", "fsdp"), None)
    flat = P(("seq", "fsdp"))
    taps = P(None, ("seq", "fsdp"))
    data = P("fsdp", "seq", None)
    return jax.shard_map(
        local,
        mesh=mesh,
        in_specs=(data, flat, split, taps, flat, P(), P(), P(), flat, split, data),
        out_specs=(data, data, flat, split, taps, flat, P(), P(), P(), flat, split),
        check_vma=False,
    )
```

time: 1440 us -> 438 us (0.30)
  waiting for transfers between devices: 751 us -> 0.02 us
  Pallas kernels: 0 us -> 335 us
  matrix products: 271 us -> 43.3 us
  other arithmetic: 153 us -> 10.6 us
  local copies, waits for them, and re-layouts: 142 us -> 34.5 us
  blocking collectives: 94.6 us -> 0 us
    reduce_scatter x2 -> x0, waiting for transfers between devices: 581 us -> none  [the longest x1 371 us: local(): lax.psum_scatter(grad_in_weight, ('seq', 'fsdp'), scatter_dimension=0, ti...]
    pallas_call x0 -> x5, Pallas kernels: none -> 335 us  [the longest x1 174 us: scan_backward(): pl.pallas_call(scan_backward_kernel, grid=(steps,), in_specs=[pl.BlockSpe...]
    dot_general x21 -> x4, matrix products: 271 us -> 43.3 us  [dot(): return lax.dot_general(a, b, dims, preferred_element_type=F32)]
    all_gather x4 -> x1, waiting for transfers between devices: 95.9 us -> 0.01 us  [local(): outw_full = lax.all_gather(later, both, axis=0, tiled=True)]
    unnamed x8 -> x1, waiting for transfers between devices: 74.7 us -> 0.02 us
    reduce_sum x12 -> x3, other arithmetic: 68.5 us -> 3.45 us  [the longest x1 2.88 us: local(): jnp.sum(own_in * in_weight.astype(F32), axis=1) / pre_gain.astype(F32)]
    reshape x13 -> x4, local copies, waits for them, and re-layouts: 59.1 us -> 3.63 us  [the longest x1 2.37 us: local(): own_main[:, :out_cols].reshape(rows, OUT_SPLIT, features).transpose(1, 0, 2)]
    unnamed x2 -> x0, blocking collectives: 54.2 us -> none
  transfers between devices with their start and end apart: 9 -> 1, of which waited for: 5 -> 0; matrix products, arithmetic and copies ran while one was open for 19% -> 8% of each run, Pallas kernels for 0% -> 18%
where the time goes in v1:
time: 438 us; the launch traced here: 437 us
  Pallas kernels  335 us (76%)
  matrix products  43.3 us (10%)
  local copies, waits for them, and re-layouts  34.5 us (8%)
  between operations  14.4 us (3%)
  other arithmetic  10.6 us (2%)
    pallas_call x1, Pallas kernels, scan_backward(): pl.pallas_call(scan_backward_kernel, grid=(steps,), in_specs=[pl.BlockSpe...  174 us
    pallas_call x1, Pallas kernels, scan_forward(): pl.pallas_call(functools.partial(scan_forward_kernel, pieces, lag), grid=...  73.8 us
    pallas_call x1, Pallas kernels, gathered(): pl.pallas_call(functools.partial(gather_kernel, pieces, start), grid=(ste...  64.7 us
    dot_general x4, matrix products, dot(): return lax.dot_general(a, b, dims, preferred_element_type=F32)  43.3 us
    pallas_call x1, Pallas kernels, gated(): pl.pallas_call(gate_kernel, grid=(positions // tile,), in_specs=[wide, wi...  16 us
  transfers between devices with their start and end apart: 1, of which 0 were waited for; matrix products, arithmetic and copies ran while one was open for 8% of the time, Pallas kernels for 18%

profile of v1, /device:TPU:0, one launch (start us, length us, event | category | flops | bytes accessed | tf_op | source)
XLA Modules:
  0.0 437.4 jit_solution(4486800609264825542)
XLA Ops:
  8.4 1.7 slice.56.late
  11.7 1.4 slice_bitcast_fusion.1.last
  14.0 64.7 %gather_rows.1 = (bf16[4,8,48,3584]{3,2,1,0:T(8,128)(2,1)}, bf16[4,48,3072]{2,1,0:T(8,128)(2,1)}, bf16[16,1536]{1,0:T(8,128)(2,1)}) custom-call(bf16[48,3584]{1,0:T(8,128)(2,1)} %concatenate.13.own, bf16[48,3072]{1,0:T(8,128)(2,1)} %slice.56.late, bf16[16,1536]{1,0:T(8,128)(2,1)} %slice_bitcast_fusion.1.last), custom_call_target="tpu_custom_call" | custom-call | bytes 11010048 | tf_op jit(solution)/shard_map/gather_rows/pallas_call | solution.py:1224
  82.8 1.3 slice_bitcast_fusion
  84.2 2.6 copy.29
  86.8 2.7 copy.30
  89.5 11.2 %fusion.12.p_ref.plast_ref = f32[528,3584]{1,0:T(8,128)} fusion(bf16[528,1536]{1,0:T(8,128)(2,1)} %copy-done.16, bf16[1536,3584]{1,0:T(8,128)(2,1)} %bitcast.54), kind=kOutput, calls=%fused_computation.37 | convolution fusion | flops 5813305344 | bytes 20201472 | tf_op jit(solution)/shard_map/dot_general | solution.py:33
  100.8 5.6 %steps.1 = (f32[12,512,16]{2,1,0:T(8,128)S(1)}, f32[12,4,512]{2,1,0:T(4,128)S(1)}, bf16[512,256]{1,0:T(8,128)(2,1)S(1)}, f32[512,128]{1,0:T(8,128)S(1)}, f32[8,128]{1,0:T(8,128)S(1)}) custom-call(f32[528,3584]{1,0:T(8,128)} %fusion.12.p_ref.plast_ref, f32[8,3584]{1,0:T(8,128)S(1)} %pad_convert_fusion.w_ref.wlast_ref, ...), custom_call_target="tpu_custom_call" | custom-call | flops 67108864 | bytes 4194304 | tf_op jit(solution)/shard_map/steps/pallas_call | solution.py:113
  106.4 1.7 copy-done
  108.1 2.1 maximum_convert_fusion
  110.2 73.8 %scan_forward.1 = (f32[512,3072]{1,0:T(8,128)}, bf16[2,3072,128]{2,1,0:T(8,128)(2,1)S(1)}, bf16[4,8,48,3072]{3,2,1,0:T(8,128)(2,1)}) custom-call(f32[8,128]{1,0:T(8,128)S(1)} %get-tuple-element.35.decays.grown_ref, f32[528,3584]{1,0:T(8,128)} %fusion.12.p_ref.plast_ref, f32[8,3584]{1,0:T(8,128)S(1)} %pad_convert_fusion.w_ref.wlast_ref, ...), custom_call_target="tpu_custom_call" | custom-call | flops 4831838208 | bytes 37748736 | tf_op jit(solution)/shard_map/scan_forward/pallas_call | solution.py:303
  185.2 11.0 %fusion.2.gate_ref = f32[512,3072]{1,0:T(8,128)} fusion(bf16[1536,3072]{1,0:T(8,128)(2,1)} %bitcast.56, bf16[528,1536]{1,0:T(8,128)(2,1)S(1)} %copy-done.17), kind=kOutput, calls=%fused_computation.9 | convolution fusion | flops 4831838208 | bytes 17301504 | tf_op jit(solution)/shard_map/dot_general | solution.py:33
  196.2 10.7 %convolution_bitcast_fusion.gno_ref = f32[512,3072]{1,0:T(8,128)} fusion(bf16[3072,1536]{1,0:T(8,128)(2,1)} %all-gather.2.cloned.1.call-done, bf16[1,512,1536]{2,1,0:T(8,128)(2,1)S(1)} %copy-done.21), kind=kOutput, calls=%fused_computation | convolution fusion | flops 4831838208 | bytes 17301504 | tf_op jit(solution)/shard_map/dot_general | solution.py:33
  206.9 16.0 %gate.1 = (bf16[512,3072]{1,0:T(8,128)(2,1)S(1)}, bf16[512,3072]{1,0:T(8,128)(2,1)}, bf16[512,3072]{1,0:T(8,128)(2,1)}, bf16[512,3072]{1,0:T(8,128)(2,1)}, f32[2,3072,128]{2,1,0:T(8,128)}) custom-call(f32[512,3072]{1,0:T(8,128)} %get-tuple-element.40.y_ref, f32[512,3072]{1,0:T(8,128)} %fusion.2.gate_ref, f32[512,3072]{1,0:T(8,128)} %convolution_bitcast_fusion.gno_ref, ...), custom_call_target="tpu_custom_call" | custom-call | flops 805306368 | bytes 37748736 | tf_op jit(solution)/shard_map/gate/pallas_call | solution.py:402
  223.0 3.3 copy.31
  226.2 2.3 copy.32
  228.6 2.6 pad_maximum_fusion.turned_ref
  231.2 174.4 %scan_backward.1 = (f32[48,9728]{1,0:T(8,128)}, f32[512,1536]{1,0:T(8,128)}, f32[8,3456]{1,0:T(8,128)}) custom-call(f32[8,128]{1,0:T(8,128)} %copy-done.11, f32[528,3584]{1,0:T(8,128)} %fusion.12.p_ref.plast_ref, f32[8,3584]{1,0:T(8,128)} %copy-done.3, f32[1,3584]{1,0:T(1,128)} %copy-done.8, f32[12,512,16]{2,1,0:T(8,128)} %copy-done, ...), custom_call_target="tpu_custom_call" | custom-call | flops 9663676416 | bytes 47185920 | tf_op jit(solution)/shard_map/scan_backward/pallas_call | solution.py:875
  405.7 2.0 slice.71
  407.6 2.9 multiply_reduce_fusion.1
  412.4 1.3 slice_bitcast_fusion.2
  413.7 2.4 reshape.126
  418.5 10.4 %fusion.1 = bf16[1,512,1536]{2,1,0:T(8,128)(2,1)} fusion(bf16[512,3072]{1,0:T(8,128)(2,1)S(1)} %copy-done.2, bf16[3072,1536]{1,0:T(8,128)(2,1)} %all-gather.2.cloned.1.call-done, f32[528,1536]{1,0:T(8,128)} %maximum_convert_fusion), kind=kOutput, calls=%fused_computation.6 | convolution fusion | flops 4833411072 | bytes 17301504 | tf_op jit(solution)/shard_map/dot_general | solution.py:33
  428.9 1.7 copy.38
  (98 shorter events, 13.2 us)
Async XLA Ops:
  7.2 74.8 %copy-start.15 = (bf16[1,512,1536]{2,1,0:T(8,128)(2,1)S(1)}, bf16[1,512,1536]{2,1,0:T(8,128)(2,1)}, u32[]{:S(2)}) copy-start(bf16[1,512,1536]{2,1,0:T(8,128)(2,1)} %param.11) | copy-start | bytes 4718596
  7.2 74.3 %copy-start.28 = (f32[48]{0:T(128)S(1)}, f32[48]{0:T(128)}, u32[]{:S(2)}) copy-start(f32[48]{0:T(128)} %param.16) | copy-start | bytes 580
  7.2 74.3 %copy-start.29 = (f32[48]{0:T(128)S(1)}, f32[48]{0:T(128)}, u32[]{:S(2)}) copy-start(f32[48]{0:T(128)} %param.17) | copy-start | bytes 580
  7.2 74.3 %copy-start.25 = (f32[48]{0:T(128)S(1)}, f32[48]{0:T(128)}, u32[]{:S(2)}) copy-start(f32[48]{0:T(128)} %param.18) | copy-start | bytes 580
  7.2 189.0 %all-gather.2.cloned.1.call-start = ((), (), s32[]{:S(2)}) async-start(), calls=%async_computation | async-start | bytes 9732096 | tf_op jit(solution)/shard_map/all_gather | solution.py:1489
  81.5 19.2 %copy-start.12 = (f32[1,128]{1,0:T(1,128)}, f32[1,128]{1,0:T(1,128)S(1)}, u32[]{:S(2)}) copy-start(f32[1,128]{1,0:T(1,128)S(1)} %pad.28.bias_ref) | copy-start | bytes 1540
  81.6 19.2 %copy-start.13 = (f32[1,128]{1,0:T(1,128)}, f32[1,128]{1,0:T(1,128)S(1)}, u32[]{:S(2)}) copy-start(f32[1,128]{1,0:T(1,128)S(1)} %pad.29.decay_ref) | copy-start | bytes 1540
  81.7 28.5 %copy-start.10 = (f32[1,3072]{1,0:T(1,128)}, f32[1,3072]{1,0:T(1,128)S(1)}, u32[]{:S(2)}) copy-start(f32[1,3072]{1,0:T(1,128)S(1)} %broadcast_in_dim_reshape.3.skip_ref) | copy-start | bytes 36868
  89.5 20.7 %copy-start.8 = (f32[1,3584]{1,0:T(1,128)}, f32[1,3584]{1,0:T(1,128)S(1)}, u32[]{:S(2)}) copy-start(f32[1,3584]{1,0:T(1,128)S(1)} %pad_convert_fusion.1.b_ref.blast_ref) | copy-start | bytes 43012
  89.5 20.7 %copy-start.3 = (f32[8,3584]{1,0:T(8,128)}, f32[8,3584]{1,0:T(8,128)S(1)}, u32[]{:S(2)}) copy-start(f32[8,3584]{1,0:T(8,128)S(1)} %pad_convert_fusion.w_ref.wlast_ref) | copy-start | bytes 344068
  100.8 7.3 %copy-start.24 = (bf16[16,1536]{1,0:T(8,128)(2,1)S(1)}, bf16[16,1536]{1,0:T(8,128)(2,1)}, u32[]{:S(2)}) copy-start(bf16[16,1536]{1,0:T(8,128)(2,1)} %copy-done.23) | copy-start | bytes 147460
  108.0 76.0 %copy-start.6 = (f32[512,128]{1,0:T(8,128)}, f32[512,128]{1,0:T(8,128)S(1)}, u32[]{:S(2)}) copy-start(f32[512,128]{1,0:T(8,128)S(1)} %get-tuple-element.43.er_ref) | copy-start | bytes 786436
  108.0 76.0 %copy-start.9 = (f32[12,4,512]{2,1,0:T(4,128)}, f32[12,4,512]{2,1,0:T(4,128)S(1)}, u32[]{:S(2)}) copy-start(f32[12,4,512]{2,1,0:T(4,128)S(1)} %get-tuple-element.37.rows_ref) | copy-start | bytes 294916
  108.0 76.0 %copy-start.11 = (f32[8,128]{1,0:T(8,128)}, f32[8,128]{1,0:T(8,128)S(1)}, u32[]{:S(2)}) copy-start(f32[8,128]{1,0:T(8,128)S(1)} %get-tuple-element.35.decays.grown_ref) | copy-start | bytes 12292
  108.0 98.9 %copy-start.5 = (bf16[512,256]{1,0:T(8,128)(2,1)}, bf16[512,256]{1,0:T(8,128)(2,1)S(1)}, u32[]{:S(2)}) copy-start(bf16[512,256]{1,0:T(8,128)(2,1)S(1)} %get-tuple-element.38.maps_ref) | copy-start | bytes 786436
  110.2 75.0 %copy-start.17 = (bf16[528,1536]{1,0:T(8,128)(2,1)S(1)}, bf16[528,1536]{1,0:T(8,128)(2,1)}, u32[]{:S(2)}) copy-start(bf16[528,1536]{1,0:T(8,128)(2,1)} %copy-done.16) | copy-start | bytes 4866052
  185.2 11.0 %copy-start.21 = (bf16[1,512,1536]{2,1,0:T(8,128)(2,1)S(1)}, bf16[1,512,1536]{2,1,0:T(8,128)(2,1)}, u32[]{:S(2)}) copy-start(bf16[1,512,1536]{2,1,0:T(8,128)(2,1)} %param.21) | copy-start | bytes 4718596
  196.2 10.7 %copy-start.7 = (f32[512,128]{1,0:T(8,128)S(1)}, f32[512,128]{1,0:T(8,128)}, u32[]{:S(2)}) copy-start(f32[512,128]{1,0:T(8,128)} %copy-done.6) | copy-start | bytes 786436
  405.7 11.6 %copy-start.22 = (bf16[96,1536]{1,0:T(8,128)(2,1)S(1)}, bf16[96,1536]{1,0:T(8,128)(2,1)}, u32[]{:S(2)}) copy-start(bf16[96,1536]{1,0:T(8,128)(2,1)} %param.20) | copy-start | bytes 884740
  407.6 9.8 %copy-start.26 = (bf16[96]{0:T(256)(128)(2,1)S(1)}, bf16[96]{0:T(256)(128)(2,1)}, u32[]{:S(2)}) copy-start(bf16[96]{0:T(256)(128)(2,1)} %param.19) | copy-start | bytes 580
  407.6 10.4 %copy-start.27 = (bf16[48]{0:T(256)(128)(2,1)S(1)}, bf16[48]{0:T(256)(128)(2,1)}, u32[]{:S(2)}) copy-start(bf16[48]{0:T(256)(128)(2,1)} %param.12) | copy-start | bytes 292
  407.6 10.9 %copy-start.2 = (bf16[512,3072]{1,0:T(8,128)(2,1)S(1)}, bf16[512,3072]{1,0:T(8,128)(2,1)}, u32[]{:S(2)}) copy-start(bf16[512,3072]{1,0:T(8,128)(2,1)} %copy-done.1) | copy-start | bytes 9437188
  417.3 11.6 %copy-start.20 = (f32[2,48,1536]{2,1,0:T(8,128)}, f32[2,48,1536]{2,1,0:T(8,128)S(1)}, u32[]{:S(2)}) copy-start(f32[2,48,1536]{2,1,0:T(8,128)S(1)} %copy.33) | copy-start | bytes 1769476
  418.5 10.4 %copy-start.19 = (f32[512,1536]{1,0:T(8,128)S(1)}, f32[512,1536]{1,0:T(8,128)}, u32[]{:S(2)}) copy-start(f32[512,1536]{1,0:T(8,128)} %get-tuple-element.50) | copy-start | bytes 9437188
  (7 other events, 19.4 us)
Sparse Core Ops, SparseCore 0:
  78.8 104.2 all-gather.1

commit v2 on v1

--- a/solution.py
+++ b/solution.py
@@ -1,4 +1,5 @@
 import functools
+import math
 import jax
 import jax.numpy as jnp
 from jax import lax
@@ -20,6 +21,7 @@
 GCOLS = GROUP * HEAD_DIM
 PAIRS = GROUP // 2
 STRIP = 128
+PART = 64
 LOG2E = 1.4426950408889634
 F32 = jnp.float32
 BF16 = jnp.bfloat16
@@ -164,9 +166,9 @@
 
 
 def scan_forward_kernel(
-    pieces, lag, decays, p_ref, w_ref, b_ref, cols_ref, late_ref, rows_ref, maps_ref, skip_ref, own,
-    y_ref, starts_ref, whole,
-    scores_ref, x_ref, states_ref, sent, got, chain_send, chain_recv, *gather_refs,
+    pieces, decays, p_ref, w_ref, b_ref, cols_ref, late_ref, rows_ref, maps_ref, skip_ref, normed_ref, own,
+    y_ref, starts_ref, gate_ref, turned_ref, whole,
+    scores_ref, x_ref, states_ref, weight_ref, weight_sem, sent, got, chain_send, chain_recv, *gather_refs,
 ):
     positions = y_ref.shape[0]
     blocks = positions // BLOCK_LEN
@@ -179,8 +181,27 @@
         site.greet()
         masked_scores(maps_ref, scores_ref, blocks)
 
+    @pl.when(step == 1)
+    def _():
+        put_turned(normed_ref, own.shape[1], lambda at: turned_ref.at[at % 2, span_of(at // 2, own.shape[1])])
+
     gather = Gather(site, own, whole, *gather_refs)
-    at_stages(gather.stages, pieces, lag, step, gather.run)
+    arrived = step - LAG * (gather.stages - 1)
+
+    def weight_copy(piece):
+        cols = pl.ds(pl.multiple_of(piece * PIECE, 128), PIECE)
+        return pltpu.make_async_copy(whole.at[:, :, :, cols], weight_ref, weight_sem)
+
+    @pl.when(jnp.logical_and(arrived >= 1, arrived <= pieces))
+    def _():
+        weight_copy(arrived - 1).wait()
+        gate_ref[...] = dot(normed_ref[...], weight_ref[...].reshape(-1, PIECE))
+
+    at_stages(gather.stages, pieces, LAG, step, gather.run)
+
+    @pl.when(jnp.logical_and(arrived >= 0, arrived < pieces))
+    def _():
+        weight_copy(arrived).start()
 
     @pl.when(step < GROUPS)
     def _():
@@ -268,11 +289,16 @@
             chain_copy(site, group, 1, sent, got, chain_send, chain_recv).wait_send()
 
 
-def hosted_steps(pieces, stages):
-    zs = lax.axis_size("seq")
-    steps = GROUPS + zs - 1
-    lag = max(1, (steps - pieces) // (stages - 1))
-    return max(steps, pieces + lag * (stages - 1)), lag
+def span_of(at, rows):
+    return slice(at * rows, (at + 1) * rows)
+
+
+def put_turned(x_ref, rows, place, lanes=slice(None)):
+    together = rows * 128 // math.gcd(rows, 128)
+    for at in range(x_ref.shape[1] // together):
+        turned = x_ref[:, span_of(at, together)].astype(F32).T
+        for index in range(together // rows):
+            place(at * (together // rows) + index)[:, lanes] = turned[span_of(index, rows)].astype(BF16)
 
 
 def chain_scratch():
@@ -285,13 +311,14 @@
     ]
 
 
-def scan_forward(decays, p, w, b, cols, rows, maps, skip, own, positions, collective_id):
+def scan_forward(decays, p, w, b, cols, rows, maps, skip, normed, own, positions, collective_id):
     blocks = positions // BLOCK_LEN
     ext = p.shape[0]
     zs, n = lax.axis_size("seq"), lax.axis_size("fsdp")
     rows_there, columns = own.shape[1:]
     pieces = columns // PIECE
-    steps, lag = hosted_steps(pieces, stages_of(n) - 1)
+    wait = LAG * (stages_of(n) - 2) + 1
+    steps = max(GROUPS + zs - 1, pieces + wait)
 
     def early(s):
         return jnp.minimum(s, GROUPS - 1)
@@ -301,7 +328,7 @@
 
     anywhere = pl.BlockSpec(memory_space=pl.ANY)
     return pl.pallas_call(
-        functools.partial(scan_forward_kernel, pieces, lag),
+        functools.partial(scan_forward_kernel, pieces),
         grid=(steps,),
         in_specs=[
             pl.BlockSpec(memory_space=pltpu.SMEM),
@@ -313,22 +340,31 @@
             pl.BlockSpec((None, GROUP, positions), lambda s: (late(s), 0, 0)),
             pl.BlockSpec((positions, 2 * STATE), lambda s: (0, 0)),
             pl.BlockSpec((1, GCOLS), lambda s: (0, late(s))),
+            pl.BlockSpec(normed.shape, lambda s: (0, 0), pipeline_mode=pl.Buffered(1)),
             anywhere,
         ],
         out_specs=[
             pl.BlockSpec((positions, GCOLS), lambda s: (0, late(s))),
             pl.BlockSpec((blocks, GCOLS, STATE), lambda s: (0, late(s), 0)),
+            pl.BlockSpec((positions, PIECE), lambda s: (0, jnp.clip(s - wait, 0, pieces - 1))),
+            pl.BlockSpec(
+                (2, zs * n // 2 * rows_there, positions), lambda s: (0, 0, 0), pipeline_mode=pl.Buffered(1)
+            ),
             anywhere,
         ],
         out_shape=[
             jax.ShapeDtypeStruct((positions, INNER), F32),
             jax.ShapeDtypeStruct((blocks, INNER, STATE), BF16),
+            jax.ShapeDtypeStruct((positions, columns), F32),
+            jax.ShapeDtypeStruct((2, zs * n // 2 * rows_there, positions), BF16),
             jax.ShapeDtypeStruct((zs, n, rows_there, columns), BF16),
         ],
         scratch_shapes=[
             pltpu.VMEM((blocks, BLOCK_LEN, BLOCK_LEN), F32),
             pltpu.VMEM((zs, positions, GCOLS), F32),
             pltpu.VMEM((zs, blocks, GCOLS, STATE), F32),
+            pltpu.VMEM((zs, n, rows_there, PIECE), BF16),
+            pltpu.SemaphoreType.DMA,
         ]
         + chain_scratch()
         + gather_scratch(pieces),
@@ -340,13 +376,14 @@
             transcendentals=HEADS * positions * BLOCK_LEN,
         ),
         name="scan_forward",
-    )(decays, p, w, b, cols, cols, rows, maps, skip, own)
+    )(decays, p, w, b, cols, cols, rows, maps, skip, normed, own)
 
 
 def gate_kernel(
     y_ref, gate_ref, gno_ref, gain_ref, er_ref, maps_ref,
-    out_ref, dy_ref, dye_ref, ggate_ref, ends_ref, gated_ref,
+    out_ref, dy_ref, dye_ref, ggate_ref, ends_ref, *more_refs,
 ):
+    gated_ref = more_refs[-1]
     rows = y_ref.shape[0]
     width = 2 * HEAD_DIM
     shape = (rows, width)
@@ -391,14 +428,27 @@
         dye_ref[:, lanes] = scaled
         ends_ref[lanes, :] += dot(scaled, maps_ref[:, STATE:], TN)
 
-
-def gated(y, gate, gno, gain, er, maps):
+    if len(more_refs) == 2:
+        turned_ref = more_refs[0]
+        own_rows = INNER // (turned_ref.shape[0] * turned_ref.shape[1] * turned_ref.shape[2])
+
+        def place(at):
+            rest, split = at // OUT_SPLIT, at % OUT_SPLIT
+            return turned_ref.at[split, rest % 2, rest // 2]
+
+        put_turned(out_ref, own_rows, place)
+
+
+def gated(y, gate, gno, gain, er, maps, own_rows):
     positions = y.shape[0]
     tile = 128
     per_block = BLOCK_LEN // tile
     wide = pl.BlockSpec((tile, INNER), lambda i: (i, 0))
     states = pl.BlockSpec((None, INNER, STATE), lambda i: (i // per_block, 0, 0))
     low = jax.ShapeDtypeStruct((positions, INNER), BF16)
+    extra = []
+    if own_rows:
+        extra.append((OUT_SPLIT, 2, INNER // (2 * OUT_SPLIT * own_rows), own_rows, positions))
     return pl.pallas_call(
         gate_kernel,
         grid=(positions // tile,),
@@ -410,14 +460,17 @@
             pl.BlockSpec((tile, 128), lambda i: (i, 0)),
             pl.BlockSpec((tile, 2 * STATE), lambda i: (i, 0)),
         ],
-        out_specs=[wide] * 4 + [states],
+        out_specs=[wide] * 4
+        + [states]
+        + [pl.BlockSpec(turned[:-1] + (tile,), lambda i: (0, 0, 0, 0, i)) for turned in extra],
         out_shape=[
             low,
             low,
             low,
             low,
             jax.ShapeDtypeStruct((positions // BLOCK_LEN, INNER, STATE), F32),
-        ],
+        ]
+        + [jax.ShapeDtypeStruct(turned, BF16) for turned in extra],
         scratch_shapes=[pltpu.VMEM((tile, INNER), F32)],
         compiler_params=pltpu.CompilerParams(vmem_limit_bytes=48 * 2**20),
         cost_estimate=pl.CostEstimate(
@@ -428,18 +481,14 @@
     )(y, gate, gno, gain, er, maps)
 
 
-OUT_PIECES = 6
-OUT_SPLIT = 2
-
-
 def scan_backward_kernel(
     decays, p_ref, w_ref, b_ref, cols_ref, rows_ref, maps_ref, skip_ref, y_ref, dy_ref,
-    dye_ref, st_ref, grads_ref, turned_ref, cot_ref, ggate_ref, wgate_ref, wconv_ref,
+    dye_ref, st_ref, grads_ref, turned_ref, turned_out_ref, cot_ref, ggate_ref, wgate_ref, wconv_ref,
     plast_ref, wlast_ref, blast_ref, bias_ref, decay_ref, grown_ref, tokens_ref, gain_ref,
     own_ref, gtokens_ref, total_ref,
     scores_ref, dscores_ref, dpad_ref, gacc_ref, dl_ref, x_ref, tail_ref, runs_ref, direct_ref, ends_ref,
-    cross_ref, sent, got, chain_send, chain_recv, edge_sent, edge_got, edge_send, edge_recv,
-    t_sent, t_got, t_send, t_recv, *scatter_refs,
+    cross_ref, conv_ref, inner_ref, outer_ref, low_ref, ended_ref, sent, got, chain_send, chain_recv,
+    edge_sent, edge_got, edge_send, edge_recv, t_sent, t_got, t_send, t_recv, *scatter_refs,
 ):
     step_at = pl.program_id(0)
     site = Site()
@@ -463,10 +512,10 @@
             recv_sem=edge_recv.at[group], device_id=(site.over(behind), site.f), device_id_type=MESH,
         )
 
-    def add_normed(weight_ref):
+    def add_normed(weight_ref, grads_of):
         def one(i, carry):
             span = pl.ds(pl.multiple_of(i * PIECE, 128), PIECE)
-            gtokens_ref[:, span] += dot(x_ref[step_at % XRING], weight_ref[span, :], NT)
+            gtokens_ref[:, span] += dot(grads_of(), weight_ref[span, :], NT)
             return carry
 
         lax.fori_loop(0, gtokens_ref.shape[1] // PIECE, one, 0)
@@ -482,7 +531,6 @@
     @pl.when(jnp.logical_and(inside, later % 2 == 1))
     def _():
         x_ref[step_at % XRING] = ggate_ref[...]
-        add_normed(wgate_ref)
 
     @pl.when(jnp.logical_and(inside, later % 2 == 0))
     def _():
@@ -501,7 +549,7 @@
             def _(group=group):
                 edge_copy(group).wait_send()
 
-        add_normed(wconv_ref)
+        add_normed(wconv_ref, lambda: x_ref[step_at % XRING])
 
     last = OUT_PIECES + 2 * gates
     start = last - LAG - 1
@@ -552,32 +600,38 @@
         def _():
             last_edge().wait_send()
 
-        add_normed(wconv_ref)
+        add_normed(wconv_ref, lambda: x_ref[step_at % XRING])
+
+    after = step_at - last - 1
+
+    @pl.when(jnp.logical_and(after >= 0, after < gates))
+    def _():
+        add_normed(wgate_ref, lambda: ggate_ref[...])
 
     tile = 128
-    after = step_at - last - 1
-
-    @pl.when(jnp.logical_and(after >= 0, after < positions // tile))
-    def _():
-        rows = pl.ds(pl.multiple_of(after * tile, tile), tile)
-        features = gtokens_ref.shape[1]
-        inputs = tokens_ref[rows, :].astype(F32)
-        r0 = lax.rsqrt(jnp.sum(inputs * inputs, axis=-1, keepdims=True) * (1.0 / features) + 1e-05)
-        f = gain_ref[...] * gtokens_ref[rows, :]
-        share = r0 * r0 * r0 * (jnp.sum(f * inputs, axis=-1, keepdims=True) * (1.0 / features))
-        gtokens_ref[rows, :] = cot_ref[rows, :].astype(F32) + r0 * f - inputs * share
+
+    @pl.when(jnp.logical_and(after >= gates, after < gates + positions // (2 * tile)))
+    def _():
+        def one(i, carry):
+            rows = pl.ds(pl.multiple_of((after - gates) * 2 * tile + i * tile, tile), tile)
+            features = gtokens_ref.shape[1]
+            inputs = tokens_ref[rows, :].astype(F32)
+            r0 = lax.rsqrt(jnp.sum(inputs * inputs, axis=-1, keepdims=True) * (1.0 / features) + 1e-05)
+            f = gain_ref[...] * gtokens_ref[rows, :]
+            share = r0 * r0 * r0 * (jnp.sum(f * inputs, axis=-1, keepdims=True) * (1.0 / features))
+            gtokens_ref[rows, :] = cot_ref[rows, :].astype(F32) + r0 * f - inputs * share
+            return carry
+
+        lax.fori_loop(0, 2, one, 0)
 
     def is_later(piece):
         return jnp.minimum(piece, OUT_PIECES) // OUT_PIECES
-
-    def kind(piece):
-        return (1 - is_later(piece)) * (1 + jnp.minimum(piece, OUT_PIECES - 1) // (OUT_PIECES // OUT_SPLIT))
 
     def column(piece):
         after = jnp.maximum(piece - OUT_PIECES, 0)
         return jnp.minimum(piece, OUT_PIECES) + is_later(piece) * (1 - after % 2) * gates + after // 2
 
-    scatter = Streamed(site, turned_ref, kind, x_ref, own_ref, column, scatter_refs)
+    scatter = Streamed(site, turned_ref, turned_out_ref, is_later, x_ref, own_ref, column, scatter_refs)
     at_stages(scatter.stages, last + 1, LAG, step_at, scatter.run)
 
     linked = step_at - (behind - site.z)
@@ -609,7 +663,8 @@
         scan_backward_group(
             group, decays, p_ref, w_ref, b_ref, cols_ref, rows_ref, maps_ref, skip_ref, y_ref,
             dy_ref, dye_ref, st_ref, grads_ref, x_ref, tail_ref, edge_sent, t_sent, runs_ref, direct_ref,
-            ends_ref, cross_ref, scores_ref, dscores_ref, dpad_ref, gacc_ref, dl_ref, got,
+            ends_ref, cross_ref, scores_ref, dscores_ref, dpad_ref, gacc_ref, dl_ref, got, conv_ref, inner_ref,
+            outer_ref, low_ref, ended_ref,
         )
 
         @pl.when(site.z > 0)
@@ -704,7 +759,8 @@
 def scan_backward_group(
     step_at, decays, p_ref, w_ref, b_ref, cols_ref, rows_ref, maps_ref, skip_ref, y_ref, dy_ref,
     dye_ref, st_ref, grads_ref, x_ref, tail_ref, edge_ref, t_sent, runs_ref, direct_ref, ends_ref,
-    cross_ref, scores_ref, dscores_ref, dpad_ref, gacc_ref, dl_ref, got,
+    cross_ref, scores_ref, dscores_ref, dpad_ref, gacc_ref, dl_ref, got, conv_ref, inner_ref, outer_ref,
+    low_ref, ended_ref,
 ):
     positions = y_ref.shape[0]
     blocks = positions // BLOCK_LEN
@@ -736,26 +792,27 @@
             )
 
     half = first_half((BLOCK_LEN, width))
-    for pair in range(PAIRS):
-        lanes = pl.ds(pair * width, width)
-        span = slice(pair * width, (pair + 1) * width)
-        gw = [jnp.zeros((1, width), F32) for _ in range(CONV + 2)]
-        for block in range(blocks):
-            lo = block * BLOCK_LEN
-            rows = slice(lo, lo + BLOCK_LEN)
-            conv = convolved(p_ref, w_ref, b_ref, lo, BLOCK_LEN, lanes)
-            sig = sigmoid(conv)
-            x = conv * sig
-            step = per_pair(cols_ref, 0, pair, rows)
-            to_end = per_pair(cols_ref, 3, pair, rows)
-            xs = x * step
-            low = xs.astype(BF16)
-            ended = (xs * to_end).astype(BF16)
+    lane_row = lax.broadcasted_iota(jnp.int32, (width, 128), 0)
+    lane_col = lax.broadcasted_iota(jnp.int32, (width, 128), 1)
+    gw = [[jnp.zeros((8, width), F32) for _ in range(CONV + 2)] for _ in range(PAIRS)]
+    for block in range(blocks):
+        lo = block * BLOCK_LEN
+        rows = slice(lo, lo + BLOCK_LEN)
+        outer_ref[...] = dot(maps_ref[rows, :STATE], dl_ref[block], NT)
+        for pair in range(PAIRS):
+            lanes = pl.ds(pair * width, width)
+            for top in range(0, BLOCK_LEN, PART):
+                part = slice(lo + top, lo + top + PART)
+                here = slice(top, top + PART)
+                conv = convolved(p_ref, w_ref, b_ref, lo + top, PART, lanes)
+                conv_ref[here, :] = conv
+                xs = conv * sigmoid(conv) * per_pair(cols_ref, 0, pair, part)
+                low_ref[here, :] = xs.astype(BF16)
+                ended_ref[here, lanes] = (xs * per_pair(cols_ref, 3, pair, part)).astype(BF16)
             dyl = dy_ref[rows, lanes]
-            dyf = dyl.astype(F32)
             none = jnp.zeros_like(dyl)
             sides = (jnp.where(half, dyl, none), jnp.where(half, none, dyl))
-            turned = dyf.T.astype(BF16)
+            turned = dyl.astype(F32).T.astype(BF16)
             dxt = [None, None]
             for strip in range(BLOCK_LEN // STRIP):
                 top = strip * STRIP
@@ -770,7 +827,7 @@
                         - rows_ref[head : head + 1, lo : lo + lim]
                     )
                     decay = jnp.exp2(jnp.minimum(gap, 0.0))
-                    gathered = gathered + dot(sides[side][top:lim], low[:lim], NT) * decay
+                    gathered = gathered + dot(sides[side][top:lim], low_ref[:lim, :], NT) * decay
                     part = dot(
                         turned[side * HEAD_DIM : (side + 1) * HEAD_DIM, top:lim],
                         (scores * decay).astype(BF16),
@@ -782,54 +839,64 @@
                     else:
                         dxt[side] = dxt[side] + part
                 dscores_ref[block, top:lim, :lim] += gathered
-            inner = jnp.concatenate(dxt, axis=0).T
-            dls = dl_ref[block, span, :]
-            outer = dot(maps_ref[rows, :STATE], dls, NT) * to_end
-            gacc_ref[rows, :STATE] += dot(ended, dls)
-            gacc_ref[rows, STATE:] += dot(dye_ref[rows, lanes], st_ref[block, span, :])
-            dxs = inner + outer
+            inner_ref[...] = jnp.concatenate(dxt, axis=0).T
             skip = skip_ref[0:1, lanes]
-            vs = xs * outer
-            runs = dyf * (y_ref[rows, lanes] - skip * x) - low.astype(F32) * inner - vs
-            direct = x * dxs
-            lane = lax.broadcasted_iota(jnp.int32, (BLOCK_LEN, 128), 1)
-            for sums_ref, values in ((runs_ref, runs), (direct_ref, direct)):
-                left = jnp.sum(jnp.where(half, values, 0.0), axis=1, keepdims=True)
-                right = jnp.sum(jnp.where(half, 0.0, values), axis=1, keepdims=True)
-                at = step_at * GROUP + 2 * pair
-                sums_ref[rows, :] += jnp.where(
-                    lane == at, left, jnp.where(lane == at + 1, right, 0.0)
-                )
+            at = step_at * GROUP + 2 * pair
+            heads_of = jnp.where(lane_col == at + lane_row // HEAD_DIM, 1.0, 0.0).astype(BF16)
+            ends = jnp.zeros((8, width), F32)
+
+            def folded(values):
+                return jnp.sum(values.reshape(PART // 8, 8, width), axis=0)
+
+            for top in range(0, BLOCK_LEN, PART):
+                part = slice(lo + top, lo + top + PART)
+                here = slice(top, top + PART)
+                conv = conv_ref[here, :]
+                sig = sigmoid(conv)
+                x = conv * sig
+                step = per_pair(cols_ref, 0, pair, part)
+                inner = inner_ref[here, :]
+                outer = outer_ref[here, lanes] * per_pair(cols_ref, 3, pair, part)
+                dyf = dy_ref[part, lanes].astype(F32)
+                dxs = inner + outer
+                vs = x * step * outer
+                ends = ends + folded(vs)
+                runs = dyf * (y_ref[part, lanes] - skip * x) - low_ref[here, :].astype(F32) * inner - vs
+                for sums_ref, values in ((runs_ref, runs), (direct_ref, x * dxs)):
+                    high = values.astype(BF16)
+                    rest = (values - high.astype(F32)).astype(BF16)
+                    sums_ref[part, :] += dot(high, heads_of) + dot(rest, heads_of)
+                gw[pair][CONV + 1] = gw[pair][CONV + 1] + folded(dyf * x)
+                dconv = (dxs * step + skip * dyf) * (sig * (1.0 + conv * (1.0 - sig)))
+                gw[pair][CONV] = gw[pair][CONV] + folded(dconv)
+                dpad_ref[8 + lo + top : 8 + lo + top + PART, lanes] = dconv
+                for tap in range(CONV):
+                    first = EDGE - CONV + 1 + tap + lo + top
+                    gw[pair][tap] = gw[pair][tap] + folded(dconv * p_ref[first : first + PART, lanes])
             group_lanes = pl.ds(pl.multiple_of(step_at * GCOLS + pair * width, width), width)
-            ends_ref[block : block + 1, group_lanes] = jnp.sum(vs, axis=0, keepdims=True)
-            gw[CONV + 1] = gw[CONV + 1] + jnp.sum(dyf * x, axis=0, keepdims=True)
-            dconv = (dxs * step + skip * dyf) * (sig * (1.0 + conv * (1.0 - sig)))
-            gw[CONV] = gw[CONV] + jnp.sum(dconv, axis=0, keepdims=True)
-            dpad_ref[8 + lo : 8 + lo + BLOCK_LEN, lanes] = dconv
-            for tap in range(CONV):
-                at = EDGE - CONV + 1 + tap + lo
-                gw[tap] = gw[tap] + jnp.sum(
-                    dconv * p_ref[at : at + BLOCK_LEN, lanes], axis=0, keepdims=True
-                )
+            ends_ref[block : block + 1, group_lanes] = jnp.sum(ends, axis=0, keepdims=True)
+        gacc_ref[rows, :STATE] += dot(ended_ref[...], dl_ref[block])
+        gacc_ref[rows, STATE:] += dot(dye_ref[rows, :], st_ref[block])
+
+    for pair in range(PAIRS):
+        lanes = pl.ds(pair * width, width)
         group_lanes = pl.ds(pl.multiple_of(step_at * GCOLS + pair * width, width), width)
         for index in range(CONV + 1):
-            t_sent[0, index : index + 1, group_lanes] = gw[index]
-        ends_ref[blocks : blocks + 1, group_lanes] = gw[CONV + 1]
+            t_sent[0, index : index + 1, group_lanes] = jnp.sum(gw[pair][index], axis=0, keepdims=True)
+        ends_ref[blocks : blocks + 1, group_lanes] = jnp.sum(gw[pair][CONV + 1], axis=0, keepdims=True)
         edge = jnp.zeros((8, width), F32)
         for tap in range(CONV):
             edge = edge + dpad_ref[CONV - 1 - tap : CONV - 1 - tap + 8, lanes] * w_ref[tap : tap + 1, lanes]
         edge_ref[step_at, :, lanes] = edge
-        for block in range(blocks):
-            lo = block * BLOCK_LEN
-            back = jnp.zeros((BLOCK_LEN, width), F32)
+        for top in range(0, positions, PART):
+            back = jnp.zeros((PART, width), F32)
             for tap in range(CONV):
-                at = 8 + CONV - 1 - tap + lo
-                back = back + dpad_ref[at : at + BLOCK_LEN, lanes] * w_ref[tap : tap + 1, lanes]
-            x_ref[slot, lo : lo + BLOCK_LEN, pl.ds(pl.multiple_of(offset + pair * width, width), width)] = (
+                at = 8 + CONV - 1 - tap + top
+                back = back + dpad_ref[at : at + PART, lanes] * w_ref[tap : tap + 1, lanes]
+            x_ref[slot, top : top + PART, pl.ds(pl.multiple_of(offset + pair * width, width), width)] = (
                 back.astype(BF16)
             )
-            if block == blocks - 1:
-                tail_ref[step_at, :, lanes] = back[BLOCK_LEN - 8 :]
+        tail_ref[step_at, :, lanes] = back[PART - 8 :]
 
     @pl.when(step_at == GROUPS - 1)
     def _():
@@ -843,7 +910,7 @@
 
 
 def scan_backward(
-    decays, p, w, b, cols, rows, maps, skip, y, dy, dye, starts, ends, turned, cot, grad_gate,
+    decays, p, w, b, cols, rows, maps, skip, y, dy, dye, starts, ends, turned, turned_out, cot, grad_gate,
     inw_gate, inw_conv, bias, decay_log, tokens, gain, own_rows, collective_id,
 ):
     positions = y.shape[0]
@@ -854,7 +921,7 @@
     gates = INNER // PIECE
     pieces = OUT_PIECES + 2 * gates + 1
     count = exchange_count(zs, n)
-    steps = pieces + max(LAG * (stages_of(n) - 1), count - LAG)
+    steps = pieces + max(LAG * (stages_of(n) - 1), count - LAG, gates + positions // 256)
     width = CHANNELS + 128
     dma = pltpu.SemaphoreType.DMA
 
@@ -863,6 +930,10 @@
 
     def turn(s, most):
         return jnp.clip((s - OUT_PIECES) // 2, 0, most)
+
+    def gate_turn(s):
+        again = jnp.maximum(s - pieces + 1, 0)
+        return turn(s - 1, gates - 1) * (1 - jnp.minimum(again, 1)) + jnp.clip(again - 1, 0, gates - 1)
 
     once = pl.Buffered(1)
     own = pl.BlockSpec((positions, GCOLS), lambda s: (0, late(s)))
@@ -890,9 +961,10 @@
             states,
             whole(ends),
             whole(turned),
+            whole(turned_out),
             whole(cot),
-            pl.BlockSpec((positions, PIECE), lambda s: (0, turn(s - 1, gates - 1))),
-            pl.BlockSpec((features, PIECE), lambda s: (0, turn(s - 1, gates - 1))),
+            pl.BlockSpec((positions, PIECE), lambda s: (0, gate_turn(s))),
+            pl.BlockSpec((features, PIECE), lambda s: (0, jnp.clip(s - pieces, 0, gates - 1))),
             pl.BlockSpec((features, PIECE), lambda s: (0, turn(s, gates))),
             pl.BlockSpec((ext, PIECE), lambda s: (0, gates), pipeline_mode=once),
             pl.BlockSpec((8, PIECE), lambda s: (0, gates), pipeline_mode=once),
@@ -925,6 +997,11 @@
             pltpu.VMEM((positions, 128), F32),
             pltpu.VMEM((8, INNER), F32),
             pltpu.VMEM((GROUPS, blocks * GROUP, STATE), F32),
+            pltpu.VMEM((BLOCK_LEN, 2 * HEAD_DIM), F32),
+            pltpu.VMEM((BLOCK_LEN, 2 * HEAD_DIM), F32),
+            pltpu.VMEM((BLOCK_LEN, GCOLS), F32),
+            pltpu.VMEM((BLOCK_LEN, 2 * HEAD_DIM), BF16),
+            pltpu.VMEM((BLOCK_LEN, GCOLS), BF16),
         ]
         + chain_scratch()
         + [
@@ -947,7 +1024,7 @@
         ),
         name="scan_backward",
     )(
-        decays, p, w, b, cols, rows, maps, skip, y, dy, dye, starts, ends, turned, cot, grad_gate,
+        decays, p, w, b, cols, rows, maps, skip, y, dy, dye, starts, ends, turned, turned_out, cot, grad_gate,
         inw_gate, inw_conv, p, w, b, bias, decay_log, decays, tokens, gain,
     )
 
@@ -1359,12 +1436,14 @@
 
 RING = 4
 XRING = 6
+OUT_PIECES = 6
+OUT_SPLIT = 2
 
 
 class Streamed(Scatter):
-    def __init__(self, site, turned, kind, x, out, column, refs):
-        self.site, self.turned, self.x, self.out = site, turned, x, out
-        self.kind, self.column = kind, column
+    def __init__(self, site, turned, turned_out, is_later, x, out, column, refs):
+        self.site, self.x, self.out = site, x, out
+        self.turned, self.turned_out, self.is_later, self.column = turned, turned_out, is_later, column
         self.ring, self.x_ring = refs[0].shape[0], x.shape[0]
         self.away, self.own, self.came = refs[:3]
         self.take(refs[3:])
@@ -1375,7 +1454,7 @@
         full = (zs, n // 2, rows, PIECE)
         return [
             pltpu.VMEM((ring,) + full, BF16),
-            pltpu.VMEM(full, F32),
+            pltpu.VMEM(full, BF16),
             pltpu.VMEM((ring,) + full, BF16),
         ] + Scatter.common(ring, rows)
 
@@ -1391,14 +1470,23 @@
         rows = self.away.shape[3]
         together = 2 - s.zs % 2
         count = together * s.chips * rows
-
-        def one(i, carry):
-            lhs = self.turned[self.kind(piece), core, pl.ds(pl.multiple_of(i * count, 16), count), :]
-            value = dot(lhs, self.x[piece % self.x_ring]).reshape(together, s.chips, rows, PIECE)
-            store(pl.ds(i * together, together), value)
-            return carry
-
-        lax.fori_loop(0, s.zs // together, one, 0)
+        share = OUT_PIECES // OUT_SPLIT
+
+        for later in range(2):
+
+            @pl.when(self.is_later(piece) == later)
+            def _(later=later):
+                def one(i, carry):
+                    span = pl.ds(pl.multiple_of(i * count, 16), count)
+                    if later:
+                        lhs = self.turned[core, span, :]
+                    else:
+                        lhs = self.turned_out[jnp.minimum(piece, OUT_PIECES - 1) // share, core, span, :]
+                    value = dot(lhs, self.x[piece % self.x_ring]).reshape(together, s.chips, rows, PIECE)
+                    store(pl.ds(i * together, together), value)
+                    return carry
+
+                lax.fori_loop(0, s.zs // together, one, 0)
 
     def begin(self, piece):
         at = self.at(piece)
@@ -1410,12 +1498,12 @@
 
     def join(self, piece):
         def store(zi, value):
-            self.own[zi] = value
+            self.own[zi] = value.astype(BF16)
 
         self.product(self.site.bit(0), piece, store)
 
     def first(self, piece, zi, index, lanes):
-        return self.own[zi, index, :, lanes]
+        return self.own[zi, index, :, lanes].astype(F32)
 
 
 def exchange_count(zs, n):
@@ -1516,25 +1604,26 @@
         p, w, b, bias, decay_row, positions
     )
     skip = jnp.repeat(skip_gain, HEAD_DIM)[None]
-    y, starts, inw_gate = scan_forward(
-        decays, p, w, b, cols, run_rows, maps, skip, gate_line, positions, 2
+    by_rows = jnp.pad(normed.reshape(positions, devices, rows), ((0, 0), (0, 0), more_rows[0]))
+    y, starts, gate, turned_in, inw_gate = scan_forward(
+        decays, p, w, b, cols, run_rows, maps, skip, by_rows.reshape(positions, -1), gate_line, positions, 2
     )
     inw_gate = inw_gate[:, :, :rows].reshape(features, INNER)
-    gate = dot(normed, inw_gate)
     cot = cotangent[0]
     grad_normed_out = dot(cot, outw_full, NT)
-    normed_out, dy, dye, grad_gate, ends = gated(
-        y, gate, grad_normed_out, normg_full, run_exp, maps
+    normed_out, dy, dye, grad_gate, ends, *turned_out = gated(
+        y, gate, grad_normed_out, normg_full, run_exp, maps, rows if rows == padded_rows else None
     )
     mixed = (inputs + dot(normed_out, outw_full)).astype(BF16)[None]
 
-    def turned(x, split):
-        x = jnp.pad(x.T.reshape(-1, 2, split, rows, positions), ((0, 0),) * 3 + more_rows)
-        return x.transpose(2, 1, 0, 3, 4).reshape(split, 2, -1, positions)
-
-    turned_all = jnp.concatenate([turned(normed, 1), turned(normed_out, OUT_SPLIT)])
+    if turned_out:
+        turned_out = turned_out[0]
+    else:
+        turned_out = normed_out.T.reshape(-1, 2, OUT_SPLIT, rows, positions)
+        turned_out = jnp.pad(turned_out, ((0, 0),) * 3 + more_rows).transpose(2, 1, 0, 3, 4)
+    turned_out = turned_out.reshape(OUT_SPLIT, 2, -1, positions)
     own_main, grad_tokens, totals = scan_backward(
-        decays, p, w, b, cols, run_rows, maps, skip, y, dy, dye, starts, ends, turned_all, cot, grad_gate,
+        decays, p, w, b, cols, run_rows, maps, skip, y, dy, dye, starts, ends, turned_in, turned_out, cot, grad_gate,
         inw_gate, inw_conv, bias, decay_row, tokens[0], gain_full, padded_rows, 3,
     )
     own_main = own_main[:rows]

time: 438 us -> 422 us (0.963)
  matrix products: 43.3 us -> 32.3 us
  local copies, waits for them, and re-layouts: 34.5 us -> 26.8 us
  Pallas kernels: 335 us -> 340 us
    transpose x5 -> x0, local copies, waits for them, and re-layouts: 12.2 us -> none  [the longest x3 7.19 us: turned(): x.T.reshape(-1, 2, split, rows, positions)]
    pallas_call x1, Pallas kernels: 73.8 us -> 85 us  [scan_forward(): pl.pallas_call(functools.partial(scan_forward_kernel, pieces), grid=(step...]
    dot_general x4 -> x3, matrix products: 43.3 us -> 32.3 us  [dot(): return lax.dot_general(a, b, dims, preferred_element_type=F32)]
    pallas_call x1, Pallas kernels: 174 us -> 168 us  [scan_backward(): pl.pallas_call(scan_backward_kernel, grid=(steps,), in_specs=[pl.BlockSpe...]
  transfers between devices with their start and end apart: 1 -> 1, of which waited for: 0 -> 0; matrix products, arithmetic and copies ran while one was open for 8% -> 4% of each run, Pallas kernels for 18% -> 21%
where the time goes in v2:
time: 422 us
  Pallas kernels  340 us (81%)
  matrix products  32.3 us (8%)
  local copies, waits for them, and re-layouts  26.8 us (6%)
  between operations  14.4 us (3%)
  other arithmetic  7.95 us (2%)
    pallas_call x1, Pallas kernels, scan_backward(): pl.pallas_call(scan_backward_kernel, grid=(steps,), in_specs=[pl.BlockSpe...  168 us
    pallas_call x1, Pallas kernels, scan_forward(): pl.pallas_call(functools.partial(scan_forward_kernel, pieces), grid=(step...  85 us
    pallas_call x1, Pallas kernels, gathered(): pl.pallas_call(functools.partial(gather_kernel, pieces, start), grid=(ste...  64.7 us
    dot_general x3, matrix products, dot(): return lax.dot_general(a, b, dims, preferred_element_type=F32)  32.3 us
    pallas_call x1, Pallas kernels, gated(): pl.pallas_call(gate_kernel, grid=(positions // tile,), in_specs=[wide, wi...  16.8 us
  transfers between devices with their start and end apart: 1, of which 0 were waited for; matrix products, arithmetic and copies ran while one was open for 4% of the time, Pallas kernels for 21%

profile of v2, /device:TPU:0, one launch (start us, length us, event | category | flops | bytes accessed | tf_op | source)
XLA Modules:
  0.0 421.7 jit_solution(16675907374692847976)
XLA Ops:
  7.3 1.1 slice.55
  8.4 1.7 slice.56.late
  11.7 1.4 slice_bitcast_fusion.last
  14.0 64.7 %gather_rows.1 = (bf16[4,8,48,3584]{3,2,1,0:T(8,128)(2,1)}, bf16[4,48,3072]{2,1,0:T(8,128)(2,1)}, bf16[16,1536]{1,0:T(8,128)(2,1)}) custom-call(bf16[48,3584]{1,0:T(8,128)(2,1)} %concatenate.10.own, bf16[48,3072]{1,0:T(8,128)(2,1)} %slice.56.late, bf16[16,1536]{1,0:T(8,128)(2,1)} %slice_bitcast_fusion.last), custom_call_target="tpu_custom_call" | custom-call | bytes 11010048 | tf_op jit(solution)/shard_map/gather_rows/pallas_call | solution.py:1301
  78.7 1.2 slice.73
  82.5 1.3 slice.77.normed_ref
  84.5 11.2 %fusion.10.p_ref.plast_ref = f32[528,3584]{1,0:T(8,128)} fusion(bf16[528,1536]{1,0:T(8,128)(2,1)} %copy-done.15, bf16[1536,3584]{1,0:T(8,128)(2,1)} %bitcast.40), kind=kOutput, calls=%fused_computation.33 | convolution fusion | flops 5813305344 | bytes 20201472 | tf_op jit(solution)/shard_map/dot_general | solution.py:35
  95.8 5.6 %steps.1 = (f32[12,512,16]{2,1,0:T(8,128)S(1)}, f32[12,4,512]{2,1,0:T(4,128)S(1)}, bf16[512,256]{1,0:T(8,128)(2,1)S(1)}, f32[512,128]{1,0:T(8,128)S(1)}, f32[8,128]{1,0:T(8,128)S(1)}) custom-call(f32[528,3584]{1,0:T(8,128)} %fusion.10.p_ref.plast_ref, f32[8,3584]{1,0:T(8,128)S(1)} %pad_convert_fusion.w_ref.wlast_ref, ...), custom_call_target="tpu_custom_call" | custom-call | flops 67108864 | bytes 4194304 | tf_op jit(solution)/shard_map/steps/pallas_call | solution.py:115
  101.3 1.7 copy-done
  103.0 2.1 maximum_convert_fusion
  105.2 85.0 %scan_forward.1 = (f32[512,3072]{1,0:T(8,128)}, bf16[2,3072,128]{2,1,0:T(8,128)(2,1)S(1)}, f32[512,3072]{1,0:T(8,128)}, bf16[2,768,512]{2,1,0:T(8,128)(2,1)S(1)}, bf16[4,8,48,3072]{3,2,1,0:T(8,128)(2,1)}) custom-call(f32[8,128]{1,0:T(8,128)S(1)} %get-tuple-element.38.decays.grown_ref, f32[528,3584]{1,0:T(8,128)} %fusion.10.p_ref.plast_ref, ...), custom_call_target="tpu_custom_call" | custom-call | flops 4831838208 | bytes 37748736 | tf_op jit(solution)/shard_map/scan_forward/pallas_call | solution.py:330
  190.2 1.1 copy-done.2
  191.3 1.2 copy-done.3
  192.5 10.7 %convolution_bitcast_fusion.gno_ref = f32[512,3072]{1,0:T(8,128)} fusion(bf16[3072,1536]{1,0:T(8,128)(2,1)} %all-gather.2.cloned.1.call-done, bf16[1,512,1536]{2,1,0:T(8,128)(2,1)S(1)} %copy-done.18), kind=kOutput, calls=%fused_computation | convolution fusion | flops 4831838208 | bytes 17301504 | tf_op jit(solution)/shard_map/dot_general | solution.py:35
  203.2 16.8 %gate.1 = (bf16[512,3072]{1,0:T(8,128)(2,1)S(1)}, bf16[512,3072]{1,0:T(8,128)(2,1)}, bf16[512,3072]{1,0:T(8,128)(2,1)}, bf16[512,3072]{1,0:T(8,128)(2,1)}, f32[2...) custom-call(f32[512,3072]{1,0:T(8,128)} %get-tuple-element.43.y_ref, f32[512,3072]{1,0:T(8,128)} %get-tuple-element.44.gate_ref, ...), custom_call_target="tpu_custom_call" | custom-call | flops 805306368 | bytes 37748736 | tf_op jit(solution)/shard_map/gate/pallas_call | solution.py:452
  219.9 1.7 copy-done.11
  221.7 168.3 %scan_backward.1 = (f32[48,9728]{1,0:T(8,128)}, f32[512,1536]{1,0:T(8,128)}, f32[8,3456]{1,0:T(8,128)}) custom-call(f32[8,128]{1,0:T(8,128)} %copy-done.8, f32[528,3584]{1,0:T(8,128)} %fusion.10.p_ref.plast_ref, f32[8,3584]{1,0:T(8,128)} %copy-done.1, f32[1,3584]{1,0:T(1,128)} %copy-done.5, f32[12,512,16]{2,1,0:T(8,128)} %copy-done, ...), custom_call_target="tpu_custom_call" | custom-call | flops 9663676416 | bytes 47185920 | tf_op jit(solution)/shard_map/scan_backward/pallas_call | solution.py:946
  389.9 2.0 slice.71
  391.9 2.9 multiply_reduce_fusion.1
  396.7 1.3 slice_bitcast_fusion.1
  398.0 2.4 reshape.116
  400.3 1.2 copy.27
  402.8 10.4 %fusion.1 = bf16[1,512,1536]{2,1,0:T(8,128)(2,1)} fusion(bf16[512,3072]{1,0:T(8,128)(2,1)S(1)} %copy-done.12, bf16[3072,1536]{1,0:T(8,128)(2,1)} %all-gather.2.cloned.1.call-done, f32[528,1536]{1,0:T(8,128)} %maximum_convert_fusion), kind=kOutput, calls=%fused_computation.5 | convolution fusion | flops 4833411072 | bytes 17301504 | tf_op jit(solution)/shard_map/dot_general | solution.py:35
  413.2 1.7 copy.32
  (82 shorter events, 8.9 us)
Async XLA Ops:
  7.2 74.4 %copy-start.14 = (bf16[1,512,1536]{2,1,0:T(8,128)(2,1)S(1)}, bf16[1,512,1536]{2,1,0:T(8,128)(2,1)}, u32[]{:S(2)}) copy-start(bf16[1,512,1536]{2,1,0:T(8,128)(2,1)} %param.11) | copy-start | bytes 4718596
  7.2 74.3 %copy-start.23 = (f32[48]{0:T(128)S(1)}, f32[48]{0:T(128)}, u32[]{:S(2)}) copy-start(f32[48]{0:T(128)} %param.16) | copy-start | bytes 580
  7.2 74.3 %copy-start.24 = (f32[48]{0:T(128)S(1)}, f32[48]{0:T(128)}, u32[]{:S(2)}) copy-start(f32[48]{0:T(128)} %param.17) | copy-start | bytes 580
  7.2 185.3 %all-gather.2.cloned.1.call-start = ((), (), s32[]{:S(2)}) async-start(), calls=%async_computation | async-start | bytes 9732096 | tf_op jit(solution)/shard_map/all_gather | solution.py:1577
  81.5 14.3 %copy-start.9 = (f32[1,128]{1,0:T(1,128)}, f32[1,128]{1,0:T(1,128)S(1)}, u32[]{:S(2)}) copy-start(f32[1,128]{1,0:T(1,128)S(1)} %pad.28.bias_ref) | copy-start | bytes 1540
  81.5 14.2 %copy-start.10 = (f32[1,128]{1,0:T(1,128)}, f32[1,128]{1,0:T(1,128)S(1)}, u32[]{:S(2)}) copy-start(f32[1,128]{1,0:T(1,128)S(1)} %pad.29.decay_ref) | copy-start | bytes 1540
  82.0 2.1 copy-start.20
  82.5 1.7 copy-start.15
  84.3 20.8 %copy-start.7 = (f32[1,3072]{1,0:T(1,128)}, f32[1,3072]{1,0:T(1,128)S(1)}, u32[]{:S(2)}) copy-start(f32[1,3072]{1,0:T(1,128)S(1)} %broadcast_in_dim_reshape.3.skip_ref) | copy-start | bytes 36868
  84.5 20.6 %copy-start.5 = (f32[1,3584]{1,0:T(1,128)}, f32[1,3584]{1,0:T(1,128)S(1)}, u32[]{:S(2)}) copy-start(f32[1,3584]{1,0:T(1,128)S(1)} %pad_convert_fusion.1.b_ref.blast_ref) | copy-start | bytes 43012
  84.5 20.6 %copy-start.1 = (f32[8,3584]{1,0:T(8,128)}, f32[8,3584]{1,0:T(8,128)S(1)}, u32[]{:S(2)}) copy-start(f32[8,3584]{1,0:T(8,128)S(1)} %pad_convert_fusion.w_ref.wlast_ref) | copy-start | bytes 344068
  101.3 1.7 copy-start
  103.0 87.2 %copy-start.6 = (f32[12,4,512]{2,1,0:T(4,128)}, f32[12,4,512]{2,1,0:T(4,128)S(1)}, u32[]{:S(2)}) copy-start(f32[12,4,512]{2,1,0:T(4,128)S(1)} %get-tuple-element.40.rows_ref) | copy-start | bytes 294916
  103.0 87.2 %copy-start.8 = (f32[8,128]{1,0:T(8,128)}, f32[8,128]{1,0:T(8,128)S(1)}, u32[]{:S(2)}) copy-start(f32[8,128]{1,0:T(8,128)S(1)} %get-tuple-element.38.decays.grown_ref) | copy-start | bytes 12292
  103.0 100.2 %copy-start.4 = (bf16[512,256]{1,0:T(8,128)(2,1)}, bf16[512,256]{1,0:T(8,128)(2,1)S(1)}, u32[]{:S(2)}) copy-start(bf16[512,256]{1,0:T(8,128)(2,1)S(1)} %get-tuple-element.41.maps_ref) | copy-start | bytes 786436
  103.0 2.1 copy-start.13
  105.1 87.4 %copy-start.18 = (bf16[1,512,1536]{2,1,0:T(8,128)(2,1)S(1)}, bf16[1,512,1536]{2,1,0:T(8,128)(2,1)}, u32[]{:S(2)}) copy-start(bf16[1,512,1536]{2,1,0:T(8,128)(2,1)} %param.21) | copy-start | bytes 4718596
  219.9 1.7 copy-start.11
  389.9 11.6 %copy-start.19 = (bf16[96,1536]{1,0:T(8,128)(2,1)S(1)}, bf16[96,1536]{1,0:T(8,128)(2,1)}, u32[]{:S(2)}) copy-start(bf16[96,1536]{1,0:T(8,128)(2,1)} %param.20) | copy-start | bytes 884740
  391.9 9.8 %copy-start.21 = (bf16[96]{0:T(256)(128)(2,1)S(1)}, bf16[96]{0:T(256)(128)(2,1)}, u32[]{:S(2)}) copy-start(bf16[96]{0:T(256)(128)(2,1)} %param.19) | copy-start | bytes 580
  391.9 10.4 %copy-start.22 = (bf16[48]{0:T(256)(128)(2,1)S(1)}, bf16[48]{0:T(256)(128)(2,1)}, u32[]{:S(2)}) copy-start(bf16[48]{0:T(256)(128)(2,1)} %param.12) | copy-start | bytes 292
  391.9 10.9 %copy-start.12 = (bf16[512,3072]{1,0:T(8,128)(2,1)S(1)}, bf16[512,3072]{1,0:T(8,128)(2,1)}, u32[]{:S(2)}) copy-start(bf16[512,3072]{1,0:T(8,128)(2,1)} %copy-done.11) | copy-start | bytes 9437188
  401.5 11.6 %copy-start.17 = (f32[2,48,1536]{2,1,0:T(8,128)}, f32[2,48,1536]{2,1,0:T(8,128)S(1)}, u32[]{:S(2)}) copy-start(f32[2,48,1536]{2,1,0:T(8,128)S(1)} %copy.27) | copy-start | bytes 1769476
  402.8 10.4 %copy-start.16 = (f32[512,1536]{1,0:T(8,128)S(1)}, f32[512,1536]{1,0:T(8,128)}, u32[]{:S(2)}) copy-start(f32[512,1536]{1,0:T(8,128)} %get-tuple-element.56) | copy-start | bytes 9437188
  (2 other events, 2.3 us)
Sparse Core Ops, SparseCore 0:
  78.8 107.2 all-gather.1

commit v3 on v2

--- a/solution.py
+++ b/solution.py
@@ -22,6 +22,7 @@
 PAIRS = GROUP // 2
 STRIP = 128
 PART = 64
+MIXED_COLS = 128
 LOG2E = 1.4426950408889634
 F32 = jnp.float32
 BF16 = jnp.bfloat16
@@ -195,7 +196,7 @@
     @pl.when(jnp.logical_and(arrived >= 1, arrived <= pieces))
     def _():
         weight_copy(arrived - 1).wait()
-        gate_ref[...] = dot(normed_ref[...], weight_ref[...].reshape(-1, PIECE))
+        gate_ref[...] = dot(normed_ref[...], weight_ref[...].reshape(-1, PIECE)).astype(BF16)
 
     at_stages(gather.stages, pieces, LAG, step, gather.run)
 
@@ -355,7 +356,7 @@
         out_shape=[
             jax.ShapeDtypeStruct((positions, INNER), F32),
             jax.ShapeDtypeStruct((blocks, INNER, STATE), BF16),
-            jax.ShapeDtypeStruct((positions, columns), F32),
+            jax.ShapeDtypeStruct((positions, columns), BF16),
             jax.ShapeDtypeStruct((2, zs * n // 2 * rows_there, positions), BF16),
             jax.ShapeDtypeStruct((zs, n, rows_there, columns), BF16),
         ],
@@ -399,11 +400,11 @@
 
     for pair in range(HEADS // 2):
         lanes = slice(pair * width, (pair + 1) * width)
-        gate = gate_ref[:, lanes]
+        gate = gate_ref[:, lanes].astype(F32)
         gated = y_ref[:, lanes] * gate * sigmoid(gate)
         gated_ref[:, lanes] = gated
         square = square + gated * gated
-        cross = cross + gated * (gain_ref[:, lanes] * gno_ref[:, lanes])
+        cross = cross + gated * (gain_ref[:, lanes] * gno_ref[:, lanes].astype(F32))
     r1 = lax.rsqrt(jnp.sum(square, axis=-1, keepdims=True) * (1.0 / INNER) + 1e-05)
     back = r1 * r1 * r1 * (jnp.sum(cross, axis=-1, keepdims=True) * (1.0 / INNER))
 
@@ -413,12 +414,12 @@
 
     for pair in range(HEADS // 2):
         lanes = slice(pair * width, (pair + 1) * width)
-        gate = gate_ref[:, lanes]
+        gate = gate_ref[:, lanes].astype(F32)
         sig = sigmoid(gate)
         gated = gated_ref[:, lanes]
         gain = gain_ref[:, lanes]
         out_ref[:, lanes] = (gated * r1 * gain).astype(BF16)
-        ggated = gno_ref[:, lanes] * r1 * gain - gated * back
+        ggated = gno_ref[:, lanes].astype(F32) * r1 * gain - gated * back
         low = (ggated * (gate * sig)).astype(BF16)
         dy_ref[:, lanes] = low
         ggate_ref[:, lanes] = (
@@ -482,6 +483,31 @@
 
 
 def scan_backward_kernel(
+    branch, decays, p_ref, w_ref, b_ref, cols_ref, rows_ref, maps_ref, skip_ref, y_ref, dy_ref,
+    dye_ref, st_ref, grads_ref, turned_ref, turned_out_ref, cot_ref, ggate_ref, wgate_ref, wconv_ref,
+    plast_ref, wlast_ref, blast_ref, bias_ref, decay_ref, grown_ref, tokens_ref, gain_ref, *more_refs,
+):
+    if branch:
+        nout_ref, wout_ref, *more_refs = more_refs
+        mixed_ref = more_refs.pop(3)
+        first = GROUPS + LAG + 1
+        at = pl.program_id(0) - first
+
+        @pl.when(jnp.logical_and(at >= 0, at < tokens_ref.shape[1] // MIXED_COLS))
+        def _():
+            lanes = pl.ds(pl.multiple_of(at * MIXED_COLS, 128), MIXED_COLS)
+            mixed_ref[...] = (
+                tokens_ref[:, lanes].astype(F32) + dot(nout_ref[...], wout_ref[...])
+            ).astype(BF16)
+
+    scan_backward_steps(
+        decays, p_ref, w_ref, b_ref, cols_ref, rows_ref, maps_ref, skip_ref, y_ref, dy_ref,
+        dye_ref, st_ref, grads_ref, turned_ref, turned_out_ref, cot_ref, ggate_ref, wgate_ref, wconv_ref,
+        plast_ref, wlast_ref, blast_ref, bias_ref, decay_ref, grown_ref, tokens_ref, gain_ref, *more_refs,
+    )
+
+
+def scan_backward_steps(
     decays, p_ref, w_ref, b_ref, cols_ref, rows_ref, maps_ref, skip_ref, y_ref, dy_ref,
     dye_ref, st_ref, grads_ref, turned_ref, turned_out_ref, cot_ref, ggate_ref, wgate_ref, wconv_ref,
     plast_ref, wlast_ref, blast_ref, bias_ref, decay_ref, grown_ref, tokens_ref, gain_ref,
@@ -911,8 +937,9 @@
 
 def scan_backward(
     decays, p, w, b, cols, rows, maps, skip, y, dy, dye, starts, ends, turned, turned_out, cot, grad_gate,
-    inw_gate, inw_conv, bias, decay_log, tokens, gain, own_rows, collective_id,
+    inw_gate, inw_conv, bias, decay_log, tokens, gain, own_rows, collective_id, *factors,
 ):
+    branch = len(factors) == 2
     positions = y.shape[0]
     features = inw_gate.shape[0]
     blocks = positions // BLOCK_LEN
@@ -943,8 +970,19 @@
     def whole(x):
         return pl.BlockSpec(x.shape, lambda s: (0,) * len(x.shape), pipeline_mode=once)
 
+    more_in, more_out, more_shapes = [], [], []
+    if branch:
+        steps = max(steps, GROUPS + LAG + 1 + features // MIXED_COLS)
+
+        def mixing(s):
+            return 0, jnp.clip(s - (GROUPS + LAG + 1), 0, features // MIXED_COLS - 1)
+
+        more_in = [whole(factors[0]), pl.BlockSpec((INNER, MIXED_COLS), mixing)]
+        more_out = [pl.BlockSpec((positions, MIXED_COLS), mixing)]
+        more_shapes = [jax.ShapeDtypeStruct((positions, features), BF16)]
+
     return pl.pallas_call(
-        scan_backward_kernel,
+        functools.partial(scan_backward_kernel, branch),
         grid=(steps,),
         in_specs=[
             pl.BlockSpec(memory_space=pltpu.SMEM),
@@ -974,17 +1012,20 @@
             whole(decays),
             whole(tokens),
             whole(gain),
-        ],
+        ]
+        + more_in,
         out_specs=[
             pl.BlockSpec((own_rows, pieces * PIECE), lambda s: (0, 0), pipeline_mode=once),
             pl.BlockSpec((positions, features), lambda s: (0, 0), pipeline_mode=once),
             pl.BlockSpec((8, width), lambda s: (0, 0), pipeline_mode=once),
-        ],
+        ]
+        + more_out,
         out_shape=[
             jax.ShapeDtypeStruct((own_rows, pieces * PIECE), F32),
             jax.ShapeDtypeStruct((positions, features), F32),
             jax.ShapeDtypeStruct((8, width), F32),
-        ],
+        ]
+        + more_shapes,
         scratch_shapes=[
             pltpu.VMEM((blocks, BLOCK_LEN, BLOCK_LEN), F32),
             pltpu.VMEM((blocks, BLOCK_LEN, BLOCK_LEN), F32),
@@ -1025,7 +1066,7 @@
         name="scan_backward",
     )(
         decays, p, w, b, cols, rows, maps, skip, y, dy, dye, starts, ends, turned, turned_out, cot, grad_gate,
-        inw_gate, inw_conv, p, w, b, bias, decay_log, decays, tokens, gain,
+        inw_gate, inw_conv, p, w, b, bias, decay_log, decays, tokens, gain, *factors,
     )
 
 
@@ -1610,11 +1651,10 @@
     )
     inw_gate = inw_gate[:, :, :rows].reshape(features, INNER)
     cot = cotangent[0]
-    grad_normed_out = dot(cot, outw_full, NT)
+    grad_normed_out = dot(cot, outw_full, NT).astype(BF16)
     normed_out, dy, dye, grad_gate, ends, *turned_out = gated(
         y, gate, grad_normed_out, normg_full, run_exp, maps, rows if rows == padded_rows else None
     )
-    mixed = (inputs + dot(normed_out, outw_full)).astype(BF16)[None]
 
     if turned_out:
         turned_out = turned_out[0]
@@ -1622,14 +1662,20 @@
         turned_out = normed_out.T.reshape(-1, 2, OUT_SPLIT, rows, positions)
         turned_out = jnp.pad(turned_out, ((0, 0),) * 3 + more_rows).transpose(2, 1, 0, 3, 4)
     turned_out = turned_out.reshape(OUT_SPLIT, 2, -1, positions)
-    own_main, grad_tokens, totals = scan_backward(
+    in_kernel = rows == padded_rows
+    own_main, grad_tokens, totals, *mixed = scan_backward(
         decays, p, w, b, cols, run_rows, maps, skip, y, dy, dye, starts, ends, turned_in, turned_out, cot, grad_gate,
         inw_gate, inw_conv, bias, decay_row, tokens[0], gain_full, padded_rows, 3,
+        *((normed_out, outw_full) if in_kernel else ()),
     )
+    if in_kernel:
+        mixed = mixed[0]
+    else:
+        mixed = (inputs + dot(normed_out, outw_full)).astype(BF16)
     own_main = own_main[:rows]
     out_cols = OUT_PIECES * PIECE
-    own_out = own_main[:, :out_cols].reshape(rows, OUT_SPLIT, features).transpose(1, 0, 2)
-    own_out = own_out.reshape(OUT_SPLIT * rows, features)
+    share = out_cols // OUT_SPLIT
+    own_out = jnp.concatenate([own_main[:, i * share : (i + 1) * share] for i in range(OUT_SPLIT)])
     own_in = own_main[:, out_cols : out_cols + PROJ]
     per_tap = conv_weight.shape[1]
     me = lax.axis_index("seq") * lax.axis_size("fsdp") + lax.axis_index("fsdp")
@@ -1637,7 +1683,7 @@
     heads = totals[:3, CHANNELS : CHANNELS + HEADS]
 
     return (
-        mixed,
+        mixed[None],
         grad_tokens[None],
         jnp.sum(own_in * in_weight.astype(F32), axis=1) / pre_gain.astype(F32),
         own_in,

time: 422 us -> 413 us (0.979)
  matrix products: 32.3 us -> 20.9 us
  Pallas kernels: 340 us -> 348 us
    dot_general x3 -> x2, matrix products: 32.3 us -> 20.9 us  [dot(): return lax.dot_general(a, b, dims, preferred_element_type=F32)]
    pallas_call x1, Pallas kernels: 168 us -> 174 us  [scan_backward(): pl.pallas_call(functools.partial(scan_backward_kernel, branch), grid=(ste...]
    unnamed x51 -> x50, local copies, waits for them, and re-layouts: 7.8 us -> 8.53 us
  transfers between devices with their start and end apart: 1 -> 1, of which waited for: 0 -> 0; matrix products, arithmetic and copies ran while one was open for 4% -> 4% of each run, Pallas kernels for 21% -> 22%
where the time goes in v3:
time: 413 us
  Pallas kernels  348 us (84%)
  local copies, waits for them, and re-layouts  23 us (6%)
  matrix products  20.9 us (5%)
  between operations  14.4 us (3%)
  other arithmetic  6.45 us (2%)
    pallas_call x1, Pallas kernels, scan_backward(): pl.pallas_call(functools.partial(scan_backward_kernel, branch), grid=(ste...  174 us
    pallas_call x1, Pallas kernels, scan_forward(): pl.pallas_call(functools.partial(scan_forward_kernel, pieces), grid=(step...  87 us
    pallas_call x1, Pallas kernels, gathered(): pl.pallas_call(functools.partial(gather_kernel, pieces, start), grid=(ste...  64.7 us
    dot_general x2, matrix products, dot(): return lax.dot_general(a, b, dims, preferred_element_type=F32)  20.9 us
    pallas_call x1, Pallas kernels, gated(): pl.pallas_call(gate_kernel, grid=(positions // tile,), in_specs=[wide, wi...  16 us
    unnamed x50, local copies, waits for them, and re-layouts  8.53 us
  transfers between devices with their start and end apart: 1, of which 0 were waited for; matrix products, arithmetic and copies ran while one was open for 4% of the time, Pallas kernels for 22%

profile of v3, /device:TPU:0, one launch (start us, length us, event | category | flops | bytes accessed | tf_op | source)
XLA Modules:
  0.0 412.5 jit_solution(6669760347686915402)
XLA Ops:
  7.3 1.8 slice.56.late
  9.1 1.0 slice.55
  11.7 1.4 slice_bitcast_fusion.last
  13.2 0.8 concatenate.13.own
  14.0 64.7 %gather_rows.1 = (bf16[4,8,48,3584]{3,2,1,0:T(8,128)(2,1)}, bf16[4,48,3072]{2,1,0:T(8,128)(2,1)}, bf16[16,1536]{1,0:T(8,128)(2,1)}) custom-call(bf16[48,3584]{1,0:T(8,128)(2,1)} %concatenate.13.own, bf16[48,3072]{1,0:T(8,128)(2,1)} %slice.56.late, bf16[16,1536]{1,0:T(8,128)(2,1)} %slice_bitcast_fusion.last), custom_call_target="tpu_custom_call" | custom-call | bytes 11010048 | tf_op jit(solution)/shard_map/gather_rows/pallas_call | solution.py:1342
  78.7 1.2 slice.72
  82.8 1.2 slice.76.normed_ref
  84.1 10.8 %fusion.13.p_ref.plast_ref = f32[528,3584]{1,0:T(8,128)} fusion(bf16[528,1536]{1,0:T(8,128)(2,1)S(1)} %fusion.3, bf16[1536,3584]{1,0:T(8,128)(2,1)} %bitcast.33), kind=kOutput, calls=%fused_computation.36 | convolution fusion | flops 5813305344 | bytes 20201472 | tf_op jit(solution)/shard_map/dot_general | solution.py:36
  94.8 5.7 %steps.1 = (f32[12,512,16]{2,1,0:T(8,128)S(1)}, f32[12,4,512]{2,1,0:T(4,128)S(1)}, bf16[512,256]{1,0:T(8,128)(2,1)S(1)}, f32[512,128]{1,0:T(8,128)S(1)}, f32[8,128]{1,0:T(8,128)S(1)}) custom-call(f32[528,3584]{1,0:T(8,128)} %fusion.13.p_ref.plast_ref, f32[8,3584]{1,0:T(8,128)S(1)} %pad_convert_fusion.w_ref.wlast_ref, ...), custom_call_target="tpu_custom_call" | custom-call | flops 67108864 | bytes 4194304 | tf_op jit(solution)/shard_map/steps/pallas_call | solution.py:116
  100.5 1.7 copy-done
  102.2 87.0 %scan_forward.1 = (f32[512,3072]{1,0:T(8,128)}, bf16[2,3072,128]{2,1,0:T(8,128)(2,1)S(1)}, bf16[512,3072]{1,0:T(8,128)(2,1)}, bf16[2,768,512]{2,1,0:T(8,128)(2,1)S(1)}, bf16[4,8,48,3072]{3,2,1,0:T(8,128)(2,1)}) custom-call(f32[8,128]{1,0:T(8,128)S(1)} %get-tuple-element.39.decays.grown_ref, f32[528,3584]{1,0:T(8,128)} %fusion.13.p_ref.plast_ref, ...), custom_call_target="tpu_custom_call" | custom-call | flops 4831838208 | bytes 37748736 | tf_op jit(solution)/shard_map/scan_forward/pallas_call | solution.py:331
  189.2 1.1 copy-done.3
  190.4 1.2 copy-done.4
  191.6 10.1 %fusion.gno_ref = bf16[512,3072]{1,0:T(8,128)(2,1)} fusion(bf16[3072,1536]{1,0:T(8,128)(2,1)} %all-gather.2.cloned.1.call-done.more_refs_1_, bf16[1,512,1536]{2,1,0:T(8,128)(2,1)S(1)} %copy-done.17), kind=kOutput, calls=%fused_computation.1 | convolution fusion | flops 4833411072 | bytes 14155776 | tf_op jit(solution)/shard_map/dot_general | solution.py:36
  201.7 16.0 %gate.1 = (bf16[512,3072]{1,0:T(8,128)(2,1)S(1)}, bf16[512,3072]{1,0:T(8,128)(2,1)}, bf16[512,3072]{1,0:T(8,128)(2,1)}, bf16[512,3072]{1,0:T(8,128)(2,1)}, f32[2...) custom-call(f32[512,3072]{1,0:T(8,128)} %get-tuple-element.44.y_ref, ...), custom_call_target="tpu_custom_call" | custom-call | flops 805306368 | bytes 37748736 | tf_op jit(solution)/shard_map/gate/pallas_call | solution.py:453
  217.7 1.6 copy-done.1
  219.3 174.4 %scan_backward.1 = (f32[48,9728]{1,0:T(8,128)}, f32[512,1536]{1,0:T(8,128)}, f32[8,3456]{1,0:T(8,128)}, bf16[512,1536]{1,0:T(8,128)(2,1)}) custom-call(f32[8,128]{1,0:T(8,128)} %copy-done.9, f32[528,3584]{1,0:T(8,128)} %fusion.13.p_ref.plast_ref, f32[8,3584]{1,0:T(8,128)} %copy-done.2, f32[1,3584]{1,0:T(1,128)} %copy-done.6, f32[12,512,16]{2,1,0:T(8,128)} %copy-done, ...), custom_call_target="tpu_custom_call" | custom-call | flops 9663676416 | bytes 47185920 | tf_op jit(solution)/shard_map/scan_backward/pallas_call | solution.py:984
  393.8 1.3 slice_bitcast_fusion.1
  395.2 0.8 constant_dynamic-slice_fusion
  397.0 1.1 fusion.12
  398.1 2.7 multiply_reduce_fusion
  401.4 1.0 multiply_reduce_fusion.1
  402.9 1.1 copy.31
  404.0 1.7 copy.32
  (77 shorter events, 6.8 us)
Async XLA Ops:
  7.2 74.7 %copy-start.13 = (bf16[1,512,1536]{2,1,0:T(8,128)(2,1)S(1)}, bf16[1,512,1536]{2,1,0:T(8,128)(2,1)}, u32[]{:S(2)}) copy-start(bf16[1,512,1536]{2,1,0:T(8,128)(2,1)} %param.11) | copy-start | bytes 4718596
  7.2 73.9 %copy-start.22 = (f32[48]{0:T(128)S(1)}, f32[48]{0:T(128)}, u32[]{:S(2)}) copy-start(f32[48]{0:T(128)} %param.16) | copy-start | bytes 580
  7.2 74.0 %copy-start.23 = (f32[48]{0:T(128)S(1)}, f32[48]{0:T(128)}, u32[]{:S(2)}) copy-start(f32[48]{0:T(128)} %param.17) | copy-start | bytes 580
  7.2 74.0 %copy-start.19 = (f32[48]{0:T(128)S(1)}, f32[48]{0:T(128)}, u32[]{:S(2)}) copy-start(f32[48]{0:T(128)} %param.18) | copy-start | bytes 580
  7.2 184.3 %all-gather.2.cloned.1.call-start = ((), (), s32[]{:S(2)}) async-start(), calls=%async_computation | async-start | bytes 9732096 | tf_op jit(solution)/shard_map/all_gather | solution.py:1618
  81.1 13.7 %copy-start.10 = (f32[1,128]{1,0:T(1,128)}, f32[1,128]{1,0:T(1,128)S(1)}, u32[]{:S(2)}) copy-start(f32[1,128]{1,0:T(1,128)S(1)} %pad.28.bias_ref) | copy-start | bytes 1540
  81.2 13.6 %copy-start.11 = (f32[1,128]{1,0:T(1,128)}, f32[1,128]{1,0:T(1,128)S(1)}, u32[]{:S(2)}) copy-start(f32[1,128]{1,0:T(1,128)S(1)} %pad.29.decay_ref) | copy-start | bytes 1540
  81.4 20.8 %copy-start.8 = (f32[1,3072]{1,0:T(1,128)}, f32[1,3072]{1,0:T(1,128)S(1)}, u32[]{:S(2)}) copy-start(f32[1,3072]{1,0:T(1,128)S(1)} %broadcast_in_dim_reshape.3.skip_ref) | copy-start | bytes 36868
  84.0 18.2 %copy-start.6 = (f32[1,3584]{1,0:T(1,128)}, f32[1,3584]{1,0:T(1,128)S(1)}, u32[]{:S(2)}) copy-start(f32[1,3584]{1,0:T(1,128)S(1)} %pad_convert_fusion.1.b_ref.blast_ref) | copy-start | bytes 43012
  84.1 18.1 %copy-start.2 = (f32[8,3584]{1,0:T(8,128)}, f32[8,3584]{1,0:T(8,128)S(1)}, u32[]{:S(2)}) copy-start(f32[8,3584]{1,0:T(8,128)S(1)} %pad_convert_fusion.w_ref.wlast_ref) | copy-start | bytes 344068
  94.8 7.4 %copy-start.12 = (bf16[4,48,3072]{2,1,0:T(8,128)(2,1)S(1)}, bf16[4,48,3072]{2,1,0:T(8,128)(2,1)}, u32[]{:S(2)}) copy-start(bf16[4,48,3072]{2,1,0:T(8,128)(2,1)} %get-tuple-element.43.own) | copy-start | bytes 3538948
  100.5 1.7 copy-start
  102.2 87.0 %copy-start.7 = (f32[12,4,512]{2,1,0:T(4,128)}, f32[12,4,512]{2,1,0:T(4,128)S(1)}, u32[]{:S(2)}) copy-start(f32[12,4,512]{2,1,0:T(4,128)S(1)} %get-tuple-element.41.rows_ref) | copy-start | bytes 294916
  102.2 87.0 %copy-start.9 = (f32[8,128]{1,0:T(8,128)}, f32[8,128]{1,0:T(8,128)S(1)}, u32[]{:S(2)}) copy-start(f32[8,128]{1,0:T(8,128)S(1)} %get-tuple-element.39.decays.grown_ref) | copy-start | bytes 12292
  102.2 99.5 %copy-start.5 = (bf16[512,256]{1,0:T(8,128)(2,1)}, bf16[512,256]{1,0:T(8,128)(2,1)S(1)}, u32[]{:S(2)}) copy-start(bf16[512,256]{1,0:T(8,128)(2,1)S(1)} %get-tuple-element.42.maps_ref) | copy-start | bytes 786436
  102.2 89.3 %copy-start.17 = (bf16[1,512,1536]{2,1,0:T(8,128)(2,1)S(1)}, bf16[1,512,1536]{2,1,0:T(8,128)(2,1)}, u32[]{:S(2)}) copy-start(bf16[1,512,1536]{2,1,0:T(8,128)(2,1)} %param.21) | copy-start | bytes 4718596
  190.4 1.2 copy-start.4
  217.7 1.6 copy-start.1
  219.3 178.8 %copy-start.15 = (bf16[48,6448]{1,0:T(8,128)(2,1)S(1)}, bf16[48,6448]{1,0:T(8,128)(2,1)}, u32[]{:S(2)}) copy-start(bf16[48,6448]{1,0:T(8,128)(2,1)} %param.13) | copy-start | bytes 1857028
  393.8 7.1 %copy-start.20 = (bf16[48]{0:T(256)(128)(2,1)S(1)}, bf16[48]{0:T(256)(128)(2,1)}, u32[]{:S(2)}) copy-start(bf16[48]{0:T(256)(128)(2,1)} %param.12) | copy-start | bytes 292
  393.8 7.6 %copy-start.18 = (bf16[96,1536]{1,0:T(8,128)(2,1)S(1)}, bf16[96,1536]{1,0:T(8,128)(2,1)}, u32[]{:S(2)}) copy-start(bf16[96,1536]{1,0:T(8,128)(2,1)} %param.20) | copy-start | bytes 884740
  393.8 8.5 %copy-start.21 = (bf16[96]{0:T(256)(128)(2,1)S(1)}, bf16[96]{0:T(256)(128)(2,1)}, u32[]{:S(2)}) copy-start(bf16[96]{0:T(256)(128)(2,1)} %param.19) | copy-start | bytes 580
  393.8 9.1 %copy-start.16 = (bf16[512,1536]{1,0:T(8,128)(2,1)S(1)}, bf16[512,1536]{1,0:T(8,128)(2,1)}, u32[]{:S(2)}) copy-start(bf16[512,1536]{1,0:T(8,128)(2,1)} %get-tuple-element.57) | copy-start | bytes 4718596
  398.1 5.9 %copy-start.14 = (f32[512,1536]{1,0:T(8,128)S(1)}, f32[512,1536]{1,0:T(8,128)}, u32[]{:S(2)}) copy-start(f32[512,1536]{1,0:T(8,128)} %get-tuple-element.58) | copy-start | bytes 9437188
  (1 other events, 1.1 us)
Sparse Core Ops, SparseCore 0:
  78.8 108.4 all-gather.1

commit v4 on v3

--- a/solution.py
+++ b/solution.py
@@ -22,7 +22,8 @@
 PAIRS = GROUP // 2
 STRIP = 128
 PART = 64
-MIXED_COLS = 128
+MIXED_COLS = 256
+EARLY = 3
 LOG2E = 1.4426950408889634
 F32 = jnp.float32
 BF16 = jnp.bfloat16
@@ -196,7 +197,7 @@
     @pl.when(jnp.logical_and(arrived >= 1, arrived <= pieces))
     def _():
         weight_copy(arrived - 1).wait()
-        gate_ref[...] = dot(normed_ref[...], weight_ref[...].reshape(-1, PIECE)).astype(BF16)
+        gate_ref[...] = dot(normed_ref[...], weight_ref[...].reshape(-1, PIECE))
 
     at_stages(gather.stages, pieces, LAG, step, gather.run)
 
@@ -356,7 +357,7 @@
         out_shape=[
             jax.ShapeDtypeStruct((positions, INNER), F32),
             jax.ShapeDtypeStruct((blocks, INNER, STATE), BF16),
-            jax.ShapeDtypeStruct((positions, columns), BF16),
+            jax.ShapeDtypeStruct((positions, columns), F32),
             jax.ShapeDtypeStruct((2, zs * n // 2 * rows_there, positions), BF16),
             jax.ShapeDtypeStruct((zs, n, rows_there, columns), BF16),
         ],
@@ -400,11 +401,11 @@
 
     for pair in range(HEADS // 2):
         lanes = slice(pair * width, (pair + 1) * width)
-        gate = gate_ref[:, lanes].astype(F32)
+        gate = gate_ref[:, lanes]
         gated = y_ref[:, lanes] * gate * sigmoid(gate)
         gated_ref[:, lanes] = gated
         square = square + gated * gated
-        cross = cross + gated * (gain_ref[:, lanes] * gno_ref[:, lanes].astype(F32))
+        cross = cross + gated * (gain_ref[:, lanes] * gno_ref[:, lanes])
     r1 = lax.rsqrt(jnp.sum(square, axis=-1, keepdims=True) * (1.0 / INNER) + 1e-05)
     back = r1 * r1 * r1 * (jnp.sum(cross, axis=-1, keepdims=True) * (1.0 / INNER))
 
@@ -414,12 +415,12 @@
 
     for pair in range(HEADS // 2):
         lanes = slice(pair * width, (pair + 1) * width)
-        gate = gate_ref[:, lanes].astype(F32)
+        gate = gate_ref[:, lanes]
         sig = sigmoid(gate)
         gated = gated_ref[:, lanes]
         gain = gain_ref[:, lanes]
         out_ref[:, lanes] = (gated * r1 * gain).astype(BF16)
-        ggated = gno_ref[:, lanes].astype(F32) * r1 * gain - gated * back
+        ggated = gno_ref[:, lanes] * r1 * gain - gated * back
         low = (ggated * (gate * sig)).astype(BF16)
         dy_ref[:, lanes] = low
         ggate_ref[:, lanes] = (
@@ -482,6 +483,16 @@
     )(y, gate, gno, gain, er, maps)
 
 
+def spread_turn(step, first):
+    return jnp.clip(step - first, 0, 2) + jnp.maximum(step - (GROUPS + LAG + 1), 0)
+
+
+def spread_now(step, first, turns):
+    early = jnp.logical_and(step >= first, step < first + 2)
+    after = step - (GROUPS + LAG + 1)
+    return jnp.logical_or(early, jnp.logical_and(after >= 0, after < turns - 2))
+
+
 def scan_backward_kernel(
     branch, decays, p_ref, w_ref, b_ref, cols_ref, rows_ref, maps_ref, skip_ref, y_ref, dy_ref,
     dye_ref, st_ref, grads_ref, turned_ref, turned_out_ref, cot_ref, ggate_ref, wgate_ref, wconv_ref,
@@ -490,10 +501,10 @@
     if branch:
         nout_ref, wout_ref, *more_refs = more_refs
         mixed_ref = more_refs.pop(3)
-        first = GROUPS + LAG + 1
-        at = pl.program_id(0) - first
-
-        @pl.when(jnp.logical_and(at >= 0, at < tokens_ref.shape[1] // MIXED_COLS))
+        step = pl.program_id(0)
+        at = spread_turn(step, 1)
+
+        @pl.when(spread_now(step, 1, tokens_ref.shape[1] // MIXED_COLS))
         def _():
             lanes = pl.ds(pl.multiple_of(at * MIXED_COLS, 128), MIXED_COLS)
             mixed_ref[...] = (
@@ -630,16 +641,18 @@
 
     after = step_at - last - 1
 
-    @pl.when(jnp.logical_and(after >= 0, after < gates))
+    @pl.when(jnp.logical_or(step_at < EARLY, jnp.logical_and(after >= 0, after < gates - EARLY)))
     def _():
         add_normed(wgate_ref, lambda: ggate_ref[...])
 
     tile = 128
 
-    @pl.when(jnp.logical_and(after >= gates, after < gates + positions // (2 * tile)))
+    backward = after - (gates - EARLY)
+
+    @pl.when(jnp.logical_and(backward >= 0, backward < positions // (2 * tile)))
     def _():
         def one(i, carry):
-            rows = pl.ds(pl.multiple_of((after - gates) * 2 * tile + i * tile, tile), tile)
+            rows = pl.ds(pl.multiple_of(backward * 2 * tile + i * tile, tile), tile)
             features = gtokens_ref.shape[1]
             inputs = tokens_ref[rows, :].astype(F32)
             r0 = lax.rsqrt(jnp.sum(inputs * inputs, axis=-1, keepdims=True) * (1.0 / features) + 1e-05)
@@ -948,7 +961,7 @@
     gates = INNER // PIECE
     pieces = OUT_PIECES + 2 * gates + 1
     count = exchange_count(zs, n)
-    steps = pieces + max(LAG * (stages_of(n) - 1), count - LAG, gates + positions // 256)
+    steps = pieces + max(LAG * (stages_of(n) - 1), count - LAG, gates - EARLY + positions // 256)
     width = CHANNELS + 128
     dma = pltpu.SemaphoreType.DMA
 
@@ -958,9 +971,12 @@
     def turn(s, most):
         return jnp.clip((s - OUT_PIECES) // 2, 0, most)
 
+    def weight_turn(s):
+        return jnp.minimum(s, EARLY - 1) + jnp.clip(s - pieces + 1, 0, gates - EARLY)
+
     def gate_turn(s):
-        again = jnp.maximum(s - pieces + 1, 0)
-        return turn(s - 1, gates - 1) * (1 - jnp.minimum(again, 1)) + jnp.clip(again - 1, 0, gates - 1)
+        within = jnp.minimum(jnp.maximum(s - EARLY + 1, 0), 1) * (1 - jnp.minimum(jnp.maximum(s - pieces + 1, 0), 1))
+        return within * turn(s - 1, gates - 1) + (1 - within) * weight_turn(s)
 
     once = pl.Buffered(1)
     own = pl.BlockSpec((positions, GCOLS), lambda s: (0, late(s)))
@@ -972,10 +988,10 @@
 
     more_in, more_out, more_shapes = [], [], []
     if branch:
-        steps = max(steps, GROUPS + LAG + 1 + features // MIXED_COLS)
+        steps = max(steps, GROUPS + LAG + features // MIXED_COLS)
 
         def mixing(s):
-            return 0, jnp.clip(s - (GROUPS + LAG + 1), 0, features // MIXED_COLS - 1)
+            return 0, jnp.minimum(spread_turn(s, 1), features // MIXED_COLS - 1)
 
         more_in = [whole(factors[0]), pl.BlockSpec((INNER, MIXED_COLS), mixing)]
         more_out = [pl.BlockSpec((positions, MIXED_COLS), mixing)]
@@ -1002,7 +1018,7 @@
             whole(turned_out),
             whole(cot),
             pl.BlockSpec((positions, PIECE), lambda s: (0, gate_turn(s))),
-            pl.BlockSpec((features, PIECE), lambda s: (0, jnp.clip(s - pieces, 0, gates - 1))),
+            pl.BlockSpec((features, PIECE), lambda s: (0, weight_turn(s))),
             pl.BlockSpec((features, PIECE), lambda s: (0, turn(s, gates))),
             pl.BlockSpec((ext, PIECE), lambda s: (0, gates), pipeline_mode=once),
             pl.BlockSpec((8, PIECE), lambda s: (0, gates), pipeline_mode=once),
@@ -1509,37 +1525,29 @@
     def product(self, core, piece, store):
         s = self.site
         rows = self.away.shape[3]
-        together = 2 - s.zs % 2
-        count = together * s.chips * rows
         share = OUT_PIECES // OUT_SPLIT
-
         for later in range(2):
 
             @pl.when(self.is_later(piece) == later)
             def _(later=later):
-                def one(i, carry):
-                    span = pl.ds(pl.multiple_of(i * count, 16), count)
-                    if later:
-                        lhs = self.turned[core, span, :]
-                    else:
-                        lhs = self.turned_out[jnp.minimum(piece, OUT_PIECES - 1) // share, core, span, :]
-                    value = dot(lhs, self.x[piece % self.x_ring]).reshape(together, s.chips, rows, PIECE)
-                    store(pl.ds(i * together, together), value)
-                    return carry
-
-                lax.fori_loop(0, s.zs // together, one, 0)
+                if later:
+                    lhs = self.turned[core]
+                else:
+                    lhs = self.turned_out[jnp.minimum(piece, OUT_PIECES - 1) // share, core]
+                value = dot(lhs, self.x[piece % self.x_ring])
+                store(value.astype(BF16).reshape(s.zs, s.chips, rows, PIECE))
 
     def begin(self, piece):
         at = self.at(piece)
 
-        def store(zi, value):
-            self.away[at, zi] = value.astype(BF16)
+        def store(value):
+            self.away[at] = value
 
         self.product(1 - self.site.bit(0), piece, store)
 
     def join(self, piece):
-        def store(zi, value):
-            self.own[zi] = value.astype(BF16)
+        def store(value):
+            self.own[...] = value
 
         self.product(self.site.bit(0), piece, store)
 
@@ -1651,7 +1659,7 @@
     )
     inw_gate = inw_gate[:, :, :rows].reshape(features, INNER)
     cot = cotangent[0]
-    grad_normed_out = dot(cot, outw_full, NT).astype(BF16)
+    grad_normed_out = dot(cot, outw_full, NT)
     normed_out, dy, dye, grad_gate, ends, *turned_out = gated(
         y, gate, grad_normed_out, normg_full, run_exp, maps, rows if rows == padded_rows else None
     )

time: 413 us -> 414 us (level)
  no operation moved by 1% of the time
where the time goes in v4:
time: 414 us; the launch traced here: 413 us
  Pallas kernels  348 us (84%)
  local copies, waits for them, and re-layouts  23.1 us (6%)
  matrix products  21.3 us (5%)
  between operations  14.4 us (3%)
  other arithmetic  6.45 us (2%)
    pallas_call x1, Pallas kernels, scan_backward(): pl.pallas_call(functools.partial(scan_backward_kernel, branch), grid=(ste...  174 us
    pallas_call x1, Pallas kernels, scan_forward(): pl.pallas_call(functools.partial(scan_forward_kernel, pieces), grid=(step...  87.2 us
    pallas_call x1, Pallas kernels, gathered(): pl.pallas_call(functools.partial(gather_kernel, pieces, start), grid=(ste...  64.7 us
    dot_general x2, matrix products, dot(): return lax.dot_general(a, b, dims, preferred_element_type=F32)  21.3 us
    pallas_call x1, Pallas kernels, gated(): pl.pallas_call(gate_kernel, grid=(positions // tile,), in_specs=[wide, wi...  16.7 us
    unnamed x50, local copies, waits for them, and re-layouts  8.62 us
  transfers between devices with their start and end apart: 1, of which 0 were waited for; matrix products, arithmetic and copies ran while one was open for 4% of the time, Pallas kernels for 22%

profile of v4, /device:TPU:0, one launch (start us, length us, event | category | flops | bytes accessed | tf_op | source)
XLA Modules:
  0.0 413.3 jit_solution(7677843575194041036)
XLA Ops:
  7.3 1.8 slice.56.late
  9.1 1.0 slice.55
  11.7 1.4 slice_bitcast_fusion.last
  13.2 0.8 concatenate.13.own
  14.0 64.7 %gather_rows.1 = (bf16[4,8,48,3584]{3,2,1,0:T(8,128)(2,1)}, bf16[4,48,3072]{2,1,0:T(8,128)(2,1)}, bf16[16,1536]{1,0:T(8,128)(2,1)}) custom-call(bf16[48,3584]{1,0:T(8,128)(2,1)} %concatenate.13.own, bf16[48,3072]{1,0:T(8,128)(2,1)} %slice.56.late, bf16[16,1536]{1,0:T(8,128)(2,1)} %slice_bitcast_fusion.last), custom_call_target="tpu_custom_call" | custom-call | bytes 11010048 | tf_op jit(solution)/shard_map/gather_rows/pallas_call | solution.py:1358
  78.7 1.2 slice.72
  82.8 1.2 slice.76.normed_ref
  84.1 10.8 %fusion.12.p_ref.plast_ref = f32[528,3584]{1,0:T(8,128)} fusion(bf16[528,1536]{1,0:T(8,128)(2,1)S(1)} %fusion.2, bf16[1536,3584]{1,0:T(8,128)(2,1)} %bitcast.33), kind=kOutput, calls=%fused_computation.35 | convolution fusion | flops 5813305344 | bytes 20201472 | tf_op jit(solution)/shard_map/dot_general | solution.py:37
  94.8 5.7 %steps.1 = (f32[12,512,16]{2,1,0:T(8,128)S(1)}, f32[12,4,512]{2,1,0:T(4,128)S(1)}, bf16[512,256]{1,0:T(8,128)(2,1)S(1)}, f32[512,128]{1,0:T(8,128)S(1)}, f32[8,128]{1,0:T(8,128)S(1)}) custom-call(f32[528,3584]{1,0:T(8,128)} %fusion.12.p_ref.plast_ref, f32[8,3584]{1,0:T(8,128)S(1)} %pad_convert_fusion.w_ref.wlast_ref, ...), custom_call_target="tpu_custom_call" | custom-call | flops 67108864 | bytes 4194304 | tf_op jit(solution)/shard_map/steps/pallas_call | solution.py:117
  100.5 1.7 copy-done
  102.2 87.2 %scan_forward.1 = (f32[512,3072]{1,0:T(8,128)}, bf16[2,3072,128]{2,1,0:T(8,128)(2,1)S(1)}, f32[512,3072]{1,0:T(8,128)}, bf16[2,768,512]{2,1,0:T(8,128)(2,1)S(1)}, bf16[4,8,48,3072]{3,2,1,0:T(8,128)(2,1)}) custom-call(f32[8,128]{1,0:T(8,128)S(1)} %get-tuple-element.39.decays.grown_ref, f32[528,3584]{1,0:T(8,128)} %fusion.12.p_ref.plast_ref, ...), custom_call_target="tpu_custom_call" | custom-call | flops 4831838208 | bytes 37748736 | tf_op jit(solution)/shard_map/scan_forward/pallas_call | solution.py:332
  189.4 1.1 copy-done.3
  190.6 1.2 copy-done.4
  191.8 10.6 %convolution_bitcast_fusion.gno_ref = f32[512,3072]{1,0:T(8,128)} fusion(bf16[3072,1536]{1,0:T(8,128)(2,1)} %all-gather.2.cloned.1.call-done.more_refs_1_, bf16[1,512,1536]{2,1,0:T(8,128)(2,1)S(1)} %copy-done.17), kind=kOutput, calls=%fused_computation | convolution fusion | flops 4831838208 | bytes 17301504 | tf_op jit(solution)/shard_map/dot_general | solution.py:37
  202.3 16.7 %gate.1 = (bf16[512,3072]{1,0:T(8,128)(2,1)S(1)}, bf16[512,3072]{1,0:T(8,128)(2,1)}, bf16[512,3072]{1,0:T(8,128)(2,1)}, bf16[512,3072]{1,0:T(8,128)(2,1)}, f32[2...) custom-call(f32[512,3072]{1,0:T(8,128)} %get-tuple-element.44.y_ref, f32[512,3072]{1,0:T(8,128)} %get-tuple-element.45.gate_ref, ...), custom_call_target="tpu_custom_call" | custom-call | flops 805306368 | bytes 37748736 | tf_op jit(solution)/shard_map/gate/pallas_call | solution.py:454
  219.0 1.7 copy-done.1
  220.7 173.8 %scan_backward.1 = (f32[48,9728]{1,0:T(8,128)}, f32[512,1536]{1,0:T(8,128)}, f32[8,3456]{1,0:T(8,128)}, bf16[512,1536]{1,0:T(8,128)(2,1)}) custom-call(f32[8,128]{1,0:T(8,128)} %copy-done.9, f32[528,3584]{1,0:T(8,128)} %fusion.12.p_ref.plast_ref, f32[8,3584]{1,0:T(8,128)} %copy-done.2, f32[1,3584]{1,0:T(1,128)} %copy-done.6, f32[12,512,16]{2,1,0:T(8,128)} %copy-done, ...), custom_call_target="tpu_custom_call" | custom-call | flops 9663676416 | bytes 47185920 | tf_op jit(solution)/shard_map/scan_backward/pallas_call | solution.py:1000
  394.6 1.3 slice_bitcast_fusion.1
  395.9 0.8 constant_dynamic-slice_fusion
  397.8 1.1 fusion.11
  398.9 2.7 multiply_reduce_fusion
  402.1 1.0 multiply_reduce_fusion.1
  403.6 1.1 copy.31
  404.8 1.7 copy.32
  (77 shorter events, 6.8 us)
Async XLA Ops:
  7.2 74.7 %copy-start.13 = (bf16[1,512,1536]{2,1,0:T(8,128)(2,1)S(1)}, bf16[1,512,1536]{2,1,0:T(8,128)(2,1)}, u32[]{:S(2)}) copy-start(bf16[1,512,1536]{2,1,0:T(8,128)(2,1)} %param.11) | copy-start | bytes 4718596
  7.2 74.0 %copy-start.22 = (f32[48]{0:T(128)S(1)}, f32[48]{0:T(128)}, u32[]{:S(2)}) copy-start(f32[48]{0:T(128)} %param.16) | copy-start | bytes 580
  7.2 74.0 %copy-start.23 = (f32[48]{0:T(128)S(1)}, f32[48]{0:T(128)}, u32[]{:S(2)}) copy-start(f32[48]{0:T(128)} %param.17) | copy-start | bytes 580
  7.2 74.0 %copy-start.19 = (f32[48]{0:T(128)S(1)}, f32[48]{0:T(128)}, u32[]{:S(2)}) copy-start(f32[48]{0:T(128)} %param.18) | copy-start | bytes 580
  7.2 184.5 %all-gather.2.cloned.1.call-start = ((), (), s32[]{:S(2)}) async-start(), calls=%async_computation | async-start | bytes 9732096 | tf_op jit(solution)/shard_map/all_gather | solution.py:1626
  81.2 13.7 %copy-start.10 = (f32[1,128]{1,0:T(1,128)}, f32[1,128]{1,0:T(1,128)S(1)}, u32[]{:S(2)}) copy-start(f32[1,128]{1,0:T(1,128)S(1)} %pad.28.bias_ref) | copy-start | bytes 1540
  81.2 13.6 %copy-start.11 = (f32[1,128]{1,0:T(1,128)}, f32[1,128]{1,0:T(1,128)S(1)}, u32[]{:S(2)}) copy-start(f32[1,128]{1,0:T(1,128)S(1)} %pad.29.decay_ref) | copy-start | bytes 1540
  81.4 20.8 %copy-start.8 = (f32[1,3072]{1,0:T(1,128)}, f32[1,3072]{1,0:T(1,128)S(1)}, u32[]{:S(2)}) copy-start(f32[1,3072]{1,0:T(1,128)S(1)} %broadcast_in_dim_reshape.3.skip_ref) | copy-start | bytes 36868
  84.0 18.2 %copy-start.6 = (f32[1,3584]{1,0:T(1,128)}, f32[1,3584]{1,0:T(1,128)S(1)}, u32[]{:S(2)}) copy-start(f32[1,3584]{1,0:T(1,128)S(1)} %pad_convert_fusion.1.b_ref.blast_ref) | copy-start | bytes 43012
  84.1 18.1 %copy-start.2 = (f32[8,3584]{1,0:T(8,128)}, f32[8,3584]{1,0:T(8,128)S(1)}, u32[]{:S(2)}) copy-start(f32[8,3584]{1,0:T(8,128)S(1)} %pad_convert_fusion.w_ref.wlast_ref) | copy-start | bytes 344068
  94.8 7.4 %copy-start.12 = (bf16[4,48,3072]{2,1,0:T(8,128)(2,1)S(1)}, bf16[4,48,3072]{2,1,0:T(8,128)(2,1)}, u32[]{:S(2)}) copy-start(bf16[4,48,3072]{2,1,0:T(8,128)(2,1)} %get-tuple-element.43.own) | copy-start | bytes 3538948
  100.5 1.7 copy-start
  102.2 87.2 %copy-start.7 = (f32[12,4,512]{2,1,0:T(4,128)}, f32[12,4,512]{2,1,0:T(4,128)S(1)}, u32[]{:S(2)}) copy-start(f32[12,4,512]{2,1,0:T(4,128)S(1)} %get-tuple-element.41.rows_ref) | copy-start | bytes 294916
  102.2 87.2 %copy-start.9 = (f32[8,128]{1,0:T(8,128)}, f32[8,128]{1,0:T(8,128)S(1)}, u32[]{:S(2)}) copy-start(f32[8,128]{1,0:T(8,128)S(1)} %get-tuple-element.39.decays.grown_ref) | copy-start | bytes 12292
  102.2 100.2 %copy-start.5 = (bf16[512,256]{1,0:T(8,128)(2,1)}, bf16[512,256]{1,0:T(8,128)(2,1)S(1)}, u32[]{:S(2)}) copy-start(bf16[512,256]{1,0:T(8,128)(2,1)S(1)} %get-tuple-element.42.maps_ref) | copy-start | bytes 786436
  102.2 89.5 %copy-start.17 = (bf16[1,512,1536]{2,1,0:T(8,128)(2,1)S(1)}, bf16[1,512,1536]{2,1,0:T(8,128)(2,1)}, u32[]{:S(2)}) copy-start(bf16[1,512,1536]{2,1,0:T(8,128)(2,1)} %param.21) | copy-start | bytes 4718596
  190.6 1.2 copy-start.4
  219.0 1.7 copy-start.1
  220.7 178.1 %copy-start.15 = (bf16[48,6448]{1,0:T(8,128)(2,1)S(1)}, bf16[48,6448]{1,0:T(8,128)(2,1)}, u32[]{:S(2)}) copy-start(bf16[48,6448]{1,0:T(8,128)(2,1)} %param.13) | copy-start | bytes 1857028
  394.5 7.1 %copy-start.20 = (bf16[48]{0:T(256)(128)(2,1)S(1)}, bf16[48]{0:T(256)(128)(2,1)}, u32[]{:S(2)}) copy-start(bf16[48]{0:T(256)(128)(2,1)} %param.12) | copy-start | bytes 292
  394.5 7.6 %copy-start.18 = (bf16[96,1536]{1,0:T(8,128)(2,1)S(1)}, bf16[96,1536]{1,0:T(8,128)(2,1)}, u32[]{:S(2)}) copy-start(bf16[96,1536]{1,0:T(8,128)(2,1)} %param.20) | copy-start | bytes 884740
  394.6 8.5 %copy-start.21 = (bf16[96]{0:T(256)(128)(2,1)S(1)}, bf16[96]{0:T(256)(128)(2,1)}, u32[]{:S(2)}) copy-start(bf16[96]{0:T(256)(128)(2,1)} %param.19) | copy-start | bytes 580
  394.6 9.1 %copy-start.16 = (bf16[512,1536]{1,0:T(8,128)(2,1)S(1)}, bf16[512,1536]{1,0:T(8,128)(2,1)}, u32[]{:S(2)}) copy-start(bf16[512,1536]{1,0:T(8,128)(2,1)} %get-tuple-element.57) | copy-start | bytes 4718596
  398.9 5.9 %copy-start.14 = (f32[512,1536]{1,0:T(8,128)S(1)}, f32[512,1536]{1,0:T(8,128)}, u32[]{:S(2)}) copy-start(f32[512,1536]{1,0:T(8,128)} %get-tuple-element.58) | copy-start | bytes 9437188
  (1 other events, 1.1 us)
Sparse Core Ops, SparseCore 0:
  78.8 108.4 all-gather.1
